TPU v7x, 32 devices: a whole 2x2x4 slice. The times are simulated.
32 devices in a mesh: gx: 4 (over z), gy: 4 (over x, core), gz: 2 (over y).
Axes of the slice: x: 2, y: 2, z: 4, core: 2. Of those that a mesh axis runs over, the one named last changes fastest.
Arguments:
- coarse_fields: float32 [4, 64, 64, 256], P(None, 'gx', 'gy', 'gz'), may hold values from -6 to 6
- coarse_wind: float32 [3, 64, 64, 256], P(None, 'gx', 'gy', 'gz'), may hold values from -0.4 to 0.4
- fine_fields: float32 [4, 128, 64, 256], P(None, 'gx', 'gy', 'gz'), may hold values from -6 to 6
- fine_wind: float32 [3, 128, 64, 256], P(None, 'gx', 'gy', 'gz'), may hold values from -0.4 to 0.4
- fine_owner: int32 [4, 4, 2], P('gx', 'gy', 'gz'), may hold values from 0 to 3, as said below
Outputs:
- coarse_next: float32 [4, 64, 64, 256], P(None, 'gx', 'gy', 'gz')
- fine_next: float32 [4, 128, 64, 256], P(None, 'gx', 'gy', 'gz')
Inputs may be any that keep to these rules, and one draw needn't show every extreme that they name: `fine_owner`: in each row of fine boxes along the first direction (fixed second and third index), fine box i refines coarse box (i + r) mod 4 for an offset r of that row, so every row names every coarse box once.
All inputs are finite; a program needn't handle non-finite values.
Results may differ from a plain program's by a relative error of at most 0.0003.
Values sent between devices are 32-bit elements; how exact they have to be, the bound alone decides.
No kernel may reach another device: no remote copies, remote signals or barrier semaphores. Data moves between devices by JAX's collectives and lax.ppermute only.
A program may use at most 128 MiB of HBM per device.

v0:
```python
import functools

import jax
import jax.numpy as jnp
from jax import lax
from jax.experimental import pallas as pl
from jax.experimental.pallas import tpu as pltpu
from jax.sharding import PartitionSpec as P

diffusion = 0.05
section_weights = (1.0 / 3.0, 0.5, 1.0)
F32 = jnp.float32
BF16 = jnp.bfloat16
PAD = 32
TOP = 8


class Sizes:
    def __init__(self, coarse_shape, fine_shape):
        self.q, self.x, self.y, self.z = coarse_shape
        self.fx = fine_shape[1]
        self.ly, self.sy = self.y // 4, self.y // 2
        self.lz, self.sz = self.z // 4, self.z // 2
        self.ex = self.x + 4
        self.ep = -(-self.ex // 8) * 8
        self.fe = self.fx + 4
        self.halo = 3 * self.q + 6
        self.rows_y = 3 * self.q * self.ex
        self.rows_e = self.rows_y + self.ep
        self.rows_z = self.sy + 2
        self.slab = self.rows_e + self.q * self.rows_z
        assert self.q == 4 and self.y == 16 and self.z == 128 and self.ex <= 20 and self.fx == 2 * self.x


def lanes_of(shape):
    return lax.broadcasted_iota(jnp.int32, shape, len(shape) - 1)


def halves(value):
    high = value.astype(BF16)
    return high, (value - high.astype(F32)).astype(BF16)


def times(value, matrix):
    high, low = halves(value)
    return jnp.dot(high, matrix, preferred_element_type=F32) + jnp.dot(low, matrix, preferred_element_type=F32)


def coefficients(wind):
    out = []
    for w in wind:
        out += [diffusion - 0.5 * w, diffusion + 0.5 * w]
    return out


def rate_of(co, center, x_low, x_high, y_low, y_high, z_low, z_high):
    along = (co[0] * x_high + co[1] * x_low) + (co[2] * y_high + co[3] * y_low) + (co[4] * z_high + co[5] * z_low)
    return along - (6.0 * diffusion) * center


def layer_of(s, own, low, high, member, at, width, first):
    size = own.shape[1]
    if at < 0:
        return low[first + width * member + at + width]
    if at >= size:
        return high[first + width * member + at - size]
    return own[member, at]


def pack_kernel(s, fields, wind, up, down, sems):
    size = fields.shape[1]
    moves = []
    for f in range(s.q):
        moves.append((fields.at[f, size - 3 : size], up.at[3 * f : 3 * f + 3]))
        moves.append((fields.at[f, 0:3], down.at[3 * f : 3 * f + 3]))
    for d in range(3):
        at = 3 * s.q + 2 * d
        moves.append((wind.at[d, size - 2 : size], up.at[at : at + 2]))
        moves.append((wind.at[d, 0:2], down.at[at : at + 2]))
    moves = [pltpu.make_async_copy(src, dst, sems.at[i]) for i, (src, dst) in enumerate(moves)]
    for move in moves:
        move.start()
    for move in moves:
        move.wait()


def column_pack(s, tiles):
    total = None
    for j, tile in enumerate(tiles):
        lane = lanes_of(tile.shape)
        part = pltpu.roll(jnp.where((lane == 0) | (lane == s.z - 1), tile, 0.0), 2 * j, 1)
        total = part if total is None else total + part
    return total


def slab_kernel(s, c0, cw, lo, hi, slab, yup, ydn, zcol, pad0, pad1, pad2):
    q, x, y, z = s.q, s.x, s.y, s.z
    own = slice(TOP, TOP + y)
    zeros = jnp.zeros((s.ep, z), F32)
    pads = (pad0, pad1, pad2)
    flats = [pad.reshape(q * s.ep * PAD, z) for pad in pads]
    for f in range(q):
        for pad in (flats[0], flats[1]):
            pad[pl.ds(f * s.ep * PAD + TOP - 1, s.ep, stride=PAD), :] = zeros
            pad[pl.ds(f * s.ep * PAD + TOP + y, s.ep, stride=PAD), :] = zeros
        for at in range(-3, x + 3):
            pad0[f, at + 3, own, :] = layer_of(s, c0, lo, hi, f, at, 3, 0)
        pad2[f, 1, own, :] = zeros[:y]
        pad2[f, s.ex, own, :] = zeros[:y]
    for step in range(2):
        src, dst = pads[step], pads[step + 1]
        for at in range(step - 2, x + 2 - step):
            j = at + 3
            co = coefficients([layer_of(s, cw, lo, hi, d, at, 2, 3 * q) for d in range(3)])
            for f in range(q):
                center = src[f, j, own, :]
                rate = rate_of(
                    co,
                    center,
                    src[f, j - 1, own, :],
                    src[f, j + 1, own, :],
                    src[f, j, TOP - 1 : TOP + y - 1, :],
                    src[f, j, TOP + 1 : TOP + y + 1, :],
                    pltpu.roll(center, 1, 1),
                    pltpu.roll(center, z - 1, 1),
                )
                base = center if step == 0 else pad0[f, j, own, :]
                dst[f, j, own, :] = base + section_weights[step] * rate
    lane_x = lanes_of((s.ex, z))
    lane_y = lanes_of((y, z))
    ends = None
    columns = (lane_y == s.lz - 1) | (lane_y == s.lz) | (lane_y == s.lz + s.sz - 1) | (lane_y == s.lz + s.sz)
    low_at = (lane_y % 2 == 0) & (lane_y < z // 2)
    high_at = (lane_y % 2 == 0) & (lane_y >= z // 2)
    for f in range(q):
        zfaces = None
        for k in range(3):
            start = (f * s.ep + 1) * PAD + TOP
            rows = [
                flats[k][pl.ds(start + at, s.ex, stride=PAD), :] for at in (s.ly - 1, s.ly, s.ly + s.sy - 1, s.ly + s.sy)
            ]
            sides = (0.75 * rows[0] + 0.25 * rows[1], 0.25 * rows[2] + 0.75 * rows[3])
            first = (k * q + f) * s.ex
            slab[first : first + s.ex, :] = jnp.where(
                lane_x < s.sz, pltpu.roll(sides[0], z - s.lz, 1), pltpu.roll(sides[1], s.lz, 1)
            )
            for side in range(2):
                e = 4 * (q * k + f) + 2 * side + 1
                before = jnp.where(lane_x == s.lz - 1, sides[side], 0.0)
                after = jnp.where(lane_x == s.lz + s.sz, sides[side], 0.0)
                part = pltpu.roll(before, (e - s.lz + 1) % z, 1) + pltpu.roll(after, (e - 1 - s.lz - s.sz) % z, 1)
                ends = part if ends is None else ends + part
            raw = None
            for a in range(0 if k == 0 else 1, s.ex if k == 0 else s.ex - 1):
                part = jnp.where(columns, pads[k][f, a + 1, own, :], 0.0)
                part = pltpu.roll(part, (2 * a - s.lz + 1) % z, 1)
                raw = part if raw is None else raw + part
            beside = pltpu.roll(raw, z - 1, 1)
            low = jnp.where(low_at, 0.75 * raw + 0.25 * beside, 0.0)
            high = jnp.where(high_at, 0.25 * raw + 0.75 * beside, 0.0)
            part = pltpu.roll(low, (2 * s.ex * k - 1) % z, 1) + pltpu.roll(high, (2 * s.ex * k - z // 2) % z, 1)
            zfaces = part if zfaces is None else zfaces + part
        at = s.rows_e + f * s.rows_z
        slab[at : at + s.rows_z, :] = zfaces[s.ly - 1 : s.ly + s.sy + 1]
    slab[s.rows_y : s.rows_y + s.ex, :] = ends
    slab[s.rows_y + s.ex : s.rows_e, :] = zeros[: s.ep - s.ex]
    for f in range(q):
        start = (f * s.ep + 1) * PAD + TOP
        yup[f] = flats[0][pl.ds(start + y - 1, s.ex, stride=PAD), :]
        ydn[f] = flats[0][pl.ds(start, s.ex, stride=PAD), :]
        zcol[f] = column_pack(s, [pad0[f, a + 1, own, :] for a in range(s.ex)])


def coarse_kernel(s, step, *refs):
    q, x, y, z = s.q, s.x, s.y, s.z
    (sides, c0, cw, lo, hi), refs = refs[:5], refs[5:]
    if step:
        state, refs = refs[0], refs[1:]
    (ylo, yhi, zin, out), refs = refs[:4], refs[4:]
    if step < 2:
        (yup, ydn, zcol), refs = refs[:3], refs[3:]
    (pad,) = refs
    own = slice(TOP, TOP + y)
    count = s.ex - 2 * step
    flat = pad.reshape(q * s.ep * PAD, z)

    def before(f, at):
        if step == 0:
            return layer_of(s, c0, lo, hi, f, at, 3, 0)
        return state[f, at + 3 - step]

    lane = lanes_of((y, z))
    keep = jnp.where(lane % 2 == 1, sides[0, 0], sides[0, 1]).astype(F32)
    for f in range(q):
        flat[pl.ds(f * s.ep * PAD + TOP - 1, count, stride=PAD), :] = ylo[f]
        flat[pl.ds(f * s.ep * PAD + TOP + y, count, stride=PAD), :] = yhi[f]
        for j in range(count):
            pad[f, j, own, :] = before(f, j + step - 2)
    ghosts = [zin[f] * keep for f in range(q)]
    for j in range(count):
        at = j + step - 2
        co = coefficients([layer_of(s, cw, lo, hi, d, at, 2, 3 * q) for d in range(3)])
        for f in range(q):
            center = before(f, at)
            ghost = pltpu.roll(ghosts[f], (-2 * j) % z, 1)
            rate = rate_of(
                co,
                center,
                before(f, at - 1),
                before(f, at + 1),
                pad[f, j, TOP - 1 : TOP + y - 1, :],
                pad[f, j, TOP + 1 : TOP + y + 1, :],
                pltpu.roll(jnp.where(lane == z - 1, ghost, center), 1, 1),
                pltpu.roll(jnp.where(lane == 0, ghost, center), z - 1, 1),
            )
            base = center if step == 0 else layer_of(s, c0, lo, hi, f, at, 3, 0)
            out[f, j] = base + section_weights[step] * rate
    if step < 2:
        made = out.reshape(q * count * y, z)
        for f in range(q):
            start = (f * count + 1) * y
            yup[f] = made[pl.ds(start + y - 1, count - 2, stride=y), :]
            ydn[f] = made[pl.ds(start, count - 2, stride=y), :]
            zcol[f] = column_pack(s, [out[f, j + 1] for j in range(count - 2)])


def fine_kernel(s, f0, fw, flo, fhi, slab, out, avg, *scratch):
    s0, s1, s2, wide_wind, faces, zface, sems = scratch
    states = (s0, s1, s2)
    q, y, z, fx, fe = s.q, s.y, s.z, s.fx, s.fe
    layers = fx + 6
    rows = slice(TOP, TOP + y)
    pairs = [(f0, s0.at[:, 3 : 3 + fx, rows]), (fw, wide_wind.at[:, 2 : 2 + fx])]
    for f in range(q):
        pairs.append((flo.at[3 * f : 3 * f + 3], s0.at[f, 0:3, rows]))
        pairs.append((fhi.at[3 * f : 3 * f + 3], s0.at[f, 3 + fx : 6 + fx, rows]))
    for d in range(3):
        at = 3 * q + 2 * d
        pairs.append((flo.at[at : at + 2], wide_wind.at[d, 0:2]))
        pairs.append((fhi.at[at : at + 2], wide_wind.at[d, 2 + fx : 4 + fx]))
    moves = [pltpu.make_async_copy(src, dst, sems.at[i]) for i, (src, dst) in enumerate(pairs)]
    for move in moves:
        move.start()
    r = lax.broadcasted_iota(jnp.int32, (z, 2 * z), 0)
    c = lax.broadcasted_iota(jnp.int32, (z, 2 * z), 1)
    near = c // 2
    far = near + 2 * (c % 2) - 1
    same = (far // s.sz == near // s.sz) & (far >= 0)
    to_fine = jnp.where(r == near, 0.75, jnp.where((r == far) & same, 0.25, 0.0)).astype(BF16)
    wide = times(slab[: s.rows_y, :], to_fine)
    ends = slab[s.rows_y : s.rows_y + s.ex, :]
    lane_x = lanes_of((s.ex, z))
    edge = (lane_x == 0) | (lane_x == z - 1)
    half = fe // 2
    for k in range(3):
        flat = states[k].reshape(q * layers * PAD, z)
        for f in range(q):
            for side in range(2):
                e = 4 * (q * k + f) + 2 * side + 1
                corner = jnp.where(edge, 0.25 * pltpu.roll(ends, z - e, 1), 0.0)
                first = (k * q + f) * s.ex
                faces[: s.ex, :] = wide[first : first + s.ex, side * z : side * z + z] + corner
                a = faces[0:half, :]
                b = faces[1 : half + 1, :]
                d = faces[2 : half + 2, :]
                row = TOP - 1 if side == 0 else TOP + y
                base = (f * layers + 1) * PAD + row
                flat[pl.ds(base, half, stride=2 * PAD), :] = 0.25 * a + 0.75 * b
                flat[pl.ds(base + PAD, half, stride=2 * PAD), :] = 0.75 * b + 0.25 * d
    evens, odds = [], []
    for f in range(q):
        at = s.rows_e + f * s.rows_z
        a = slab[at : at + s.sy, :]
        b = slab[at + 1 : at + 1 + s.sy, :]
        d = slab[at + 2 : at + 2 + s.sy, :]
        zface[pl.ds(0, s.sy, stride=2), :] = 0.25 * a + 0.75 * b
        zface[pl.ds(1, s.sy, stride=2), :] = 0.75 * b + 0.25 * d
        a = zface[...]
        b = pltpu.roll(a, z - 2, 1)
        d = pltpu.roll(a, z - 4, 1)
        evens.append(0.25 * a + 0.75 * b)
        odds.append(0.75 * b + 0.25 * d)
    for move in moves:
        move.wait()
    lane = lanes_of((y, z))
    is_first, is_last = lane == 0, lane == z - 1
    for k in range(3):
        src, fraction = states[k], section_weights[k]
        begin, end = (0, half) if k < 2 else (1, half - 1)
        shift = -(2 * s.ex * k + 2 * begin) % z
        carried = tuple(pltpu.roll(g, shift, 1) if shift else g for g in evens + odds)

        def pair_of_layers(t, ghosts, k=k, src=src, fraction=fraction):
            for odd in range(2):
                b = 2 * t + odd
                co = coefficients([wide_wind[d, b] for d in range(3)])
                for f in range(q):
                    center = src[f, b + 1, rows, :]
                    ghost = ghosts[odd * q + f]
                    rate = rate_of(
                        co,
                        center,
                        src[f, b, rows, :],
                        src[f, b + 2, rows, :],
                        src[f, b + 1, TOP - 1 : TOP + y - 1, :],
                        src[f, b + 1, TOP + 1 : TOP + y + 1, :],
                        pltpu.roll(jnp.where(is_last, ghost, center), 1, 1),
                        pltpu.roll(jnp.where(is_first, ghost, center), z - 1, 1),
                    )
                    value = (center if k == 0 else s0[f, b + 1, rows, :]) + fraction * rate
                    if k < 2:
                        states[k + 1][f, b + 1, rows, :] = value
                    else:
                        out[f, b - 2] = value
            return tuple(pltpu.roll(g, z - 2, 1) for g in ghosts)

        lax.fori_loop(begin, end, pair_of_layers, carried)
    rz = lax.broadcasted_iota(jnp.int32, (z, z), 0)
    cz = lax.broadcasted_iota(jnp.int32, (z, z), 1)
    flat = out.reshape(q * fx * y, z)
    pairs_z = [jnp.where(cz == rz // 2 + odd * s.sz, 0.125, 0.0).astype(BF16) for odd in range(2)]
    for f in range(q):
        sums = []
        for odd in range(2):
            parts = []
            for p in range(s.x // 2):
                base = (f * fx + 4 * p + 2 * odd) * y
                part = None
                for more in (0, 1, y, y + 1):
                    piece = flat[pl.ds(base + more, y // 2, stride=2), :]
                    part = piece if part is None else part + piece
                parts.append(part)
            sums.append(times(jnp.concatenate(parts, axis=0), pairs_z[odd]))
        avg[f] = (sums[0] + sums[1]).reshape(s.x // 2, y // 2, z)


def merge_kernel(s, c3, avg, out):
    lane = lanes_of((s.sy, s.z))
    inside = (lane >= s.lz) & (lane < s.lz + s.sz)
    for f in range(s.q):
        for p in range(s.x // 2):
            both = avg[f, p]
            for odd in range(2):
                at = 2 * p + odd
                moved = pltpu.roll(both, s.lz if odd == 0 else s.z - s.lz, 1)
                out[f, at] = c3[f, at]
                out[f, at, s.ly : s.ly + s.sy, :] = jnp.where(inside, moved, c3[f, at, s.ly : s.ly + s.sy, :])


VMEM = pl.BlockSpec(memory_space=pltpu.VMEM)
SMEM = pl.BlockSpec(memory_space=pltpu.SMEM)
HBM = pl.BlockSpec(memory_space=pltpu.HBM)
ANY = pl.BlockSpec(memory_space=pl.ANY)


def params(megabytes):
    return pltpu.CompilerParams(vmem_limit_bytes=megabytes << 20)


def shape(*dims):
    return jax.ShapeDtypeStruct(dims, F32)


def ring(array, axis, by):
    size = lax.axis_size(axis)
    return lax.ppermute(array, axis, [(i, (i + by) % size) for i in range(size)])


def move_by(array, amount):
    size = lax.axis_size("gx")
    if size <= 8:
        return lax.switch(amount, [lambda a, k=k: a if k == 0 else ring(a, "gx", k) for k in range(size)], array)
    for bit in range((size - 1).bit_length()):
        array = jnp.where((amount >> bit) % 2 == 1, ring(array, "gx", 1 << bit), array)
    return array


def z_columns(zcol):
    size = lax.axis_size("gz")
    if size == 1:
        return jnp.zeros_like(zcol)
    if size == 2:
        return lax.ppermute(zcol, "gz", [(0, 1), (1, 0)])
    odd = lax.broadcasted_iota(jnp.int32, zcol.shape, 2) % 2 == 1
    return jnp.where(odd, ring(zcol, "gz", 1), ring(zcol, "gz", -1))


def pack(s, fields, wind, name):
    return pl.pallas_call(
        functools.partial(pack_kernel, s),
        out_shape=(shape(s.halo, s.y, s.z),) * 2,
        in_specs=[HBM, HBM],
        out_specs=(ANY, ANY),
        scratch_shapes=[pltpu.SemaphoreType.DMA((2 * (s.q + 3),))],
        name=name,
    )(fields, wind)


def shards(coarse_fields, coarse_wind, fine_fields, fine_wind, fine_owner):
    s = Sizes(coarse_fields.shape, fine_fields.shape)
    q, x, y, z, fx = s.q, s.x, s.y, s.z, s.fx
    size = lax.axis_size("gx")
    offset = (fine_owner[0, 0, 0] - lax.axis_index("gx")) % size
    level = lax.axis_index("gz")
    neighbours = jnp.stack([level > 0, level < lax.axis_size("gz") - 1]).astype(jnp.int32).reshape(1, 2)
    up, down = pack(s, coarse_fields, coarse_wind, "pack_coarse")
    lo, hi = ring(up, "gx", 1), ring(down, "gx", -1)
    up, down = pack(s, fine_fields, fine_wind, "pack_fine")
    flo, fhi = ring(up, "gx", 1), ring(down, "gx", -1)
    padded = pltpu.VMEM((q, s.ep, PAD, z), F32)
    slab, yup, ydn, zcol = pl.pallas_call(
        functools.partial(slab_kernel, s),
        out_shape=(shape(s.slab, z), shape(q, s.ex, z), shape(q, s.ex, z), shape(q, y, z)),
        in_specs=[VMEM] * 4,
        out_specs=(VMEM,) * 4,
        scratch_shapes=[padded] * 3,
        compiler_params=params(24),
        name="slab",
    )(coarse_fields, coarse_wind, lo, hi)
    state = None
    for step in range(3):
        count = s.ex - 2 * step
        ylo, yhi = ring(yup, "gy", 1), ring(ydn, "gy", -1)
        zin = z_columns(zcol)
        outs = [shape(q, count, y, z)]
        if step < 2:
            outs += [shape(q, count - 2, z), shape(q, count - 2, z), shape(q, y, z)]
        ins = [neighbours, coarse_fields, coarse_wind, lo, hi] + ([state] if step else []) + [ylo, yhi, zin]
        made = pl.pallas_call(
            functools.partial(coarse_kernel, s, step),
            out_shape=tuple(outs),
            in_specs=[SMEM] + [VMEM] * (len(ins) - 1),
            out_specs=(VMEM,) * len(outs),
            scratch_shapes=[padded],
            compiler_params=params(16),
            name="coarse",
        )(*ins)
        state = made[0]
        if step < 2:
            yup, ydn, zcol = made[1:]
    slab = move_by(slab, (size - offset) % size)
    layers = fx + 6
    fine_next, averaged = pl.pallas_call(
        functools.partial(fine_kernel, s),
        out_shape=(shape(q, fx, y, z), shape(q, x // 2, y // 2, z)),
        in_specs=[ANY, ANY, ANY, ANY, VMEM],
        out_specs=(VMEM, VMEM),
        scratch_shapes=[
            pltpu.VMEM((q, layers, PAD, z), F32),
            pltpu.VMEM((q, layers, PAD, z), F32),
            pltpu.VMEM((q, layers, PAD, z), F32),
            pltpu.VMEM((3, s.fe, y, z), F32),
            pltpu.VMEM((s.ep, z), F32),
            pltpu.VMEM((y, z), F32),
            pltpu.SemaphoreType.DMA((2 + 2 * (q + 3),)),
        ],
        compiler_params=params(32),
        name="fine",
    )(fine_fields, fine_wind, flo, fhi, slab)
    averaged = move_by(averaged, offset)
    coarse_next = pl.pallas_call(
        functools.partial(merge_kernel, s),
        out_shape=shape(q, x, y, z),
        in_specs=[VMEM, VMEM],
        out_specs=VMEM,
        compiler_params=params(16),
        name="merge",
    )(state, averaged)
    return coarse_next, fine_next


def solution(mesh):
    spec = P(None, "gx", "gy", "gz")
    return jax.shard_map(
        shards,
        mesh=mesh,
        in_specs=(spec, spec, spec, spec, P("gx", "gy", "gz")),
        out_specs=(spec, spec),
        check_vma=False,
    )
```

profile of v0, /device:TPU:0, one launch (start us, length us, event | category | flops | bytes accessed | tf_op | source)
XLA Modules:
  0.0 92.8 jit_solution(18113194543667180135)
XLA Ops:
  0.6 10.2 %pack_coarse.1 = (f32[18,16,128]{2,1,0:T(8,128)}, f32[18,16,128]{2,1,0:T(8,128)}) custom-call(f32[4,16,16,128]{3,2,1,0:T(8,128)} %refs_1_.5, f32[3,16,16,128]{3,2,1,0:T(8,128)} %refs_2_.5), custom_call_target="tpu_custom_call" | custom-call | tf_op jit(solution)/shard_map/pack_coarse/pallas_call | solution.py:389
  10.8 3.1 %collective-permute-start.6 = (f32[18,16,128]{2,1,0:T(8,128)}, f32[18,16,128]{2,1,0:T(8,128)S(1)}, u32[]{:S(2)}, u32[]{:S(2)}) collective-permute-start(f32[18,16,128]{2,1,0:T(8,128)} %get-tuple-element.38), channel_id=1, source_target_pairs={{0,8},{8,16},{16,24},{24,0},{1,9},{9,17},{17,25},{25,1},{2,10},{10... | collective-permute-start | bytes 442376 | tf_op jit(solution)/shard_map/ppermute | solution.py:366
  13.9 2.1 %collective-permute-start.7 = (f32[18,16,128]{2,1,0:T(8,128)}, f32[18,16,128]{2,1,0:T(8,128)S(1)}, u32[]{:S(2)}, u32[]{:S(2)}) collective-permute-start(f32[18,16,128]{2,1,0:T(8,128)} %get-tuple-element.39), channel_id=1, source_target_pairs={{0,24},{8,0},{16,8},{24,16},{1,25},{9,1},{17,9},{25,17},{2,26},{10... | collective-permute-start | bytes 442376 | tf_op jit(solution)/shard_map/ppermute | solution.py:366
  16.0 10.2 %pack_fine.1 = (f32[18,16,128]{2,1,0:T(8,128)}, f32[18,16,128]{2,1,0:T(8,128)}) custom-call(f32[4,32,16,128]{3,2,1,0:T(8,128)} %f0.1, f32[3,32,16,128]{3,2,1,0:T(8,128)} %fw.1), custom_call_target="tpu_custom_call" | custom-call | tf_op jit(solution)/shard_map/pack_fine/pallas_call | solution.py:389
  26.2 0.1 collective-permute-start.17
  26.2 3.8 %collective-permute-start.18 = (f32[18,16,128]{2,1,0:T(8,128)}, f32[18,16,128]{2,1,0:T(8,128)S(1)}, u32[]{:S(2)}, u32[]{:S(2)}) collective-permute-start(f32[18,16,128]{2,1,0:T(8,128)} %get-tuple-element.52), channel_id=1, source_target_pairs={{0,24},{8,0},{16,8},{24,16},{1,25},{9,1},{17,9},{25,17},{2,26},{10... | collective-permute-start | bytes 442376 | tf_op jit(solution)/shard_map/ppermute | solution.py:366
  30.0 0.0 collective-permute-done.6.lo.refs_3_
  30.0 0.0 collective-permute-done.7.hi.refs_4_
  30.0 0.0 copy-done
  30.1 4.1 %slab.1 = (f32[304,128]{1,0:T(8,128)}, f32[4,20,128]{2,1,0:T(8,128)S(1)}, f32[4,20,128]{2,1,0:T(8,128)S(1)}, f32[4,16,128]{2,1,0:T(8,128)S(1)}) custom-call(f32[4,16,16,128]{3,2,1,0:T(8,128)S(1)} %copy-done, f32[3,16,16,128]{3,2,1,0:T(8,128)S(1)} %copy-done.1, f32[18,16,128]{2,1,0:T(8,128)S(1)} %collective-permute-done.6.lo.refs_3_, ...), custom_call_target="tpu_custom_call" | custom-call | tf_op jit(solution)/shard_map/slab/pallas_call | solution.py:411
  34.2 1.7 %collective-permute-start.10 = (f32[4,16,128]{2,1,0:T(8,128)S(1)}, f32[4,16,128]{2,1,0:T(8,128)S(1)}, u32[]{:S(2)}, u32[]{:S(2)}) collective-permute-start(f32[4,16,128]{2,1,0:T(8,128)S(1)} %get-tuple-element.42), channel_id=1, source_target_pairs={{0,1},{1,0},{2,3},{3,2},{4,5},{5,4},{6,7},{7,6},{8,9},{9,8},{10,11... | collective-permute-start | bytes 98312 | tf_op jit(solution)/shard_map/ppermute | solution.py:383
  35.8 0.0 collective-permute-start.8
  35.8 1.7 %collective-permute-start.9 = (f32[4,20,128]{2,1,0:T(8,128)S(1)}, f32[4,20,128]{2,1,0:T(8,128)S(1)}, u32[]{:S(2)}, u32[]{:S(2)}) collective-permute-start(f32[4,20,128]{2,1,0:T(8,128)S(1)} %get-tuple-element.41), channel_id=1, source_target_pairs={{0,6},{2,0},{4,2},{6,4},{1,7},{3,1},{5,3},{7,5},{8,14},{10,8},{12,... | collective-permute-start | bytes 122888 | tf_op jit(solution)/shard_map/ppermute | solution.py:366
  37.6 0.1 add_convert_fusion.refs_0_
  37.6 0.4 collective-permute-done.10.refs_7_
  38.1 1.3 %collective-permute-done.8.refs_5_ = f32[4,20,128]{2,1,0:T(8,128)S(1)} collective-permute-done((f32[4,20,128]{2,1,0:T(8,128)S(1)}, f32[4,20,128]{2,1,0:T(8,128)S(1)}, u32[]{:S(2)}, u32[]{:S(2)}) %collective-permute-start.8) | collective-permute-done | bytes 40992 | tf_op jit(solution)/shard_map/ppermute | solution.py:366
  39.3 0.0 collective-permute-done.9.refs_6_
  39.3 5.7 %coarse.3 = (f32[4,20,16,128]{3,2,1,0:T(8,128)S(1)}, f32[4,18,128]{2,1,0:T(8,128)S(1)}, f32[4,18,128]{2,1,0:T(8,128)S(1)}, f32[4,16,128]{2,1,0:T(8,128)S(1)}) custom-call(s32[1,2]{1,0:T(1,128)S(1)} %add_convert_fusion.refs_0_, f32[4,16,16,128]{3,2,1,0:T(8,128)S(1)} %copy-done, f32[3,16,16,128]{3,2,1,0:T(8,128)S(1)} %copy-done.1, ...), custom_call_target="tpu_custom_call" | custom-call | tf_op jit(solution)/shard_map/coarse/pallas_call | solution.py:429
  45.0 0.0 copy-start.4
  45.0 0.8 copy-done.4
  45.8 1.6 %collective-permute-start.11 = (f32[4,18,128]{2,1,0:T(8,128)S(1)}, f32[4,18,128]{2,1,0:T(8,128)S(1)}, u32[]{:S(2)}, u32[]{:S(2)}) collective-permute-start(f32[4,18,128]{2,1,0:T(8,128)S(1)} %get-tuple-element.44), channel_id=1, source_target_pairs={{0,2},{2,4},{4,6},{6,0},{1,3},{3,5},{5,7},{7,1},{8,10},{10,12},{12... | collective-permute-start | bytes 110600 | tf_op jit(solution)/shard_map/ppermute | solution.py:366
  47.4 0.1 collective-permute-start.12
  48.3 9.2 %conditional.2 = (f32[304,128]{1,0:T(8,128)}) conditional(s32[]{:T(128)} %clamp.7, f32[304,128]{1,0:T(8,128)} %get-tuple-element.53, f32[304,128]{1,0:T(8,128)} %get-tuple-element.53, f32[304,128]{1,0:T(8,128)} %get-tuple-element.53, f32[304,128]{1,0:T(8,128)} %get-tuple-element.53), branch_computations={%region_0.1_spmd, %region_1.2_spmd, %region_2.3_spmd, %region_3.4_... | conditional | bytes 933936 | solution.py:372
  48.3 0.1 collective-permute-start.1
  48.4 8.4 %collective-permute-done.1 = f32[304,128]{1,0:T(8,128)S(1)} collective-permute-done((f32[304,128]{1,0:T(8,128)}, f32[304,128]{1,0:T(8,128)S(1)}, u32[]{:S(2)}, u32[]{:S(2)}) %collective-permute-start.1) | collective-permute-done | bytes 155680 | tf_op jit(solution)/shard_map/cond/branch_2_fun/ppermute | solution.py:366
  56.8 0.7 copy.9
  57.5 0.0 collective-permute-start.13
  57.5 3.9 %collective-permute-done.13.refs_8_ = f32[4,16,128]{2,1,0:T(8,128)S(1)} collective-permute-done((f32[4,16,128]{2,1,0:T(8,128)S(1)}, f32[4,16,128]{2,1,0:T(8,128)S(1)}, u32[]{:S(2)}, u32[]{:S(2)}) %collective-permute-start.13) | collective-permute-done | bytes 32800 | tf_op jit(solution)/shard_map/ppermute | solution.py:383
  61.4 0.0 collective-permute-done.11.refs_6_
  61.4 0.0 collective-permute-done.12.refs_7_
  61.4 1.1 %copy-done.5 = f32[4,20,16,128]{3,2,1,0:T(8,128)S(1)} copy-done((f32[4,20,16,128]{3,2,1,0:T(8,128)S(1)}, f32[4,20,16,128]{3,2,1,0:T(8,128)}, u32[]{:S(2)}) %copy-start.5) | copy-done | bytes 655384
  62.5 5.1 %coarse.4 = (f32[4,18,16,128]{3,2,1,0:T(8,128)S(1)}, f32[4,16,128]{2,1,0:T(8,128)S(1)}, f32[4,16,128]{2,1,0:T(8,128)S(1)}, f32[4,16,128]{2,1,0:T(8,128)S(1)}) custom-call(s32[1,2]{1,0:T(1,128)S(1)} %add_convert_fusion.refs_0_, f32[4,16,16,128]{3,2,1,0:T(8,128)S(1)} %copy-done, f32[3,16,16,128]{3,2,1,0:T(8,128)S(1)} %copy-done.1, ...), custom_call_target="tpu_custom_call" | custom-call | tf_op jit(solution)/shard_map/coarse/pallas_call | solution.py:429
  67.6 0.8 copy-done.6
  68.4 0.0 collective-permute-start.14
  68.4 1.7 %collective-permute-start.15 = (f32[4,16,128]{2,1,0:T(8,128)S(1)}, f32[4,16,128]{2,1,0:T(8,128)S(1)}, u32[]{:S(2)}, u32[]{:S(2)}) collective-permute-start(f32[4,16,128]{2,1,0:T(8,128)S(1)} %get-tuple-element.49), channel_id=1, source_target_pairs={{0,6},{2,0},{4,2},{6,4},{1,7},{3,1},{5,3},{7,5},{8,14},{10,8},{12,... | collective-permute-start | bytes 98312 | tf_op jit(solution)/shard_map/ppermute | solution.py:366
  70.1 0.0 collective-permute-start.16
  70.1 0.0 collective-permute-done.17.flo
  70.1 0.0 collective-permute-done.18.fhi
  70.2 9.5 %fine.1 = (f32[4,32,16,128]{3,2,1,0:T(8,128)}, f32[4,8,8,128]{3,2,1,0:T(8,128)}) custom-call(f32[4,32,16,128]{3,2,1,0:T(8,128)S(1)} %copy-done.2, f32[3,32,16,128]{3,2,1,0:T(8,128)S(1)} %copy-done.3, f32[18,16,128]{2,1,0:T(8,128)S(1)} %collective-permute-done.17.flo, f32[18,16,128]{2,1,0:T(8,128)S(1)} %collective-permute-done.18.fhi, ...), custom_call_target="tpu_custom_call" | custom-call | tf_op jit(solution)/shard_map/fine/pallas_call | solution.py:443
  79.7 8.5 %conditional.3 = (f32[4,8,8,128]{3,2,1,0:T(8,128)}) conditional(s32[]{:T(128)} %clamp.6, f32[4,8,8,128]{3,2,1,0:T(8,128)} %get-tuple-element.54, f32[4,8,8,128]{3,2,1,0:T(8,128)} %get-tuple-element.54, f32[4,8,8,128]{3,2,1,0:T(8,128)} %get-tuple-element.54, f32[4,8,8,128]{3,2,1,0:T(8,128)} %get-tuple-element.54), branch_computations={%region_4.5_spmd, %region_5.6_spmd, %region_6.7_spmd, %region_7.8_... | conditional | bytes 786480 | solution.py:372
  79.8 0.1 collective-permute-start.4
  79.8 7.7 %collective-permute-done.4 = f32[4,8,8,128]{3,2,1,0:T(8,128)S(1)} collective-permute-done((f32[4,8,8,128]{3,2,1,0:T(8,128)}, f32[4,8,8,128]{3,2,1,0:T(8,128)S(1)}, u32[]{:S(2)}, u32[]{:S(2)}) %collective-permute-start.4) | collective-permute-done | bytes 131104 | tf_op jit(solution)/shard_map/cond/branch_2_fun/ppermute | solution.py:366
  87.6 0.7 copy.13
  88.2 0.0 collective-permute-done.14.refs_6_
  88.2 0.0 collective-permute-done.15.refs_7_
  88.2 0.0 collective-permute-done.16.refs_8_
  88.3 3.6 %coarse.5.c3 = f32[4,16,16,128]{3,2,1,0:T(8,128)S(1)} custom-call(s32[1,2]{1,0:T(1,128)S(1)} %add_convert_fusion.refs_0_, f32[4,16,16,128]{3,2,1,0:T(8,128)S(1)} %copy-done, f32[3,16,16,128]{3,2,1,0:T(8,128)S(1)} %copy-done.1, f32[18,16,128]{2,1,0:T(8,128)S(1)} %collective-permute-done.6.lo.refs_3_, f32[18,16,128]{2,1,0:T(8,128)S(1)} %collective-permute-done.7.hi.refs_4_, ...), custom_call_target="tpu_custom_call" | custom-call | tf_op jit(solution)/shard_map/coarse/pallas_call | solution.py:429
  91.9 0.9 %merge.1 = f32[4,16,16,128]{3,2,1,0:T(8,128)} custom-call(f32[4,16,16,128]{3,2,1,0:T(8,128)S(1)} %coarse.5.c3, f32[4,8,8,128]{3,2,1,0:T(8,128)S(1)} %copy-done.8), custom_call_target="tpu_custom_call" | custom-call | tf_op jit(solution)/shard_map/merge/pallas_call | solution.py:461
  (13 shorter events, 0.0 us)
Async XLA Ops:
  10.8 19.2 %collective-permute-start.6 = (f32[18,16,128]{2,1,0:T(8,128)}, f32[18,16,128]{2,1,0:T(8,128)S(1)}, u32[]{:S(2)}, u32[]{:S(2)}) collective-permute-start(f32[18,16,128]{2,1,0:T(8,128)} %get-tuple-element.38), channel_id=1, source_target_pairs={{0,8},{8,16},{16,24},{24,0},{1,9},{9,17},{17,25},{25,1},{2,10},{10... | collective-permute-start | bytes 442376 | tf_op jit(solution)/shard_map/ppermute | solution.py:366
  13.9 16.2 %copy-start = (f32[4,16,16,128]{3,2,1,0:T(8,128)S(1)}, f32[4,16,16,128]{3,2,1,0:T(8,128)}, u32[]{:S(2)}) copy-start(f32[4,16,16,128]{3,2,1,0:T(8,128)} %refs_1_.5) | copy-start | bytes 1572868
  13.9 16.2 %copy-start.1 = (f32[3,16,16,128]{3,2,1,0:T(8,128)S(1)}, f32[3,16,16,128]{3,2,1,0:T(8,128)}, u32[]{:S(2)}) copy-start(f32[3,16,16,128]{3,2,1,0:T(8,128)} %refs_2_.5) | copy-start | bytes 1179652
  13.9 16.2 %collective-permute-start.7 = (f32[18,16,128]{2,1,0:T(8,128)}, f32[18,16,128]{2,1,0:T(8,128)S(1)}, u32[]{:S(2)}, u32[]{:S(2)}) collective-permute-start(f32[18,16,128]{2,1,0:T(8,128)} %get-tuple-element.39), channel_id=1, source_target_pairs={{0,24},{8,0},{16,8},{24,16},{1,25},{9,1},{17,9},{25,17},{2,26},{10... | collective-permute-start | bytes 442376 | tf_op jit(solution)/shard_map/ppermute | solution.py:366
  26.2 44.0 %collective-permute-start.17 = (f32[18,16,128]{2,1,0:T(8,128)}, f32[18,16,128]{2,1,0:T(8,128)S(1)}, u32[]{:S(2)}, u32[]{:S(2)}) collective-permute-start(f32[18,16,128]{2,1,0:T(8,128)} %get-tuple-element.51), channel_id=1, source_target_pairs={{0,8},{8,16},{16,24},{24,0},{1,9},{9,17},{17,25},{25,1},{2,10},{10... | collective-permute-start | bytes 442376 | tf_op jit(solution)/shard_map/ppermute | solution.py:366
  26.2 43.9 %collective-permute-start.18 = (f32[18,16,128]{2,1,0:T(8,128)}, f32[18,16,128]{2,1,0:T(8,128)S(1)}, u32[]{:S(2)}, u32[]{:S(2)}) collective-permute-start(f32[18,16,128]{2,1,0:T(8,128)} %get-tuple-element.52), channel_id=1, source_target_pairs={{0,24},{8,0},{16,8},{24,16},{1,25},{9,1},{17,9},{25,17},{2,26},{10... | collective-permute-start | bytes 442376 | tf_op jit(solution)/shard_map/ppermute | solution.py:366
  34.2 3.9 %collective-permute-start.10 = (f32[4,16,128]{2,1,0:T(8,128)S(1)}, f32[4,16,128]{2,1,0:T(8,128)S(1)}, u32[]{:S(2)}, u32[]{:S(2)}) collective-permute-start(f32[4,16,128]{2,1,0:T(8,128)S(1)} %get-tuple-element.42), channel_id=1, source_target_pairs={{0,1},{1,0},{2,3},{3,2},{4,5},{5,4},{6,7},{7,6},{8,9},{9,8},{10,11... | collective-permute-start | bytes 98312 | tf_op jit(solution)/shard_map/ppermute | solution.py:383
  35.8 3.5 %collective-permute-start.8 = (f32[4,20,128]{2,1,0:T(8,128)S(1)}, f32[4,20,128]{2,1,0:T(8,128)S(1)}, u32[]{:S(2)}, u32[]{:S(2)}) collective-permute-start(f32[4,20,128]{2,1,0:T(8,128)S(1)} %get-tuple-element.40), channel_id=1, source_target_pairs={{0,2},{2,4},{4,6},{6,0},{1,3},{3,5},{5,7},{7,1},{8,10},{10,12},{12... | collective-permute-start | bytes 122888 | tf_op jit(solution)/shard_map/ppermute | solution.py:366
  35.8 3.5 %collective-permute-start.9 = (f32[4,20,128]{2,1,0:T(8,128)S(1)}, f32[4,20,128]{2,1,0:T(8,128)S(1)}, u32[]{:S(2)}, u32[]{:S(2)}) collective-permute-start(f32[4,20,128]{2,1,0:T(8,128)S(1)} %get-tuple-element.41), channel_id=1, source_target_pairs={{0,6},{2,0},{4,2},{6,4},{1,7},{3,1},{5,3},{7,5},{8,14},{10,8},{12,... | collective-permute-start | bytes 122888 | tf_op jit(solution)/shard_map/ppermute | solution.py:366
  45.0 0.8 copy-start.4
  45.8 15.6 %collective-permute-start.11 = (f32[4,18,128]{2,1,0:T(8,128)S(1)}, f32[4,18,128]{2,1,0:T(8,128)S(1)}, u32[]{:S(2)}, u32[]{:S(2)}) collective-permute-start(f32[4,18,128]{2,1,0:T(8,128)S(1)} %get-tuple-element.44), channel_id=1, source_target_pairs={{0,2},{2,4},{4,6},{6,0},{1,3},{3,5},{5,7},{7,1},{8,10},{10,12},{12... | collective-permute-start | bytes 110600 | tf_op jit(solution)/shard_map/ppermute | solution.py:366
  47.4 14.0 %collective-permute-start.12 = (f32[4,18,128]{2,1,0:T(8,128)S(1)}, f32[4,18,128]{2,1,0:T(8,128)S(1)}, u32[]{:S(2)}, u32[]{:S(2)}) collective-permute-start(f32[4,18,128]{2,1,0:T(8,128)S(1)} %get-tuple-element.45), channel_id=1, source_target_pairs={{0,6},{2,0},{4,2},{6,4},{1,7},{3,1},{5,3},{7,5},{8,14},{10,8},{12,... | collective-permute-start | bytes 110600 | tf_op jit(solution)/shard_map/ppermute | solution.py:366
  48.3 8.5 %collective-permute-start.1 = (f32[304,128]{1,0:T(8,128)}, f32[304,128]{1,0:T(8,128)S(1)}, u32[]{:S(2)}, u32[]{:S(2)}) collective-permute-start(f32[304,128]{1,0:T(8,128)} %param.2), channel_id=1, source_target_pairs={{0,16},{8,24},{16,0},{24,8},{1,17},{9,25},{17,1},{25,9},{2,18},{10... | collective-permute-start | bytes 466952 | tf_op jit(solution)/shard_map/cond/branch_2_fun/ppermute | solution.py:366
  57.5 12.7 %copy-start.2 = (f32[4,32,16,128]{3,2,1,0:T(8,128)S(1)}, f32[4,32,16,128]{3,2,1,0:T(8,128)}, u32[]{:S(2)}) copy-start(f32[4,32,16,128]{3,2,1,0:T(8,128)} %f0.1) | copy-start | bytes 3145732
  57.5 3.9 %collective-permute-start.13 = (f32[4,16,128]{2,1,0:T(8,128)S(1)}, f32[4,16,128]{2,1,0:T(8,128)S(1)}, u32[]{:S(2)}, u32[]{:S(2)}) collective-permute-start(f32[4,16,128]{2,1,0:T(8,128)S(1)} %get-tuple-element.46), channel_id=1, source_target_pairs={{0,1},{1,0},{2,3},{3,2},{4,5},{5,4},{6,7},{7,6},{8,9},{9,8},{10,11... | collective-permute-start | bytes 98312 | tf_op jit(solution)/shard_map/ppermute | solution.py:383
  61.4 1.1 %copy-start.5 = (f32[4,20,16,128]{3,2,1,0:T(8,128)S(1)}, f32[4,20,16,128]{3,2,1,0:T(8,128)}, u32[]{:S(2)}) copy-start(f32[4,20,16,128]{3,2,1,0:T(8,128)} %copy-done.4) | copy-start | bytes 1966084
  62.5 7.7 %copy-start.3 = (f32[3,32,16,128]{3,2,1,0:T(8,128)S(1)}, f32[3,32,16,128]{3,2,1,0:T(8,128)}, u32[]{:S(2)}) copy-start(f32[3,32,16,128]{3,2,1,0:T(8,128)} %fw.1) | copy-start | bytes 2359300
  67.6 0.8 copy-start.6
  68.4 19.8 %collective-permute-start.14 = (f32[4,16,128]{2,1,0:T(8,128)S(1)}, f32[4,16,128]{2,1,0:T(8,128)S(1)}, u32[]{:S(2)}, u32[]{:S(2)}) collective-permute-start(f32[4,16,128]{2,1,0:T(8,128)S(1)} %get-tuple-element.48), channel_id=1, source_target_pairs={{0,2},{2,4},{4,6},{6,0},{1,3},{3,5},{5,7},{7,1},{8,10},{10,12},{12... | collective-permute-start | bytes 98312 | tf_op jit(solution)/shard_map/ppermute | solution.py:366
  68.4 19.8 %collective-permute-start.15 = (f32[4,16,128]{2,1,0:T(8,128)S(1)}, f32[4,16,128]{2,1,0:T(8,128)S(1)}, u32[]{:S(2)}, u32[]{:S(2)}) collective-permute-start(f32[4,16,128]{2,1,0:T(8,128)S(1)} %get-tuple-element.49), channel_id=1, source_target_pairs={{0,6},{2,0},{4,2},{6,4},{1,7},{3,1},{5,3},{7,5},{8,14},{10,8},{12,... | collective-permute-start | bytes 98312 | tf_op jit(solution)/shard_map/ppermute | solution.py:366
  70.1 18.1 %collective-permute-start.16 = (f32[4,16,128]{2,1,0:T(8,128)S(1)}, f32[4,16,128]{2,1,0:T(8,128)S(1)}, u32[]{:S(2)}, u32[]{:S(2)}) collective-permute-start(f32[4,16,128]{2,1,0:T(8,128)S(1)} %get-tuple-element.50), channel_id=1, source_target_pairs={{0,1},{1,0},{2,3},{3,2},{4,5},{5,4},{6,7},{7,6},{8,9},{9,8},{10,11... | collective-permute-start | bytes 98312 | tf_op jit(solution)/shard_map/ppermute | solution.py:383
  79.7 8.5 %copy-start.7 = (f32[4,18,16,128]{3,2,1,0:T(8,128)S(1)}, f32[4,18,16,128]{3,2,1,0:T(8,128)}, u32[]{:S(2)}) copy-start(f32[4,18,16,128]{3,2,1,0:T(8,128)} %copy-done.6) | copy-start | bytes 1769476
  79.8 7.8 %collective-permute-start.4 = (f32[4,8,8,128]{3,2,1,0:T(8,128)}, f32[4,8,8,128]{3,2,1,0:T(8,128)S(1)}, u32[]{:S(2)}, u32[]{:S(2)}) collective-permute-start(f32[4,8,8,128]{3,2,1,0:T(8,128)} %param.6), channel_id=1, source_target_pairs={{0,16},{8,24},{16,0},{24,8},{1,17},{9,25},{17,1},{25,9},{2,18},{10... | collective-permute-start | bytes 393224 | tf_op jit(solution)/shard_map/cond/branch_2_fun/ppermute | solution.py:366
  88.2 3.6 %copy-start.8 = (f32[4,8,8,128]{3,2,1,0:T(8,128)S(1)}, f32[4,8,8,128]{3,2,1,0:T(8,128)}, u32[]{:S(2)}) copy-start(f32[4,8,8,128]{3,2,1,0:T(8,128)} %get-tuple-element.57.avg) | copy-start | bytes 393220
where the time goes:
time: 91.5 us; the launch traced here: 92.8 us
  Pallas kernels  49.2 us (54%)
  waiting for transfers between devices  21.8 us (24%)
  starting transfers between devices  16.1 us (18%)
  local copies, waits for them, and re-layouts  4.06 us (4%)
  between operations  1.47 us (2%)
    pallas_call x2, Pallas kernels, pack(): pl.pallas_call(functools.partial(pack_kernel, s), out_shape=(shape(s.halo...  20.3 us
    ppermute x12, waiting for transfers between devices, ring(): lax.ppermute(array, axis, [(i, (i + by) % size) for i in range(size)])  17.5 us
    ppermute x12, starting transfers between devices, ring(): lax.ppermute(array, axis, [(i, (i + by) % size) for i in range(size)])  14.4 us
    pallas_call x3, Pallas kernels, shards(): pl.pallas_call(functools.partial(coarse_kernel, s, step), out_shape=tuple...  14.3 us
    pallas_call x1, Pallas kernels, shards(): pl.pallas_call(functools.partial(fine_kernel, s), out_shape=(shape(q, fx,...  9.54 us
    ppermute x3, waiting for transfers between devices, z_columns(): return lax.ppermute(zcol, 'gz', [(0, 1), (1, 0)])  4.35 us
    pallas_call x1, Pallas kernels, shards(): pl.pallas_call(functools.partial(slab_kernel, s), out_shape=(shape(s.slab...  4.11 us
    unnamed x18, local copies, waits for them, and re-layouts  2.74 us
  transfers between devices with their start and end apart: 15, of which 5 were waited for; matrix products, arithmetic and copies ran while one was open for 1% of the time, Pallas kernels for 37%

commit v1 on v0

--- a/solution.py
+++ b/solution.py
@@ -84,16 +84,7 @@
         move.wait()
 
 
-def column_pack(s, tiles):
-    total = None
-    for j, tile in enumerate(tiles):
-        lane = lanes_of(tile.shape)
-        part = pltpu.roll(jnp.where((lane == 0) | (lane == s.z - 1), tile, 0.0), 2 * j, 1)
-        total = part if total is None else total + part
-    return total
-
-
-def slab_kernel(s, c0, cw, lo, hi, slab, yup, ydn, zcol, pad0, pad1, pad2):
+def slab_kernel(s, c0, cw, lo, hi, slab, yup, ydn, pad0, pad1, pad2):
     q, x, y, z = s.q, s.x, s.y, s.z
     own = slice(TOP, TOP + y)
     zeros = jnp.zeros((s.ep, z), F32)
@@ -166,62 +157,128 @@
     slab[s.rows_y + s.ex : s.rows_e, :] = zeros[: s.ep - s.ex]
     for f in range(q):
         start = (f * s.ep + 1) * PAD + TOP
-        yup[f] = flats[0][pl.ds(start + y - 1, s.ex, stride=PAD), :]
-        ydn[f] = flats[0][pl.ds(start, s.ex, stride=PAD), :]
-        zcol[f] = column_pack(s, [pad0[f, a + 1, own, :] for a in range(s.ex)])
-
-
-def coarse_kernel(s, step, *refs):
+        for r in range(3):
+            yup[3 * f + r] = flats[0][pl.ds(start + y - 3 + r, s.ex, stride=PAD), :]
+            ydn[3 * f + r] = flats[0][pl.ds(start + r, s.ex, stride=PAD), :]
+    flat_cw = cw.reshape(3 * x * y, z)
+    flat_lo = lo.reshape(s.halo * y, z)
+    flat_hi = hi.reshape(s.halo * y, z)
+    for d in range(3):
+        at = (3 * q + 2 * d) * y
+        for r in range(2):
+            for dst, row in ((yup, y - 2 + r), (ydn, r)):
+                here = dst.at[3 * q + 2 * d + r]
+                here[0:2, :] = flat_lo[pl.ds(at + row, 2, stride=y), :]
+                here[2 : 2 + x, :] = flat_cw[pl.ds(d * x * y + row, x, stride=y), :]
+                here[2 + x : 4 + x, :] = flat_hi[pl.ds(at + row, 2, stride=y), :]
+
+
+WTOP, WPAD = 12, 40
+BLOCK = slice(8, 32)
+
+
+def assemble(s, c0, cw, lo, hi, ylo, yhi, pad, wind):
     q, x, y, z = s.q, s.x, s.y, s.z
-    (sides, c0, cw, lo, hi), refs = refs[:5], refs[5:]
-    if step:
-        state, refs = refs[0], refs[1:]
-    (ylo, yhi, zin, out), refs = refs[:4], refs[4:]
-    if step < 2:
-        (yup, ydn, zcol), refs = refs[:3], refs[3:]
-    (pad,) = refs
-    own = slice(TOP, TOP + y)
-    count = s.ex - 2 * step
-    flat = pad.reshape(q * s.ep * PAD, z)
-
-    def before(f, at):
-        if step == 0:
-            return layer_of(s, c0, lo, hi, f, at, 3, 0)
-        return state[f, at + 3 - step]
-
-    lane = lanes_of((y, z))
-    keep = jnp.where(lane % 2 == 1, sides[0, 0], sides[0, 1]).astype(F32)
-    for f in range(q):
-        flat[pl.ds(f * s.ep * PAD + TOP - 1, count, stride=PAD), :] = ylo[f]
-        flat[pl.ds(f * s.ep * PAD + TOP + y, count, stride=PAD), :] = yhi[f]
-        for j in range(count):
-            pad[f, j, own, :] = before(f, j + step - 2)
-    ghosts = [zin[f] * keep for f in range(q)]
-    for j in range(count):
-        at = j + step - 2
-        co = coefficients([layer_of(s, cw, lo, hi, d, at, 2, 3 * q) for d in range(3)])
+    flat = pad.reshape(q * s.ep * WPAD, z)
+    flat_wind = wind.reshape(3 * s.ex * 24, z)
+    for f in range(q):
+        for at in range(-3, x + 3):
+            pad[f, at + 3, WTOP : WTOP + y, :] = layer_of(s, c0, lo, hi, f, at, 3, 0)
+        base = (f * s.ep + 1) * WPAD + WTOP
+        for r in range(3):
+            flat[pl.ds(base - 3 + r, s.ex, stride=WPAD), :] = ylo[3 * f + r]
+            flat[pl.ds(base + y + r, s.ex, stride=WPAD), :] = yhi[3 * f + r]
+    for d in range(3):
+        for at in range(-2, x + 2):
+            wind[d, at + 2, 4 : 4 + y, :] = layer_of(s, cw, lo, hi, d, at, 2, 3 * q)
+        base = d * s.ex * 24 + 4
+        for r in range(2):
+            flat_wind[pl.ds(base - 2 + r, s.ex, stride=24), :] = ylo[3 * q + 2 * d + r]
+            flat_wind[pl.ds(base + y + r, s.ex, stride=24), :] = yhi[3 * q + 2 * d + r]
+
+
+def edge_lanes(s, lane, width):
+    return (lane < width) | (lane >= s.z - width)
+
+
+def zpack_kernel(s, c0, cw, lo, hi, ylo, yhi, out, pad, wind):
+    assemble(s, c0, cw, lo, hi, ylo, yhi, pad, wind)
+    lane = lanes_of((24, s.z))
+    keep = edge_lanes(s, lane, 3)
+    for m in range(s.q + 3):
+        total = None
+        for a in range(s.ex):
+            tile = pad[m, a + 1, BLOCK, :] if m < s.q else wind[m - s.q, a]
+            part = pltpu.roll(jnp.where(keep, tile, 0.0), (6 * a + 3) % s.z, 1)
+            total = part if total is None else total + part
+        out[m] = total
+
+
+def coarse_kernel(s, sides, c0, cw, lo, hi, ylo, yhi, zown, zin, out, pad0, pad1, pad2, wind, kept):
+    q, x, y, z = s.q, s.x, s.y, s.z
+    assemble(s, c0, cw, lo, hi, ylo, yhi, pad0, wind)
+    pads = (pad0, pad1, pad2)
+    lane = lanes_of((24, z))
+    is_first, is_last = lane == 0, lane == z - 1
+    ends = edge_lanes(s, lane, 1)
+    group = lane % 6
+    from_low = group == 2
+    from_high = group == 3
+    exists = jnp.where(group < 3, sides[0, 0], sides[0, 1]).astype(F32)
+    co_z = coefficients([zin[q + d] for d in range(3)])
+    beyond = [zin[f] * exists for f in range(q)]
+    nearest = [zown[f] for f in range(q)]
+    for step in range(3):
+        src = pads[step]
+        fraction = section_weights[step]
+        packed = [None] * q
+        for at in range(step - 2, x + 2 - step):
+            a = at + 2
+            co = coefficients([wind[d, a] for d in range(3)])
+            for f in range(q):
+                center = src[f, a + 1, BLOCK, :]
+                ghost = pltpu.roll(beyond[f], (-6 * a - 3) % z, 1)
+                rate = rate_of(
+                    co,
+                    center,
+                    src[f, a, BLOCK, :],
+                    src[f, a + 2, BLOCK, :],
+                    src[f, a + 1, 7:31, :],
+                    src[f, a + 1, 9:33, :],
+                    pltpu.roll(jnp.where(is_last, ghost, center), 1, 1),
+                    pltpu.roll(jnp.where(is_first, ghost, center), z - 1, 1),
+                )
+                base = center if step == 0 else pad0[f, a + 1, BLOCK, :]
+                value = base + fraction * rate
+                if step == 2:
+                    kept[f, at, :, :] = value
+                    continue
+                pads[step + 1][f, a + 1, BLOCK, :] = value
+                if step == 0 and 0 < a < s.ex - 1:
+                    part = pltpu.roll(jnp.where(ends, value, 0.0), (6 * a + 3) % z, 1)
+                    packed[f] = part if packed[f] is None else packed[f] + part
+        if step == 2:
+            break
+        later = []
         for f in range(q):
-            center = before(f, at)
-            ghost = pltpu.roll(ghosts[f], (-2 * j) % z, 1)
+            here, near = beyond[f], nearest[f]
             rate = rate_of(
-                co,
-                center,
-                before(f, at - 1),
-                before(f, at + 1),
-                pad[f, j, TOP - 1 : TOP + y - 1, :],
-                pad[f, j, TOP + 1 : TOP + y + 1, :],
-                pltpu.roll(jnp.where(lane == z - 1, ghost, center), 1, 1),
-                pltpu.roll(jnp.where(lane == 0, ghost, center), z - 1, 1),
+                co_z,
+                here,
+                pltpu.roll(here, 6, 1),
+                pltpu.roll(here, z - 6, 1),
+                pltpu.roll(here, 1, 0),
+                pltpu.roll(here, 23, 0),
+                pltpu.roll(jnp.where(from_low, near, here), 1, 1),
+                pltpu.roll(jnp.where(from_high, near, here), z - 1, 1),
             )
-            base = center if step == 0 else layer_of(s, c0, lo, hi, f, at, 3, 0)
-            out[f, j] = base + section_weights[step] * rate
-    if step < 2:
-        made = out.reshape(q * count * y, z)
-        for f in range(q):
-            start = (f * count + 1) * y
-            yup[f] = made[pl.ds(start + y - 1, count - 2, stride=y), :]
-            ydn[f] = made[pl.ds(start, count - 2, stride=y), :]
-            zcol[f] = column_pack(s, [out[f, j + 1] for j in range(count - 2)])
+            base = here if step == 0 else zin[f] * exists
+            later.append((base + fraction * rate) * exists)
+        beyond = later
+        nearest = packed
+    for f in range(q):
+        for at in range(x):
+            out[f, at] = kept[f, at, 4 : 4 + y, :]
 
 
 def fine_kernel(s, f0, fw, flo, fhi, slab, out, avg, *scratch):
@@ -366,23 +423,28 @@
     return lax.ppermute(array, axis, [(i, (i + by) % size) for i in range(size)])
 
 
-def move_by(array, amount):
+def move_by(array, amount, beside=None):
     size = lax.axis_size("gx")
+    work, operands = beside or (lambda: (), ())
     if size <= 8:
-        return lax.switch(amount, [lambda a, k=k: a if k == 0 else ring(a, "gx", k) for k in range(size)], array)
+
+        def branch(by, array, *operands):
+            return array if by == 0 else ring(array, "gx", by), work(*operands)
+
+        return lax.switch(amount, [functools.partial(branch, by) for by in range(size)], array, *operands)
     for bit in range((size - 1).bit_length()):
         array = jnp.where((amount >> bit) % 2 == 1, ring(array, "gx", 1 << bit), array)
-    return array
-
-
-def z_columns(zcol):
+    return array, work(*operands)
+
+
+def z_columns(zown):
     size = lax.axis_size("gz")
     if size == 1:
-        return jnp.zeros_like(zcol)
+        return zown
     if size == 2:
-        return lax.ppermute(zcol, "gz", [(0, 1), (1, 0)])
-    odd = lax.broadcasted_iota(jnp.int32, zcol.shape, 2) % 2 == 1
-    return jnp.where(odd, ring(zcol, "gz", 1), ring(zcol, "gz", -1))
+        return lax.ppermute(zown, "gz", [(0, 1), (1, 0)])
+    below = lax.broadcasted_iota(jnp.int32, zown.shape, 2) % 6 < 3
+    return jnp.where(below, ring(zown, "gz", 1), ring(zown, "gz", -1))
 
 
 def pack(s, fields, wind, name):
@@ -390,7 +452,7 @@
         functools.partial(pack_kernel, s),
         out_shape=(shape(s.halo, s.y, s.z),) * 2,
         in_specs=[HBM, HBM],
-        out_specs=(ANY, ANY),
+        out_specs=(VMEM, VMEM),
         scratch_shapes=[pltpu.SemaphoreType.DMA((2 * (s.q + 3),))],
         name=name,
     )(fields, wind)
@@ -407,38 +469,43 @@
     lo, hi = ring(up, "gx", 1), ring(down, "gx", -1)
     up, down = pack(s, fine_fields, fine_wind, "pack_fine")
     flo, fhi = ring(up, "gx", 1), ring(down, "gx", -1)
-    padded = pltpu.VMEM((q, s.ep, PAD, z), F32)
-    slab, yup, ydn, zcol = pl.pallas_call(
+    edges = s.halo
+    slab, yup, ydn = pl.pallas_call(
         functools.partial(slab_kernel, s),
-        out_shape=(shape(s.slab, z), shape(q, s.ex, z), shape(q, s.ex, z), shape(q, y, z)),
+        out_shape=(shape(s.slab, z), shape(edges, s.ex, z), shape(edges, s.ex, z)),
         in_specs=[VMEM] * 4,
-        out_specs=(VMEM,) * 4,
-        scratch_shapes=[padded] * 3,
+        out_specs=(VMEM,) * 3,
+        scratch_shapes=[pltpu.VMEM((q, s.ep, PAD, z), F32)] * 3,
         compiler_params=params(24),
         name="slab",
     )(coarse_fields, coarse_wind, lo, hi)
-    state = None
-    for step in range(3):
-        count = s.ex - 2 * step
-        ylo, yhi = ring(yup, "gy", 1), ring(ydn, "gy", -1)
-        zin = z_columns(zcol)
-        outs = [shape(q, count, y, z)]
-        if step < 2:
-            outs += [shape(q, count - 2, z), shape(q, count - 2, z), shape(q, y, z)]
-        ins = [neighbours, coarse_fields, coarse_wind, lo, hi] + ([state] if step else []) + [ylo, yhi, zin]
-        made = pl.pallas_call(
-            functools.partial(coarse_kernel, s, step),
-            out_shape=tuple(outs),
-            in_specs=[SMEM] + [VMEM] * (len(ins) - 1),
-            out_specs=(VMEM,) * len(outs),
-            scratch_shapes=[padded],
-            compiler_params=params(16),
+    ylo, yhi = ring(yup, "gy", 1), ring(ydn, "gy", -1)
+    slab, _ = move_by(slab, (size - offset) % size)
+    padded = pltpu.VMEM((q, s.ep, WPAD, z), F32)
+    wind_rows = pltpu.VMEM((3, s.ex, 24, z), F32)
+    zown = pl.pallas_call(
+        functools.partial(zpack_kernel, s),
+        out_shape=shape(q + 3, 24, z),
+        in_specs=[VMEM] * 6,
+        out_specs=VMEM,
+        scratch_shapes=[padded, wind_rows],
+        compiler_params=params(24),
+        name="zpack",
+    )(coarse_fields, coarse_wind, lo, hi, ylo, yhi)
+    zin = z_columns(zown)
+
+    def coarse(*operands):
+        return pl.pallas_call(
+            functools.partial(coarse_kernel, s),
+            out_shape=shape(q, x, y, z),
+            in_specs=[SMEM] + [VMEM] * 8,
+            out_specs=VMEM,
+            scratch_shapes=[padded] * 3 + [wind_rows, pltpu.VMEM((q, x, 24, z), F32)],
+            compiler_params=params(24),
+            cost_estimate=pl.CostEstimate(flops=40_000_000, bytes_accessed=4_000_000, transcendentals=0),
             name="coarse",
-        )(*ins)
-        state = made[0]
-        if step < 2:
-            yup, ydn, zcol = made[1:]
-    slab = move_by(slab, (size - offset) % size)
+        )(*operands)
+
     layers = fx + 6
     fine_next, averaged = pl.pallas_call(
         functools.partial(fine_kernel, s),
@@ -457,7 +524,11 @@
         compiler_params=params(32),
         name="fine",
     )(fine_fields, fine_wind, flo, fhi, slab)
-    averaged = move_by(averaged, offset)
+    averaged, state = move_by(
+        averaged,
+        offset,
+        (coarse, (neighbours, coarse_fields, coarse_wind, lo, hi, ylo, yhi, zown, zin)),
+    )
     coarse_next = pl.pallas_call(
         functools.partial(merge_kernel, s),
         out_shape=shape(q, x, y, z),

time: 91.5 us -> 70.1 us (0.77); the launches traced: 92.8 us -> 69.8 us
  Pallas kernels: 49.2 us -> 40.4 us
  waiting for transfers between devices: 21.8 us -> 13.8 us
  local copies, waits for them, and re-layouts: 4.06 us -> 0.71 us
  starting transfers between devices: 16.1 us -> 13.1 us
    pallas_call x2, Pallas kernels: 20.3 us -> 3.49 us  [pack(): pl.pallas_call(functools.partial(pack_kernel, s), out_shape=(shape(s.halo...]
    pallas_call x3 -> x2, Pallas kernels: 14.3 us -> 22.4 us  [the longest x1 21.2 us: coarse(): pl.pallas_call(functools.partial(coarse_kernel, s), out_shape=shape(q, x,...]
    ppermute x3 -> x1, waiting for transfers between devices: 4.35 us -> 0.01 us  [z_columns(): return lax.ppermute(zown, 'gz', [(0, 1), (1, 0)])]
    ppermute x12 -> x8, waiting for transfers between devices: 17.5 us -> 13.8 us  [ring(): lax.ppermute(array, axis, [(i, (i + by) % size) for i in range(size)])]
    ppermute x12 -> x8, starting transfers between devices: 14.4 us -> 11.5 us  [ring(): lax.ppermute(array, axis, [(i, (i + by) % size) for i in range(size)])]
    unnamed x18 -> x16, local copies, waits for them, and re-layouts: 2.74 us -> 0.03 us
  transfers between devices with their start and end apart: 15 -> 9, of which waited for: 5 -> 3; matrix products, arithmetic and copies ran while one was open for 1% -> 1% of each run, Pallas kernels for 37% -> 48%
where the time goes in v1:
time: 70.1 us; the launch traced here: 69.8 us
  Pallas kernels  40.4 us (58%)
  waiting for transfers between devices  13.8 us (20%)
  starting transfers between devices  13.1 us (19%)
  between operations  1.46 us (2%)
  local copies, waits for them, and re-layouts  0.71 us (1%)
    pallas_call x1, Pallas kernels, coarse(): pl.pallas_call(functools.partial(coarse_kernel, s), out_shape=shape(q, x,...  21.2 us
    ppermute x8, waiting for transfers between devices, ring(): lax.ppermute(array, axis, [(i, (i + by) % size) for i in range(size)])  13.8 us
    ppermute x8, starting transfers between devices, ring(): lax.ppermute(array, axis, [(i, (i + by) % size) for i in range(size)])  11.5 us
    pallas_call x1, Pallas kernels, shards(): pl.pallas_call(functools.partial(fine_kernel, s), out_shape=(shape(q, fx,...  9.56 us
    pallas_call x1, Pallas kernels, shards(): pl.pallas_call(functools.partial(slab_kernel, s), out_shape=(shape(s.slab...  4 us
    pallas_call x2, Pallas kernels, pack(): pl.pallas_call(functools.partial(pack_kernel, s), out_shape=(shape(s.halo...  3.49 us
    ppermute x1, starting transfers between devices, z_columns(): return lax.ppermute(zown, 'gz', [(0, 1), (1, 0)])  1.52 us
  transfers between devices with their start and end apart: 9, of which 3 were waited for; matrix products, arithmetic and copies ran while one was open for 1% of the time, Pallas kernels for 48%

profile of v1, /device:TPU:0, one launch (start us, length us, event | category | flops | bytes accessed | tf_op | source)
XLA Modules:
  0.0 69.8 jit_solution(7457677150263310605)
XLA Ops:
  0.6 0.0 copy-start.3
  0.6 0.0 copy-start.2
  0.6 1.8 %pack_coarse.1 = (f32[18,16,128]{2,1,0:T(8,128)}, f32[18,16,128]{2,1,0:T(8,128)}) custom-call(f32[4,16,16,128]{3,2,1,0:T(8,128)} %c0.3, f32[3,16,16,128]{3,2,1,0:T(8,128)} %cw.3), custom_call_target="tpu_custom_call" | custom-call | tf_op jit(solution)/shard_map/pack_coarse/pallas_call | solution.py:451
  2.4 3.1 %collective-permute-start.6 = (f32[18,16,128]{2,1,0:T(8,128)}, f32[18,16,128]{2,1,0:T(8,128)S(1)}, u32[]{:S(2)}, u32[]{:S(2)}) collective-permute-start(f32[18,16,128]{2,1,0:T(8,128)} %get-tuple-element.142), channel_id=1, source_target_pairs={{0,8},{8,16},{16,24},{24,0},{1,9},{9,17},{17,25},{25,1},{2,10},{10... | collective-permute-start | bytes 442376 | tf_op jit(solution)/shard_map/ppermute | solution.py:423
  5.5 2.1 %collective-permute-start.7 = (f32[18,16,128]{2,1,0:T(8,128)}, f32[18,16,128]{2,1,0:T(8,128)S(1)}, u32[]{:S(2)}, u32[]{:S(2)}) collective-permute-start(f32[18,16,128]{2,1,0:T(8,128)} %get-tuple-element.143), channel_id=1, source_target_pairs={{0,24},{8,0},{16,8},{24,16},{1,25},{9,1},{17,9},{25,17},{2,26},{10... | collective-permute-start | bytes 442376 | tf_op jit(solution)/shard_map/ppermute | solution.py:423
  7.6 4.9 %collective-permute-done.6.lo = f32[18,16,128]{2,1,0:T(8,128)S(1)} collective-permute-done((f32[18,16,128]{2,1,0:T(8,128)}, f32[18,16,128]{2,1,0:T(8,128)S(1)}, u32[]{:S(2)}, u32[]{:S(2)}) %collective-permute-start.6) | collective-permute-done | bytes 147488 | tf_op jit(solution)/shard_map/ppermute | solution.py:423
  12.5 0.0 copy-start.4
  12.5 1.7 %collective-permute-done.7.hi = f32[18,16,128]{2,1,0:T(8,128)S(1)} collective-permute-done((f32[18,16,128]{2,1,0:T(8,128)}, f32[18,16,128]{2,1,0:T(8,128)S(1)}, u32[]{:S(2)}, u32[]{:S(2)}) %collective-permute-start.7) | collective-permute-done | bytes 147488 | tf_op jit(solution)/shard_map/ppermute | solution.py:423
  14.2 0.0 copy-done.3
  14.2 0.0 copy-done.2
  14.2 0.0 copy-start.6
  14.2 4.0 %slab.1 = (f32[304,128]{1,0:T(8,128)}, f32[18,20,128]{2,1,0:T(8,128)S(1)}, f32[18,20,128]{2,1,0:T(8,128)S(1)}) custom-call(f32[4,16,16,128]{3,2,1,0:T(8,128)S(1)} %copy-done.2, f32[3,16,16,128]{3,2,1,0:T(8,128)S(1)} %copy-done.3, f32[18,16,128]{2,1,0:T(8,128)S(1)} %collective-permute-done.6.lo, f32[18,16,128]{2,1,0:T(8,128)S(1)} %collective-permute-done.7.hi), custom_call_target="tpu_custom_call" | custom-call | tf_op jit(solution)/shard_map/slab/pallas_call | solution.py:473
  18.2 0.0 collective-permute-start.8
  18.2 1.7 %collective-permute-start.9 = (f32[18,20,128]{2,1,0:T(8,128)S(1)}, f32[18,20,128]{2,1,0:T(8,128)S(1)}, u32[]{:S(2)}, u32[]{:S(2)}) collective-permute-start(f32[18,20,128]{2,1,0:T(8,128)S(1)} %get-tuple-element.145), channel_id=1, source_target_pairs={{0,6},{2,0},{4,2},{6,4},{1,7},{3,1},{5,3},{7,5},{8,14},{10,8},{12,... | collective-permute-start | bytes 552968 | tf_op jit(solution)/shard_map/ppermute | solution.py:423
  19.9 1.7 %pack_fine.1 = (f32[18,16,128]{2,1,0:T(8,128)}, f32[18,16,128]{2,1,0:T(8,128)}) custom-call(f32[4,32,16,128]{3,2,1,0:T(8,128)} %f0.1, f32[3,32,16,128]{3,2,1,0:T(8,128)} %fw.1), custom_call_target="tpu_custom_call" | custom-call | tf_op jit(solution)/shard_map/pack_fine/pallas_call | solution.py:451
  21.7 1.2 %collective-permute-start.11 = (f32[18,16,128]{2,1,0:T(8,128)}, f32[18,16,128]{2,1,0:T(8,128)S(1)}, u32[]{:S(2)}, u32[]{:S(2)}) collective-permute-start(f32[18,16,128]{2,1,0:T(8,128)} %get-tuple-element.146), channel_id=1, source_target_pairs={{0,8},{8,16},{16,24},{24,0},{1,9},{9,17},{17,25},{25,1},{2,10},{10... | collective-permute-start | bytes 442376 | tf_op jit(solution)/shard_map/ppermute | solution.py:423
  22.9 2.7 %collective-permute-start.12 = (f32[18,16,128]{2,1,0:T(8,128)}, f32[18,16,128]{2,1,0:T(8,128)S(1)}, u32[]{:S(2)}, u32[]{:S(2)}) collective-permute-start(f32[18,16,128]{2,1,0:T(8,128)} %get-tuple-element.147), channel_id=1, source_target_pairs={{0,24},{8,0},{16,8},{24,16},{1,25},{9,1},{17,9},{25,17},{2,26},{10... | collective-permute-start | bytes 442376 | tf_op jit(solution)/shard_map/ppermute | solution.py:423
  26.2 0.0 copy-start
  26.2 0.0 collective-permute-done.8.ylo
  26.3 0.0 collective-permute-done.9.yhi
  26.3 0.0 copy-done.4
  26.3 0.0 copy-done.6
  26.3 1.2 %zpack.1 = f32[7,24,128]{2,1,0:T(8,128)} custom-call(f32[4,16,16,128]{3,2,1,0:T(8,128)S(1)} %copy-done.2, f32[3,16,16,128]{3,2,1,0:T(8,128)S(1)} %copy-done.3, f32[18,16,128]{2,1,0:T(8,128)S(1)} %collective-permute-done.6.lo, f32[18,16,128]{2,1,0:T(8,128)S(1)} %collective-permute-done.7.hi, f32[18,20,128]{2,1,0:T(8,128)S(1)} %collective-permute-done.8.ylo, ...), custom_call_target="tpu_custom_call" | custom-call | tf_op jit(solution)/shard_map/zpack/pallas_call | solution.py:486
  27.5 0.0 copy-start.1
  27.5 1.5 %collective-permute-start.10 = (f32[7,24,128]{2,1,0:T(8,128)}, f32[7,24,128]{2,1,0:T(8,128)}, u32[]{:S(2)}, u32[]{:S(2)}) collective-permute-start(f32[7,24,128]{2,1,0:T(8,128)} %zpack.1), channel_id=1, source_target_pairs={{0,1},{1,0},{2,3},{3,2},{4,5},{5,4},{6,7},{7,6},{8,9},{9,8},{10,11... | collective-permute-start | bytes 258056 | tf_op jit(solution)/shard_map/ppermute | solution.py:445
  29.0 0.1 add_convert_fusion
  29.1 7.9 %conditional.2 = (f32[304,128]{1,0:T(8,128)}) conditional(s32[]{:T(128)} %clamp.7, f32[304,128]{1,0:T(8,128)} %get-tuple-element.148, f32[304,128]{1,0:T(8,128)} %get-tuple-element.148, f32[304,128]{1,0:T(8,128)} %get-tuple-element.148, f32[304,128]{1,0:T(8,128)} %get-tuple-element.148), branch_computations={%region_0.1_spmd, %region_1.2_spmd, %region_2.3_spmd, %region_3.4_... | conditional | bytes 933936 | solution.py:434
  29.1 0.0 collective-permute-start
  29.1 7.2 %collective-permute-done = f32[304,128]{1,0:T(8,128)S(1)} collective-permute-done((f32[304,128]{1,0:T(8,128)}, f32[304,128]{1,0:T(8,128)S(1)}, u32[]{:S(2)}, u32[]{:S(2)}) %collective-permute-start) | collective-permute-done | bytes 155680 | tf_op jit(solution)/shard_map/cond/branch_1_fun/ppermute | solution.py:423
  36.3 0.7 copy.8
  37.0 0.0 copy-start.5
  37.0 0.0 copy-start.7
  37.0 0.0 collective-permute-done.11.flo
  37.0 0.0 collective-permute-done.12.fhi
  37.0 0.0 copy-done
  37.0 0.0 copy-done.1
  37.0 9.6 %fine.1 = (f32[4,32,16,128]{3,2,1,0:T(8,128)}, f32[4,8,8,128]{3,2,1,0:T(8,128)S(1)}) custom-call(f32[4,32,16,128]{3,2,1,0:T(8,128)S(1)} %copy-done, f32[3,32,16,128]{3,2,1,0:T(8,128)S(1)} %copy-done.1, f32[18,16,128]{2,1,0:T(8,128)S(1)} %collective-permute-done.11.flo, f32[18,16,128]{2,1,0:T(8,128)S(1)} %collective-permute-done.12.fhi, ...), custom_call_target="tpu_custom_call" | custom-call | tf_op jit(solution)/shard_map/fine/pallas_call | solution.py:510
  46.6 0.0 collective-permute-done.10
  46.6 0.0 copy-done.5
  46.6 0.0 copy-done.7
  46.6 22.3 %conditional.3 = (f32[4,8,8,128]{3,2,1,0:T(8,128)S(1)}, f32[4,16,16,128]{3,2,1,0:T(8,128)S(1)}) conditional(s32[]{:T(128)} %clamp.6, (s32[1,2]{1,0:T(1,128)S(1)}, f32[4,16,16,128]{3,2,1,0:T(8,128)S(1)}, f32[3,16,16,128]{3,2,1,0:T(8,128)S(1)}, f32[18,16,128]{2,1,0:T(8,128)S(1)}, f32[18,16,128]{2,1,0:T(8,128)S(1)}, ...), branch_computations={%region_4.5_spmd, %region_5.6_spmd, %region_6.7_spmd, %region_7.8_... | conditional | flops 40000000 | bytes 4786488 | solution.py:434
  46.8 0.8 %collective-permute-start.5 = (f32[4,8,8,128]{3,2,1,0:T(8,128)S(1)}, f32[4,8,8,128]{3,2,1,0:T(8,128)S(1)}, u32[]{:S(2)}, u32[]{:S(2)}) collective-permute-start(f32[4,8,8,128]{3,2,1,0:T(8,128)S(1)} %get-tuple-element.119), channel_id=1, source_target_pairs={{0,24},{8,0},{16,8},{24,16},{1,25},{9,1},{17,9},{25,17},{2,26},{10... | collective-permute-start | bytes 393224 | tf_op jit(solution)/shard_map/cond/branch_3_fun/ppermute | solution.py:423
  47.6 21.2 %coarse.7 = f32[4,16,16,128]{3,2,1,0:T(8,128)S(1)} custom-call(s32[1,2]{1,0:T(1,128)S(1)} %get-tuple-element.120.sides, f32[4,16,16,128]{3,2,1,0:T(8,128)S(1)} %get-tuple-element.121.c0, f32[3,16,16,128]{3,2,1,0:T(8,128)S(1)} %get-tuple-element.122.cw, f32[18,16,128]{2,1,0:T(8,128)S(1)} %get-tuple-element.123.lo, f32[18,16,128]{2,1,0:T(8,128)S(1)} %get-tuple-element.124.hi, ...), custom_call_target="tpu_custom_call" | custom-call | flops 40000000 | bytes 4000000 | tf_op jit(solution)/shard_map/cond/branch_3_fun/coarse/pallas_call | solution.py:498
  68.8 0.0 collective-permute-done.5
  68.9 0.9 %merge.1 = f32[4,16,16,128]{3,2,1,0:T(8,128)} custom-call(f32[4,16,16,128]{3,2,1,0:T(8,128)S(1)} %get-tuple-element.150.c3, f32[4,8,8,128]{3,2,1,0:T(8,128)S(1)} %get-tuple-element.151.avg), custom_call_target="tpu_custom_call" | custom-call | tf_op jit(solution)/shard_map/merge/pallas_call | solution.py:532
  (1 shorter events, 0.0 us)
Async XLA Ops:
  0.6 13.6 %copy-start.3 = (f32[3,16,16,128]{3,2,1,0:T(8,128)S(1)}, f32[3,16,16,128]{3,2,1,0:T(8,128)}, u32[]{:S(2)}) copy-start(f32[3,16,16,128]{3,2,1,0:T(8,128)} %cw.3) | copy-start | bytes 1179652
  0.6 13.5 %copy-start.2 = (f32[4,16,16,128]{3,2,1,0:T(8,128)S(1)}, f32[4,16,16,128]{3,2,1,0:T(8,128)}, u32[]{:S(2)}) copy-start(f32[4,16,16,128]{3,2,1,0:T(8,128)} %c0.3) | copy-start | bytes 1572868
  2.4 10.0 %collective-permute-start.6 = (f32[18,16,128]{2,1,0:T(8,128)}, f32[18,16,128]{2,1,0:T(8,128)S(1)}, u32[]{:S(2)}, u32[]{:S(2)}) collective-permute-start(f32[18,16,128]{2,1,0:T(8,128)} %get-tuple-element.142), channel_id=1, source_target_pairs={{0,8},{8,16},{16,24},{24,0},{1,9},{9,17},{17,25},{25,1},{2,10},{10... | collective-permute-start | bytes 442376 | tf_op jit(solution)/shard_map/ppermute | solution.py:423
  5.5 8.7 %collective-permute-start.7 = (f32[18,16,128]{2,1,0:T(8,128)}, f32[18,16,128]{2,1,0:T(8,128)S(1)}, u32[]{:S(2)}, u32[]{:S(2)}) collective-permute-start(f32[18,16,128]{2,1,0:T(8,128)} %get-tuple-element.143), channel_id=1, source_target_pairs={{0,24},{8,0},{16,8},{24,16},{1,25},{9,1},{17,9},{25,17},{2,26},{10... | collective-permute-start | bytes 442376 | tf_op jit(solution)/shard_map/ppermute | solution.py:423
  12.5 13.8 %copy-start.4 = (f32[18,16,128]{2,1,0:T(8,128)}, f32[18,16,128]{2,1,0:T(8,128)S(1)}, u32[]{:S(2)}) copy-start(f32[18,16,128]{2,1,0:T(8,128)S(1)} %collective-permute-done.6.lo) | copy-start | bytes 442372
  14.2 12.1 %copy-start.6 = (f32[18,16,128]{2,1,0:T(8,128)}, f32[18,16,128]{2,1,0:T(8,128)S(1)}, u32[]{:S(2)}) copy-start(f32[18,16,128]{2,1,0:T(8,128)S(1)} %collective-permute-done.7.hi) | copy-start | bytes 442372
  18.2 8.1 %collective-permute-start.8 = (f32[18,20,128]{2,1,0:T(8,128)S(1)}, f32[18,20,128]{2,1,0:T(8,128)S(1)}, u32[]{:S(2)}, u32[]{:S(2)}) collective-permute-start(f32[18,20,128]{2,1,0:T(8,128)S(1)} %get-tuple-element.144), channel_id=1, source_target_pairs={{0,2},{2,4},{4,6},{6,0},{1,3},{3,5},{5,7},{7,1},{8,10},{10,12},{12... | collective-permute-start | bytes 552968 | tf_op jit(solution)/shard_map/ppermute | solution.py:423
  18.2 8.1 %collective-permute-start.9 = (f32[18,20,128]{2,1,0:T(8,128)S(1)}, f32[18,20,128]{2,1,0:T(8,128)S(1)}, u32[]{:S(2)}, u32[]{:S(2)}) collective-permute-start(f32[18,20,128]{2,1,0:T(8,128)S(1)} %get-tuple-element.145), channel_id=1, source_target_pairs={{0,6},{2,0},{4,2},{6,4},{1,7},{3,1},{5,3},{7,5},{8,14},{10,8},{12,... | collective-permute-start | bytes 552968 | tf_op jit(solution)/shard_map/ppermute | solution.py:423
  21.7 15.3 %collective-permute-start.11 = (f32[18,16,128]{2,1,0:T(8,128)}, f32[18,16,128]{2,1,0:T(8,128)S(1)}, u32[]{:S(2)}, u32[]{:S(2)}) collective-permute-start(f32[18,16,128]{2,1,0:T(8,128)} %get-tuple-element.146), channel_id=1, source_target_pairs={{0,8},{8,16},{16,24},{24,0},{1,9},{9,17},{17,25},{25,1},{2,10},{10... | collective-permute-start | bytes 442376 | tf_op jit(solution)/shard_map/ppermute | solution.py:423
  22.9 14.1 %collective-permute-start.12 = (f32[18,16,128]{2,1,0:T(8,128)}, f32[18,16,128]{2,1,0:T(8,128)S(1)}, u32[]{:S(2)}, u32[]{:S(2)}) collective-permute-start(f32[18,16,128]{2,1,0:T(8,128)} %get-tuple-element.147), channel_id=1, source_target_pairs={{0,24},{8,0},{16,8},{24,16},{1,25},{9,1},{17,9},{25,17},{2,26},{10... | collective-permute-start | bytes 442376 | tf_op jit(solution)/shard_map/ppermute | solution.py:423
  26.2 10.7 %copy-start = (f32[4,32,16,128]{3,2,1,0:T(8,128)S(1)}, f32[4,32,16,128]{3,2,1,0:T(8,128)}, u32[]{:S(2)}) copy-start(f32[4,32,16,128]{3,2,1,0:T(8,128)} %f0.1) | copy-start | bytes 3145732
  27.5 9.5 %copy-start.1 = (f32[3,32,16,128]{3,2,1,0:T(8,128)S(1)}, f32[3,32,16,128]{3,2,1,0:T(8,128)}, u32[]{:S(2)}) copy-start(f32[3,32,16,128]{3,2,1,0:T(8,128)} %fw.1) | copy-start | bytes 2359300
  27.5 19.1 %collective-permute-start.10 = (f32[7,24,128]{2,1,0:T(8,128)}, f32[7,24,128]{2,1,0:T(8,128)}, u32[]{:S(2)}, u32[]{:S(2)}) collective-permute-start(f32[7,24,128]{2,1,0:T(8,128)} %zpack.1), channel_id=1, source_target_pairs={{0,1},{1,0},{2,3},{3,2},{4,5},{5,4},{6,7},{7,6},{8,9},{9,8},{10,11... | collective-permute-start | bytes 258056 | tf_op jit(solution)/shard_map/ppermute | solution.py:445
  29.1 7.2 %collective-permute-start = (f32[304,128]{1,0:T(8,128)}, f32[304,128]{1,0:T(8,128)S(1)}, u32[]{:S(2)}, u32[]{:S(2)}) collective-permute-start(f32[304,128]{1,0:T(8,128)} %param.1), channel_id=1, source_target_pairs={{0,8},{8,16},{16,24},{24,0},{1,9},{9,17},{17,25},{25,1},{2,10},{10... | collective-permute-start | bytes 466952 | tf_op jit(solution)/shard_map/cond/branch_1_fun/ppermute | solution.py:423
  37.0 9.6 %copy-start.5 = (f32[18,16,128]{2,1,0:T(8,128)S(1)}, f32[18,16,128]{2,1,0:T(8,128)}, u32[]{:S(2)}) copy-start(f32[18,16,128]{2,1,0:T(8,128)} %copy-done.4) | copy-start | bytes 442372
  37.0 9.6 %copy-start.7 = (f32[18,16,128]{2,1,0:T(8,128)S(1)}, f32[18,16,128]{2,1,0:T(8,128)}, u32[]{:S(2)}) copy-start(f32[18,16,128]{2,1,0:T(8,128)} %copy-done.6) | copy-start | bytes 442372
  46.8 22.0 %collective-permute-start.5 = (f32[4,8,8,128]{3,2,1,0:T(8,128)S(1)}, f32[4,8,8,128]{3,2,1,0:T(8,128)S(1)}, u32[]{:S(2)}, u32[]{:S(2)}) collective-permute-start(f32[4,8,8,128]{3,2,1,0:T(8,128)S(1)} %get-tuple-element.119), channel_id=1, source_target_pairs={{0,24},{8,0},{16,8},{24,16},{1,25},{9,1},{17,9},{25,17},{2,26},{10... | collective-permute-start | bytes 393224 | tf_op jit(solution)/shard_map/cond/branch_3_fun/ppermute | solution.py:423

commit v2 on v1

--- a/solution.py
+++ b/solution.py
@@ -25,6 +25,7 @@
         self.ep = -(-self.ex // 8) * 8
         self.fe = self.fx + 4
         self.halo = 3 * self.q + 6
+        self.rows_f, self.rows_w = self.q * (3 * self.x + 6), 3 * (2 * self.x + 2)
         self.rows_y = 3 * self.q * self.ex
         self.rows_e = self.rows_y + self.ep
         self.rows_z = self.sy + 2
@@ -67,16 +68,17 @@
     return own[member, at]
 
 
-def pack_kernel(s, fields, wind, up, down, sems):
-    size = fields.shape[1]
+def pack_kernel(s, c0, cw, f0, fw, cup, cdown, fup, fdown, sems):
     moves = []
-    for f in range(s.q):
-        moves.append((fields.at[f, size - 3 : size], up.at[3 * f : 3 * f + 3]))
-        moves.append((fields.at[f, 0:3], down.at[3 * f : 3 * f + 3]))
-    for d in range(3):
-        at = 3 * s.q + 2 * d
-        moves.append((wind.at[d, size - 2 : size], up.at[at : at + 2]))
-        moves.append((wind.at[d, 0:2], down.at[at : at + 2]))
+    for fields, wind, up, down in ((c0, cw, cup, cdown), (f0, fw, fup, fdown)):
+        size = fields.shape[1]
+        for f in range(s.q):
+            moves.append((fields.at[f, size - 3 : size], up.at[3 * f : 3 * f + 3]))
+            moves.append((fields.at[f, 0:3], down.at[3 * f : 3 * f + 3]))
+        for d in range(3):
+            at = 3 * s.q + 2 * d
+            moves.append((wind.at[d, size - 2 : size], up.at[at : at + 2]))
+            moves.append((wind.at[d, 0:2], down.at[at : at + 2]))
     moves = [pltpu.make_async_copy(src, dst, sems.at[i]) for i, (src, dst) in enumerate(moves)]
     for move in moves:
         move.start()
@@ -84,7 +86,33 @@
         move.wait()
 
 
-def slab_kernel(s, c0, cw, lo, hi, slab, yup, ydn, pad0, pad1, pad2):
+def y_rows(s, members, width):
+    below, above = [], []
+    for out, extra in ((below, lambda r: r), (above, lambda r: width - 1 - r)):
+        at = 0
+        for m in range(members):
+            for r in range(width):
+                out.append((m, r, extra(r), at))
+                at += s.x + 2 * extra(r)
+    return below, above
+
+
+def ypack_kernel(s, c0, cw, lo, hi, up, dn):
+    x, y, z = s.x, s.y, s.z
+    flat_lo = lo.reshape(s.halo * y, z)
+    flat_hi = hi.reshape(s.halo * y, z)
+    for own, members, width, first, place in ((c0, s.q, 3, 0, 0), (cw, 3, 2, 3 * s.q, s.rows_f)):
+        flat = own.reshape(members * x * y, z)
+        for dst, rows, start in zip((up, dn), y_rows(s, members, width), (y - width, 0)):
+            for m, r, e, at in rows:
+                row, at = start + r, at + place
+                if e:
+                    dst[at : at + e, :] = flat_lo[pl.ds((first + width * (m + 1) - e) * y + row, e, stride=y), :]
+                    dst[at + e + x : at + x + 2 * e, :] = flat_hi[pl.ds((first + width * m) * y + row, e, stride=y), :]
+                dst[at + e : at + e + x, :] = flat[pl.ds(m * x * y + row, x, stride=y), :]
+
+
+def slab_kernel(s, c0, cw, lo, hi, slab, pad0, pad1, pad2, wind):
     q, x, y, z = s.q, s.x, s.y, s.z
     own = slice(TOP, TOP + y)
     zeros = jnp.zeros((s.ep, z), F32)
@@ -98,25 +126,34 @@
             pad0[f, at + 3, own, :] = layer_of(s, c0, lo, hi, f, at, 3, 0)
         pad2[f, 1, own, :] = zeros[:y]
         pad2[f, s.ex, own, :] = zeros[:y]
+    for d in range(3):
+        for at in range(-2, x + 2):
+            wind[d, at + 2] = layer_of(s, cw, lo, hi, d, at, 2, 3 * q)
     for step in range(2):
-        src, dst = pads[step], pads[step + 1]
-        for at in range(step - 2, x + 2 - step):
-            j = at + 3
-            co = coefficients([layer_of(s, cw, lo, hi, d, at, 2, 3 * q) for d in range(3)])
-            for f in range(q):
-                center = src[f, j, own, :]
-                rate = rate_of(
-                    co,
-                    center,
-                    src[f, j - 1, own, :],
-                    src[f, j + 1, own, :],
-                    src[f, j, TOP - 1 : TOP + y - 1, :],
-                    src[f, j, TOP + 1 : TOP + y + 1, :],
-                    pltpu.roll(center, 1, 1),
-                    pltpu.roll(center, z - 1, 1),
-                )
-                base = center if step == 0 else pad0[f, j, own, :]
-                dst[f, j, own, :] = base + section_weights[step] * rate
+        src, flat, dst = pads[step], flats[step], pads[step + 1]
+
+        def two_layers(t, carry, step=step, src=src, flat=flat, dst=dst):
+            for odd in range(2):
+                j = 2 * t + odd + step + 1
+                co = coefficients([wind[d, j - 1] for d in range(3)])
+                for f in range(q):
+                    center = src[f, j, own, :]
+                    row = (f * s.ep + j) * PAD + TOP
+                    rate = rate_of(
+                        co,
+                        center,
+                        src[f, j - 1, own, :],
+                        src[f, j + 1, own, :],
+                        flat[pl.ds(row - 1, y), :],
+                        flat[pl.ds(row + 1, y), :],
+                        pltpu.roll(center, 1, 1),
+                        pltpu.roll(center, z - 1, 1),
+                    )
+                    base = center if step == 0 else pad0[f, j, own, :]
+                    dst[f, j, own, :] = base + section_weights[step] * rate
+            return carry
+
+        lax.fori_loop(0, s.ex // 2 - step, two_layers, 0)
     lane_x = lanes_of((s.ex, z))
     lane_y = lanes_of((y, z))
     ends = None
@@ -155,54 +192,38 @@
         slab[at : at + s.rows_z, :] = zfaces[s.ly - 1 : s.ly + s.sy + 1]
     slab[s.rows_y : s.rows_y + s.ex, :] = ends
     slab[s.rows_y + s.ex : s.rows_e, :] = zeros[: s.ep - s.ex]
-    for f in range(q):
-        start = (f * s.ep + 1) * PAD + TOP
-        for r in range(3):
-            yup[3 * f + r] = flats[0][pl.ds(start + y - 3 + r, s.ex, stride=PAD), :]
-            ydn[3 * f + r] = flats[0][pl.ds(start + r, s.ex, stride=PAD), :]
-    flat_cw = cw.reshape(3 * x * y, z)
-    flat_lo = lo.reshape(s.halo * y, z)
-    flat_hi = hi.reshape(s.halo * y, z)
-    for d in range(3):
-        at = (3 * q + 2 * d) * y
-        for r in range(2):
-            for dst, row in ((yup, y - 2 + r), (ydn, r)):
-                here = dst.at[3 * q + 2 * d + r]
-                here[0:2, :] = flat_lo[pl.ds(at + row, 2, stride=y), :]
-                here[2 : 2 + x, :] = flat_cw[pl.ds(d * x * y + row, x, stride=y), :]
-                here[2 + x : 4 + x, :] = flat_hi[pl.ds(at + row, 2, stride=y), :]
 
 
 WTOP, WPAD = 12, 40
 BLOCK = slice(8, 32)
 
 
-def assemble(s, c0, cw, lo, hi, ylo, yhi, pad, wind):
+def assemble(s, c0, cw, lo, hi, below, above, pad, wind):
     q, x, y, z = s.q, s.x, s.y, s.z
     flat = pad.reshape(q * s.ep * WPAD, z)
     flat_wind = wind.reshape(3 * s.ex * 24, z)
     for f in range(q):
         for at in range(-3, x + 3):
             pad[f, at + 3, WTOP : WTOP + y, :] = layer_of(s, c0, lo, hi, f, at, 3, 0)
-        base = (f * s.ep + 1) * WPAD + WTOP
-        for r in range(3):
-            flat[pl.ds(base - 3 + r, s.ex, stride=WPAD), :] = ylo[3 * f + r]
-            flat[pl.ds(base + y + r, s.ex, stride=WPAD), :] = yhi[3 * f + r]
     for d in range(3):
         for at in range(-2, x + 2):
             wind[d, at + 2, 4 : 4 + y, :] = layer_of(s, cw, lo, hi, d, at, 2, 3 * q)
-        base = d * s.ex * 24 + 4
-        for r in range(2):
-            flat_wind[pl.ds(base - 2 + r, s.ex, stride=24), :] = ylo[3 * q + 2 * d + r]
-            flat_wind[pl.ds(base + y + r, s.ex, stride=24), :] = yhi[3 * q + 2 * d + r]
+    for src, rows, start in zip((below, above), y_rows(s, q, 3), (WTOP - 3, WTOP + y)):
+        for m, r, e, at in rows:
+            count = x + 2 * e
+            flat[pl.ds((m * s.ep + 3 - e) * WPAD + start + r, count, stride=WPAD), :] = src[at : at + count, :]
+    for src, rows, start in zip((below, above), y_rows(s, 3, 2), (2, 4 + y)):
+        for m, r, e, at in rows:
+            count, at = x + 2 * e, at + s.rows_f
+            flat_wind[pl.ds((m * s.ex + 2 - e) * 24 + start + r, count, stride=24), :] = src[at : at + count, :]
 
 
 def edge_lanes(s, lane, width):
     return (lane < width) | (lane >= s.z - width)
 
 
-def zpack_kernel(s, c0, cw, lo, hi, ylo, yhi, out, pad, wind):
-    assemble(s, c0, cw, lo, hi, ylo, yhi, pad, wind)
+def zpack_kernel(s, c0, cw, lo, hi, below, above, out, pad, wind):
+    assemble(s, c0, cw, lo, hi, below, above, pad, wind)
     lane = lanes_of((24, s.z))
     keep = edge_lanes(s, lane, 3)
     for m in range(s.q + 3):
@@ -214,71 +235,78 @@
         out[m] = total
 
 
-def coarse_kernel(s, sides, c0, cw, lo, hi, ylo, yhi, zown, zin, out, pad0, pad1, pad2, wind, kept):
+def coarse_kernel(
+    s, sides, c0, cw, lo, hi, below, above, zown, zin, out, pad0, pad1, pad2, wind, beyond, nearest
+):
     q, x, y, z = s.q, s.x, s.y, s.z
-    assemble(s, c0, cw, lo, hi, ylo, yhi, pad0, wind)
+    assemble(s, c0, cw, lo, hi, below, above, pad0, wind)
     pads = (pad0, pad1, pad2)
     lane = lanes_of((24, z))
-    is_first, is_last = lane == 0, lane == z - 1
-    ends = edge_lanes(s, lane, 1)
     group = lane % 6
     from_low = group == 2
     from_high = group == 3
     exists = jnp.where(group < 3, sides[0, 0], sides[0, 1]).astype(F32)
     co_z = coefficients([zin[q + d] for d in range(3)])
-    beyond = [zin[f] * exists for f in range(q)]
-    nearest = [zown[f] for f in range(q)]
+    for f in range(q):
+        beyond[0, f] = zin[f] * exists
+        nearest[0, f] = zown[f]
     for step in range(3):
-        src = pads[step]
-        fraction = section_weights[step]
-        packed = [None] * q
-        for at in range(step - 2, x + 2 - step):
-            a = at + 2
-            co = coefficients([wind[d, a] for d in range(3)])
+        src, fraction = pads[step], section_weights[step]
+        flat = src.reshape(q * s.ep * WPAD, z)
+        flat0 = pad0.reshape(q * s.ep * WPAD, z)
+        flat_wind = wind.reshape(3 * s.ex * 24, z)
+        flat_beyond = beyond.reshape(3 * q * 24, z)
+        skip, height = (0, 24) if step < 2 else (4, y)
+        here = lanes_of((height, z))
+        is_first, is_last = here == 0, here == z - 1
+
+        def layer(a, packed, step=step, flat=flat, fraction=fraction, skip=skip, height=height):
+            made = []
+            co = coefficients([flat_wind[pl.ds((d * s.ex + a) * 24 + skip, height), :] for d in range(3)])
             for f in range(q):
-                center = src[f, a + 1, BLOCK, :]
-                ghost = pltpu.roll(beyond[f], (-6 * a - 3) % z, 1)
+                row = (f * s.ep + a + 1) * WPAD + 8 + skip
+                center = flat[pl.ds(row, height), :]
+                ghost = pltpu.roll(flat_beyond[pl.ds((step * q + f) * 24 + skip, height), :], 2 * z - 6 * a - 3, 1)
                 rate = rate_of(
                     co,
                     center,
-                    src[f, a, BLOCK, :],
-                    src[f, a + 2, BLOCK, :],
-                    src[f, a + 1, 7:31, :],
-                    src[f, a + 1, 9:33, :],
+                    flat[pl.ds(row - WPAD, height), :],
+                    flat[pl.ds(row + WPAD, height), :],
+                    flat[pl.ds(row - 1, height), :],
+                    flat[pl.ds(row + 1, height), :],
                     pltpu.roll(jnp.where(is_last, ghost, center), 1, 1),
                     pltpu.roll(jnp.where(is_first, ghost, center), z - 1, 1),
                 )
-                base = center if step == 0 else pad0[f, a + 1, BLOCK, :]
+                base = center if step == 0 else flat0[pl.ds(row, height), :]
                 value = base + fraction * rate
                 if step == 2:
-                    kept[f, at, :, :] = value
-                    continue
-                pads[step + 1][f, a + 1, BLOCK, :] = value
-                if step == 0 and 0 < a < s.ex - 1:
-                    part = pltpu.roll(jnp.where(ends, value, 0.0), (6 * a + 3) % z, 1)
-                    packed[f] = part if packed[f] is None else packed[f] + part
+                    out[f, a - 2] = value
+                else:
+                    pads[step + 1][f, a + 1, BLOCK, :] = value
+                if step == 0:
+                    made.append(packed[f] + pltpu.roll(jnp.where(is_first | is_last, value, 0.0), 6 * a + 3, 1))
+            return tuple(made)
+
+        begin, end = step, s.ex - step
+        start = tuple(jnp.zeros((24, z), F32) for _ in range(q)) if step == 0 else ()
+        packed = lax.fori_loop(begin, end, layer, start)
         if step == 2:
             break
-        later = []
         for f in range(q):
-            here, near = beyond[f], nearest[f]
+            if step == 0:
+                nearest[1, f] = packed[f]
+            ghost, near = beyond[step, f], nearest[step, f]
             rate = rate_of(
                 co_z,
-                here,
-                pltpu.roll(here, 6, 1),
-                pltpu.roll(here, z - 6, 1),
-                pltpu.roll(here, 1, 0),
-                pltpu.roll(here, 23, 0),
-                pltpu.roll(jnp.where(from_low, near, here), 1, 1),
-                pltpu.roll(jnp.where(from_high, near, here), z - 1, 1),
+                ghost,
+                pltpu.roll(ghost, 6, 1),
+                pltpu.roll(ghost, z - 6, 1),
+                pltpu.roll(ghost, 1, 0),
+                pltpu.roll(ghost, 23, 0),
+                pltpu.roll(jnp.where(from_low, near, ghost), 1, 1),
+                pltpu.roll(jnp.where(from_high, near, ghost), z - 1, 1),
             )
-            base = here if step == 0 else zin[f] * exists
-            later.append((base + fraction * rate) * exists)
-        beyond = later
-        nearest = packed
-    for f in range(q):
-        for at in range(x):
-            out[f, at] = kept[f, at, 4 : 4 + y, :]
+            beyond[step + 1, f] = (beyond[0, f] + fraction * rate) * exists
 
 
 def fine_kernel(s, f0, fw, flo, fhi, slab, out, avg, *scratch):
@@ -316,10 +344,11 @@
                 e = 4 * (q * k + f) + 2 * side + 1
                 corner = jnp.where(edge, 0.25 * pltpu.roll(ends, z - e, 1), 0.0)
                 first = (k * q + f) * s.ex
-                faces[: s.ex, :] = wide[first : first + s.ex, side * z : side * z + z] + corner
-                a = faces[0:half, :]
-                b = faces[1 : half + 1, :]
-                d = faces[2 : half + 2, :]
+                here = faces.at[(k * q + f) * 2 + side]
+                here[: s.ex, :] = wide[first : first + s.ex, side * z : side * z + z] + corner
+                a = here[0:half, :]
+                b = here[1 : half + 1, :]
+                d = here[2 : half + 2, :]
                 row = TOP - 1 if side == 0 else TOP + y
                 base = (f * layers + 1) * PAD + row
                 flat[pl.ds(base, half, stride=2 * PAD), :] = 0.25 * a + 0.75 * b
@@ -330,9 +359,9 @@
         a = slab[at : at + s.sy, :]
         b = slab[at + 1 : at + 1 + s.sy, :]
         d = slab[at + 2 : at + 2 + s.sy, :]
-        zface[pl.ds(0, s.sy, stride=2), :] = 0.25 * a + 0.75 * b
-        zface[pl.ds(1, s.sy, stride=2), :] = 0.75 * b + 0.25 * d
-        a = zface[...]
+        zface[pl.ds(f * y, s.sy, stride=2), :] = 0.25 * a + 0.75 * b
+        zface[pl.ds(f * y + 1, s.sy, stride=2), :] = 0.75 * b + 0.25 * d
+        a = zface[f * y : f * y + y, :]
         b = pltpu.roll(a, z - 2, 1)
         d = pltpu.roll(a, z - 4, 1)
         evens.append(0.25 * a + 0.75 * b)
@@ -343,24 +372,26 @@
     is_first, is_last = lane == 0, lane == z - 1
     for k in range(3):
         src, fraction = states[k], section_weights[k]
+        flat = src.reshape(q * layers * PAD, z)
         begin, end = (0, half) if k < 2 else (1, half - 1)
         shift = -(2 * s.ex * k + 2 * begin) % z
         carried = tuple(pltpu.roll(g, shift, 1) if shift else g for g in evens + odds)
 
-        def pair_of_layers(t, ghosts, k=k, src=src, fraction=fraction):
+        def pair_of_layers(t, ghosts, k=k, src=src, flat=flat, fraction=fraction):
             for odd in range(2):
                 b = 2 * t + odd
                 co = coefficients([wide_wind[d, b] for d in range(3)])
                 for f in range(q):
                     center = src[f, b + 1, rows, :]
                     ghost = ghosts[odd * q + f]
+                    row = (f * layers + b + 1) * PAD + TOP
                     rate = rate_of(
                         co,
                         center,
                         src[f, b, rows, :],
                         src[f, b + 2, rows, :],
-                        src[f, b + 1, TOP - 1 : TOP + y - 1, :],
-                        src[f, b + 1, TOP + 1 : TOP + y + 1, :],
+                        flat[pl.ds(row - 1, y), :],
+                        flat[pl.ds(row + 1, y), :],
                         pltpu.roll(jnp.where(is_last, ghost, center), 1, 1),
                         pltpu.roll(jnp.where(is_first, ghost, center), z - 1, 1),
                     )
@@ -410,6 +441,9 @@
 ANY = pl.BlockSpec(memory_space=pl.ANY)
 
 
+SHORT = pl.CostEstimate(flops=1, bytes_accessed=1, transcendentals=0)
+
+
 def params(megabytes):
     return pltpu.CompilerParams(vmem_limit_bytes=megabytes << 20)
 
@@ -447,17 +481,6 @@
     return jnp.where(below, ring(zown, "gz", 1), ring(zown, "gz", -1))
 
 
-def pack(s, fields, wind, name):
-    return pl.pallas_call(
-        functools.partial(pack_kernel, s),
-        out_shape=(shape(s.halo, s.y, s.z),) * 2,
-        in_specs=[HBM, HBM],
-        out_specs=(VMEM, VMEM),
-        scratch_shapes=[pltpu.SemaphoreType.DMA((2 * (s.q + 3),))],
-        name=name,
-    )(fields, wind)
-
-
 def shards(coarse_fields, coarse_wind, fine_fields, fine_wind, fine_owner):
     s = Sizes(coarse_fields.shape, fine_fields.shape)
     q, x, y, z, fx = s.q, s.x, s.y, s.z, s.fx
@@ -465,22 +488,37 @@
     offset = (fine_owner[0, 0, 0] - lax.axis_index("gx")) % size
     level = lax.axis_index("gz")
     neighbours = jnp.stack([level > 0, level < lax.axis_size("gz") - 1]).astype(jnp.int32).reshape(1, 2)
-    up, down = pack(s, coarse_fields, coarse_wind, "pack_coarse")
-    lo, hi = ring(up, "gx", 1), ring(down, "gx", -1)
-    up, down = pack(s, fine_fields, fine_wind, "pack_fine")
-    flo, fhi = ring(up, "gx", 1), ring(down, "gx", -1)
-    edges = s.halo
-    slab, yup, ydn = pl.pallas_call(
+    cup, cdown, fup, fdown = pl.pallas_call(
+        functools.partial(pack_kernel, s),
+        out_shape=(shape(s.halo, y, z),) * 4,
+        in_specs=[HBM] * 4,
+        out_specs=(VMEM,) * 4,
+        scratch_shapes=[pltpu.SemaphoreType.DMA((4 * (q + 3),))],
+        cost_estimate=SHORT,
+        name="pack",
+    )(coarse_fields, coarse_wind, fine_fields, fine_wind)
+    lo, hi = ring(cup, "gx", 1), ring(cdown, "gx", -1)
+    flo, fhi = ring(fup, "gx", 1), ring(fdown, "gx", -1)
+    yup, ydn = pl.pallas_call(
+        functools.partial(ypack_kernel, s),
+        out_shape=(shape(s.rows_f + s.rows_w, z),) * 2,
+        in_specs=[VMEM] * 4,
+        out_specs=(VMEM,) * 2,
+        cost_estimate=SHORT,
+        name="ypack",
+    )(coarse_fields, coarse_wind, lo, hi)
+    yrows = [ring(yup, "gy", 1), ring(ydn, "gy", -1)]
+    slab = pl.pallas_call(
         functools.partial(slab_kernel, s),
-        out_shape=(shape(s.slab, z), shape(edges, s.ex, z), shape(edges, s.ex, z)),
+        out_shape=shape(s.slab, z),
         in_specs=[VMEM] * 4,
-        out_specs=(VMEM,) * 3,
-        scratch_shapes=[pltpu.VMEM((q, s.ep, PAD, z), F32)] * 3,
+        out_specs=VMEM,
+        scratch_shapes=[pltpu.VMEM((q, s.ep, PAD, z), F32)] * 3 + [pltpu.VMEM((3, s.ex, y, z), F32)],
         compiler_params=params(24),
+        cost_estimate=SHORT,
         name="slab",
     )(coarse_fields, coarse_wind, lo, hi)
-    ylo, yhi = ring(yup, "gy", 1), ring(ydn, "gy", -1)
-    slab, _ = move_by(slab, (size - offset) % size)
+    yrows, slab = lax.optimization_barrier((yrows, slab))
     padded = pltpu.VMEM((q, s.ep, WPAD, z), F32)
     wind_rows = pltpu.VMEM((3, s.ex, 24, z), F32)
     zown = pl.pallas_call(
@@ -490,17 +528,19 @@
         out_specs=VMEM,
         scratch_shapes=[padded, wind_rows],
         compiler_params=params(24),
+        cost_estimate=SHORT,
         name="zpack",
-    )(coarse_fields, coarse_wind, lo, hi, ylo, yhi)
+    )(coarse_fields, coarse_wind, lo, hi, *yrows)
     zin = z_columns(zown)
-
+    slab, flo, fhi = lax.optimization_barrier((slab, flo, fhi))
+    slab, _ = move_by(slab, (size - offset) % size)
     def coarse(*operands):
         return pl.pallas_call(
             functools.partial(coarse_kernel, s),
             out_shape=shape(q, x, y, z),
             in_specs=[SMEM] + [VMEM] * 8,
             out_specs=VMEM,
-            scratch_shapes=[padded] * 3 + [wind_rows, pltpu.VMEM((q, x, 24, z), F32)],
+            scratch_shapes=[padded] * 3 + [wind_rows, pltpu.VMEM((3, q, 24, z), F32), pltpu.VMEM((2, q, 24, z), F32)],
             compiler_params=params(24),
             cost_estimate=pl.CostEstimate(flops=40_000_000, bytes_accessed=4_000_000, transcendentals=0),
             name="coarse",
@@ -517,8 +557,8 @@
             pltpu.VMEM((q, layers, PAD, z), F32),
             pltpu.VMEM((q, layers, PAD, z), F32),
             pltpu.VMEM((3, s.fe, y, z), F32),
-            pltpu.VMEM((s.ep, z), F32),
-            pltpu.VMEM((y, z), F32),
+            pltpu.VMEM((6 * q, s.ep, z), F32),
+            pltpu.VMEM((q * y, z), F32),
             pltpu.SemaphoreType.DMA((2 + 2 * (q + 3),)),
         ],
         compiler_params=params(32),
@@ -527,7 +567,7 @@
     averaged, state = move_by(
         averaged,
         offset,
-        (coarse, (neighbours, coarse_fields, coarse_wind, lo, hi, ylo, yhi, zown, zin)),
+        (coarse, (neighbours, coarse_fields, coarse_wind, lo, hi, *yrows, zown, zin)),
     )
     coarse_next = pl.pallas_call(
         functools.partial(merge_kernel, s),

time: 70.1 us -> 60.7 us (0.87)
  Pallas kernels: 40.4 us -> 31.4 us
    pallas_call x1, Pallas kernels: 21.2 us -> 11.7 us  [coarse(): pl.pallas_call(functools.partial(coarse_kernel, s), out_shape=shape(q, x,...]
    ppermute x8, starting transfers between devices: 11.5 us -> 10.8 us  [ring(): lax.ppermute(array, axis, [(i, (i + by) % size) for i in range(size)])]
  transfers between devices with their start and end apart: 9 -> 9, of which waited for: 3 -> 3; matrix products, arithmetic and copies ran while one was open for 1% -> 1% of each run, Pallas kernels for 48% -> 46%
where the time goes in v2:
time: 60.7 us; the launch traced here: 60.4 us
  Pallas kernels  31.4 us (52%)
  waiting for transfers between devices  13.8 us (23%)
  starting transfers between devices  12.4 us (20%)
  between operations  1.4 us (2%)
  local copies, waits for them, and re-layouts  1.36 us (2%)
    ppermute x8, waiting for transfers between devices, ring(): lax.ppermute(array, axis, [(i, (i + by) % size) for i in range(size)])  13.8 us
    pallas_call x1, Pallas kernels, coarse(): pl.pallas_call(functools.partial(coarse_kernel, s), out_shape=shape(q, x,...  11.7 us
    ppermute x8, starting transfers between devices, ring(): lax.ppermute(array, axis, [(i, (i + by) % size) for i in range(size)])  10.8 us
    pallas_call x1, Pallas kernels, shards(): pl.pallas_call(functools.partial(fine_kernel, s), out_shape=(shape(q, fx,...  9.49 us
    pallas_call x1, Pallas kernels, shards(): pl.pallas_call(functools.partial(slab_kernel, s), out_shape=shape(s.slab,...  5.13 us
    pallas_call x1, Pallas kernels, shards(): pl.pallas_call(functools.partial(pack_kernel, s), out_shape=(shape(s.halo...  2.09 us
    ppermute x1, starting transfers between devices, z_columns(): return lax.ppermute(zown, 'gz', [(0, 1), (1, 0)])  1.52 us
  transfers between devices with their start and end apart: 9, of which 3 were waited for; matrix products, arithmetic and copies ran while one was open for 1% of the time, Pallas kernels for 46%

profile of v2, /device:TPU:0, one launch (start us, length us, event | category | flops | bytes accessed | tf_op | source)
XLA Modules:
  0.0 60.4 jit_solution(12615417653238299820)
XLA Ops:
  0.6 0.0 copy-start.3
  0.6 0.0 copy-start.2
  0.6 2.1 %pack.1 = (f32[18,16,128]{2,1,0:T(8,128)}, f32[18,16,128]{2,1,0:T(8,128)}, f32[18,16,128]{2,1,0:T(8,128)}, f32[18,16,128]{2,1,0:T(8,128)}) custom-call(f32[4,16,16,128]{3,2,1,0:T(8,128)} %c0.7, f32[3,16,16,128]{3,2,1,0:T(8,128)} %cw.7, f32[4,32,16,128]{3,2,1,0:T(8,128)} %f0.3, f32[3,32,16,128]{3,2,1,0:T(8,128)} %fw.3), custom_call_target="tpu_custom_call" | custom-call | flops 1 | bytes 1 | tf_op jit(solution)/shard_map/pack/pallas_call | solution.py:491
  2.7 3.1 %collective-permute-start.6 = (f32[18,16,128]{2,1,0:T(8,128)}, f32[18,16,128]{2,1,0:T(8,128)S(1)}, u32[]{:S(2)}, u32[]{:S(2)}) collective-permute-start(f32[18,16,128]{2,1,0:T(8,128)} %get-tuple-element.147), channel_id=1, source_target_pairs={{0,8},{8,16},{16,24},{24,0},{1,9},{9,17},{17,25},{25,1},{2,10},{10... | collective-permute-start | bytes 442376 | tf_op jit(solution)/shard_map/ppermute | solution.py:457
  5.8 2.1 %collective-permute-start.7 = (f32[18,16,128]{2,1,0:T(8,128)}, f32[18,16,128]{2,1,0:T(8,128)S(1)}, u32[]{:S(2)}, u32[]{:S(2)}) collective-permute-start(f32[18,16,128]{2,1,0:T(8,128)} %get-tuple-element.148), channel_id=1, source_target_pairs={{0,24},{8,0},{16,8},{24,16},{1,25},{9,1},{17,9},{25,17},{2,26},{10... | collective-permute-start | bytes 442376 | tf_op jit(solution)/shard_map/ppermute | solution.py:457
  7.9 4.9 %collective-permute-done.6.lo = f32[18,16,128]{2,1,0:T(8,128)S(1)} collective-permute-done((f32[18,16,128]{2,1,0:T(8,128)}, f32[18,16,128]{2,1,0:T(8,128)S(1)}, u32[]{:S(2)}, u32[]{:S(2)}) %collective-permute-start.6) | collective-permute-done | bytes 147488 | tf_op jit(solution)/shard_map/ppermute | solution.py:457
  12.8 1.7 %collective-permute-done.7.hi = f32[18,16,128]{2,1,0:T(8,128)S(1)} collective-permute-done((f32[18,16,128]{2,1,0:T(8,128)}, f32[18,16,128]{2,1,0:T(8,128)S(1)}, u32[]{:S(2)}, u32[]{:S(2)}) %collective-permute-start.7) | collective-permute-done | bytes 147488 | tf_op jit(solution)/shard_map/ppermute | solution.py:457
  14.5 0.0 copy-done.3
  14.5 0.0 copy-done.2
  14.5 0.8 %ypack.1 = (f32[318,128]{1,0:T(8,128)}, f32[318,128]{1,0:T(8,128)}) custom-call(f32[4,16,16,128]{3,2,1,0:T(8,128)S(1)} %copy-done.2, f32[3,16,16,128]{3,2,1,0:T(8,128)S(1)} %copy-done.3, f32[18,16,128]{2,1,0:T(8,128)S(1)} %collective-permute-done.6.lo, f32[18,16,128]{2,1,0:T(8,128)S(1)} %collective-permute-done.7.hi), custom_call_target="tpu_custom_call" | custom-call | flops 1 | bytes 1 | tf_op jit(solution)/shard_map/ypack/pallas_call | solution.py:502
  15.3 0.0 collective-permute-start.8
  15.3 1.7 %collective-permute-start.9 = (f32[318,128]{1,0:T(8,128)}, f32[318,128]{1,0:T(8,128)S(1)}, u32[]{:S(2)}, u32[]{:S(2)}) collective-permute-start(f32[318,128]{1,0:T(8,128)} %get-tuple-element.150), channel_id=1, source_target_pairs={{0,6},{2,0},{4,2},{6,4},{1,7},{3,1},{5,3},{7,5},{8,14},{10,8},{12,... | collective-permute-start | bytes 488456 | tf_op jit(solution)/shard_map/ppermute | solution.py:457
  17.1 1.1 %collective-permute-start.11 = (f32[18,16,128]{2,1,0:T(8,128)}, f32[18,16,128]{2,1,0:T(8,128)S(1)}, u32[]{:S(2)}, u32[]{:S(2)}) collective-permute-start(f32[18,16,128]{2,1,0:T(8,128)} %get-tuple-element.154), channel_id=1, source_target_pairs={{0,8},{8,16},{16,24},{24,0},{1,9},{9,17},{17,25},{25,1},{2,10},{10... | collective-permute-start | bytes 442376 | tf_op jit(solution)/shard_map/ppermute | solution.py:457
  18.2 2.7 %collective-permute-start.12 = (f32[18,16,128]{2,1,0:T(8,128)}, f32[18,16,128]{2,1,0:T(8,128)S(1)}, u32[]{:S(2)}, u32[]{:S(2)}) collective-permute-start(f32[18,16,128]{2,1,0:T(8,128)} %get-tuple-element.155), channel_id=1, source_target_pairs={{0,24},{8,0},{16,8},{24,16},{1,25},{9,1},{17,9},{25,17},{2,26},{10... | collective-permute-start | bytes 442376 | tf_op jit(solution)/shard_map/ppermute | solution.py:457
  21.6 5.1 %slab.1 = f32[304,128]{1,0:T(8,128)} custom-call(f32[4,16,16,128]{3,2,1,0:T(8,128)S(1)} %copy-done.2, f32[3,16,16,128]{3,2,1,0:T(8,128)S(1)} %copy-done.3, f32[18,16,128]{2,1,0:T(8,128)S(1)} %collective-permute-done.6.lo, f32[18,16,128]{2,1,0:T(8,128)S(1)} %collective-permute-done.7.hi), custom_call_target="tpu_custom_call" | custom-call | flops 1 | bytes 1 | tf_op jit(solution)/shard_map/slab/pallas_call | solution.py:511
  26.7 0.0 copy-start
  26.7 0.0 collective-permute-done.8.below
  26.7 0.0 collective-permute-done.9.above
  26.8 0.0 copy-start.4
  26.8 0.7 %copy-done.4 = f32[318,128]{1,0:T(8,128)} copy-done((f32[318,128]{1,0:T(8,128)}, f32[318,128]{1,0:T(8,128)S(1)}, u32[]{:S(2)}) %copy-start.4) | copy-done | bytes 162840
  27.4 1.2 %zpack.1 = f32[7,24,128]{2,1,0:T(8,128)} custom-call(f32[4,16,16,128]{3,2,1,0:T(8,128)S(1)} %copy-done.2, f32[3,16,16,128]{3,2,1,0:T(8,128)S(1)} %copy-done.3, f32[18,16,128]{2,1,0:T(8,128)S(1)} %collective-permute-done.6.lo, f32[18,16,128]{2,1,0:T(8,128)S(1)} %collective-permute-done.7.hi, f32[318,128]{1,0:T(8,128)S(1)} %collective-permute-done.8.below, ...), custom_call_target="tpu_custom_call" | custom-call | flops 1 | bytes 1 | tf_op jit(solution)/shard_map/zpack/pallas_call | solution.py:524
  28.6 0.0 copy-start.1
  28.6 1.5 %collective-permute-start.10 = (f32[7,24,128]{2,1,0:T(8,128)}, f32[7,24,128]{2,1,0:T(8,128)}, u32[]{:S(2)}, u32[]{:S(2)}) collective-permute-start(f32[7,24,128]{2,1,0:T(8,128)} %zpack.1), channel_id=1, source_target_pairs={{0,1},{1,0},{2,3},{3,2},{4,5},{5,4},{6,7},{7,6},{8,9},{9,8},{10,11... | collective-permute-start | bytes 258056 | tf_op jit(solution)/shard_map/ppermute | solution.py:479
  30.1 0.1 add_convert_fusion
  30.2 0.0 collective-permute-done.11.flo
  30.2 0.0 collective-permute-done.12.fhi
  30.2 7.9 %conditional.2 = (f32[304,128]{1,0:T(8,128)}) conditional(s32[]{:T(128)} %clamp.7, f32[304,128]{1,0:T(8,128)} %slab.1, f32[304,128]{1,0:T(8,128)} %slab.1, f32[304,128]{1,0:T(8,128)} %slab.1, f32[304,128]{1,0:T(8,128)} %slab.1), branch_computations={%region_0.1_spmd, %region_1.2_spmd, %region_2.3_spmd, %region_3.4_... | conditional | bytes 933936 | solution.py:468
  30.2 0.0 collective-permute-start
  30.2 7.2 %collective-permute-done = f32[304,128]{1,0:T(8,128)S(1)} collective-permute-done((f32[304,128]{1,0:T(8,128)}, f32[304,128]{1,0:T(8,128)S(1)}, u32[]{:S(2)}, u32[]{:S(2)}) %collective-permute-start) | collective-permute-done | bytes 155680 | tf_op jit(solution)/shard_map/cond/branch_1_fun/ppermute | solution.py:457
  37.5 0.7 %copy.8 = f32[304,128]{1,0:T(8,128)} copy(f32[304,128]{1,0:T(8,128)S(1)} %collective-permute-done) | data formatting | bytes 311296 | tf_op jit(solution)/shard_map/cond
  38.1 0.0 copy-done
  38.1 0.0 copy-done.1
  38.1 0.0 copy-start.5
  38.1 9.5 %fine.1 = (f32[4,32,16,128]{3,2,1,0:T(8,128)}, f32[4,8,8,128]{3,2,1,0:T(8,128)S(1)}) custom-call(f32[4,32,16,128]{3,2,1,0:T(8,128)S(1)} %copy-done, f32[3,32,16,128]{3,2,1,0:T(8,128)S(1)} %copy-done.1, f32[18,16,128]{2,1,0:T(8,128)S(1)} %collective-permute-done.11.flo, f32[18,16,128]{2,1,0:T(8,128)S(1)} %collective-permute-done.12.fhi, ...), custom_call_target="tpu_custom_call" | custom-call | tf_op jit(solution)/shard_map/fine/pallas_call | solution.py:550
  47.6 0.0 collective-permute-done.10
  47.6 0.0 copy-done.5
  47.6 11.9 %conditional.3 = (f32[4,8,8,128]{3,2,1,0:T(8,128)S(1)}, f32[4,16,16,128]{3,2,1,0:T(8,128)S(1)}) conditional(s32[]{:T(128)} %clamp.6, (s32[1,2]{1,0:T(1,128)S(1)}, f32[4,16,16,128]{3,2,1,0:T(8,128)S(1)}, f32[3,16,16,128]{3,2,1,0:T(8,128)S(1)}, f32[18,16,128]{2,1,0:T(8,128)S(1)}, f32[18,16,128]{2,1,0:T(8,128)S(1)}, ...), branch_computations={%region_4.5_spmd, %region_5.6_spmd, %region_6.7_spmd, %region_7.8_... | conditional | flops 40000000 | bytes 4786488 | solution.py:468
  47.7 0.1 collective-permute-start.5
  47.7 11.7 %coarse.7 = f32[4,16,16,128]{3,2,1,0:T(8,128)S(1)} custom-call(s32[1,2]{1,0:T(1,128)S(1)} %get-tuple-element.120.sides, f32[4,16,16,128]{3,2,1,0:T(8,128)S(1)} %get-tuple-element.121.c0, f32[3,16,16,128]{3,2,1,0:T(8,128)S(1)} %get-tuple-element.122.cw, f32[18,16,128]{2,1,0:T(8,128)S(1)} %get-tuple-element.123.lo, f32[18,16,128]{2,1,0:T(8,128)S(1)} %get-tuple-element.124.hi, ...), custom_call_target="tpu_custom_call" | custom-call | flops 40000000 | bytes 4000000 | tf_op jit(solution)/shard_map/cond/branch_3_fun/coarse/pallas_call | solution.py:538
  59.5 0.0 collective-permute-done.5
  59.5 0.9 %merge.1 = f32[4,16,16,128]{3,2,1,0:T(8,128)} custom-call(f32[4,16,16,128]{3,2,1,0:T(8,128)S(1)} %get-tuple-element.160.c3, f32[4,8,8,128]{3,2,1,0:T(8,128)S(1)} %get-tuple-element.161.avg), custom_call_target="tpu_custom_call" | custom-call | tf_op jit(solution)/shard_map/merge/pallas_call | solution.py:572
  (1 shorter events, 0.0 us)
Async XLA Ops:
  0.6 13.9 %copy-start.3 = (f32[3,16,16,128]{3,2,1,0:T(8,128)S(1)}, f32[3,16,16,128]{3,2,1,0:T(8,128)}, u32[]{:S(2)}) copy-start(f32[3,16,16,128]{3,2,1,0:T(8,128)} %cw.7) | copy-start | bytes 1179652
  0.6 13.9 %copy-start.2 = (f32[4,16,16,128]{3,2,1,0:T(8,128)S(1)}, f32[4,16,16,128]{3,2,1,0:T(8,128)}, u32[]{:S(2)}) copy-start(f32[4,16,16,128]{3,2,1,0:T(8,128)} %c0.7) | copy-start | bytes 1572868
  2.7 10.0 %collective-permute-start.6 = (f32[18,16,128]{2,1,0:T(8,128)}, f32[18,16,128]{2,1,0:T(8,128)S(1)}, u32[]{:S(2)}, u32[]{:S(2)}) collective-permute-start(f32[18,16,128]{2,1,0:T(8,128)} %get-tuple-element.147), channel_id=1, source_target_pairs={{0,8},{8,16},{16,24},{24,0},{1,9},{9,17},{17,25},{25,1},{2,10},{10... | collective-permute-start | bytes 442376 | tf_op jit(solution)/shard_map/ppermute | solution.py:457
  5.8 8.7 %collective-permute-start.7 = (f32[18,16,128]{2,1,0:T(8,128)}, f32[18,16,128]{2,1,0:T(8,128)S(1)}, u32[]{:S(2)}, u32[]{:S(2)}) collective-permute-start(f32[18,16,128]{2,1,0:T(8,128)} %get-tuple-element.148), channel_id=1, source_target_pairs={{0,24},{8,0},{16,8},{24,16},{1,25},{9,1},{17,9},{25,17},{2,26},{10... | collective-permute-start | bytes 442376 | tf_op jit(solution)/shard_map/ppermute | solution.py:457
  15.3 11.4 %collective-permute-start.8 = (f32[318,128]{1,0:T(8,128)}, f32[318,128]{1,0:T(8,128)S(1)}, u32[]{:S(2)}, u32[]{:S(2)}) collective-permute-start(f32[318,128]{1,0:T(8,128)} %get-tuple-element.149), channel_id=1, source_target_pairs={{0,2},{2,4},{4,6},{6,0},{1,3},{3,5},{5,7},{7,1},{8,10},{10,12},{12... | collective-permute-start | bytes 488456 | tf_op jit(solution)/shard_map/ppermute | solution.py:457
  15.3 11.4 %collective-permute-start.9 = (f32[318,128]{1,0:T(8,128)}, f32[318,128]{1,0:T(8,128)S(1)}, u32[]{:S(2)}, u32[]{:S(2)}) collective-permute-start(f32[318,128]{1,0:T(8,128)} %get-tuple-element.150), channel_id=1, source_target_pairs={{0,6},{2,0},{4,2},{6,4},{1,7},{3,1},{5,3},{7,5},{8,14},{10,8},{12,... | collective-permute-start | bytes 488456 | tf_op jit(solution)/shard_map/ppermute | solution.py:457
  17.1 13.1 %collective-permute-start.11 = (f32[18,16,128]{2,1,0:T(8,128)}, f32[18,16,128]{2,1,0:T(8,128)S(1)}, u32[]{:S(2)}, u32[]{:S(2)}) collective-permute-start(f32[18,16,128]{2,1,0:T(8,128)} %get-tuple-element.154), channel_id=1, source_target_pairs={{0,8},{8,16},{16,24},{24,0},{1,9},{9,17},{17,25},{25,1},{2,10},{10... | collective-permute-start | bytes 442376 | tf_op jit(solution)/shard_map/ppermute | solution.py:457
  18.2 12.0 %collective-permute-start.12 = (f32[18,16,128]{2,1,0:T(8,128)}, f32[18,16,128]{2,1,0:T(8,128)S(1)}, u32[]{:S(2)}, u32[]{:S(2)}) collective-permute-start(f32[18,16,128]{2,1,0:T(8,128)} %get-tuple-element.155), channel_id=1, source_target_pairs={{0,24},{8,0},{16,8},{24,16},{1,25},{9,1},{17,9},{25,17},{2,26},{10... | collective-permute-start | bytes 442376 | tf_op jit(solution)/shard_map/ppermute | solution.py:457
  26.7 11.4 %copy-start = (f32[4,32,16,128]{3,2,1,0:T(8,128)S(1)}, f32[4,32,16,128]{3,2,1,0:T(8,128)}, u32[]{:S(2)}) copy-start(f32[4,32,16,128]{3,2,1,0:T(8,128)} %f0.3) | copy-start | bytes 3145732
  26.8 0.7 %copy-start.4 = (f32[318,128]{1,0:T(8,128)}, f32[318,128]{1,0:T(8,128)S(1)}, u32[]{:S(2)}) copy-start(f32[318,128]{1,0:T(8,128)S(1)} %collective-permute-done.9.above) | copy-start | bytes 488452
  28.6 9.5 %copy-start.1 = (f32[3,32,16,128]{3,2,1,0:T(8,128)S(1)}, f32[3,32,16,128]{3,2,1,0:T(8,128)}, u32[]{:S(2)}) copy-start(f32[3,32,16,128]{3,2,1,0:T(8,128)} %fw.3) | copy-start | bytes 2359300
  28.6 19.0 %collective-permute-start.10 = (f32[7,24,128]{2,1,0:T(8,128)}, f32[7,24,128]{2,1,0:T(8,128)}, u32[]{:S(2)}, u32[]{:S(2)}) collective-permute-start(f32[7,24,128]{2,1,0:T(8,128)} %zpack.1), channel_id=1, source_target_pairs={{0,1},{1,0},{2,3},{3,2},{4,5},{5,4},{6,7},{7,6},{8,9},{9,8},{10,11... | collective-permute-start | bytes 258056 | tf_op jit(solution)/shard_map/ppermute | solution.py:479
  30.2 7.3 %collective-permute-start = (f32[304,128]{1,0:T(8,128)}, f32[304,128]{1,0:T(8,128)S(1)}, u32[]{:S(2)}, u32[]{:S(2)}) collective-permute-start(f32[304,128]{1,0:T(8,128)} %param.1), channel_id=1, source_target_pairs={{0,8},{8,16},{16,24},{24,0},{1,9},{9,17},{17,25},{25,1},{2,10},{10... | collective-permute-start | bytes 466952 | tf_op jit(solution)/shard_map/cond/branch_1_fun/ppermute | solution.py:457
  38.1 9.5 %copy-start.5 = (f32[318,128]{1,0:T(8,128)S(1)}, f32[318,128]{1,0:T(8,128)}, u32[]{:S(2)}) copy-start(f32[318,128]{1,0:T(8,128)} %copy-done.4) | copy-start | bytes 488452
  47.7 11.8 %collective-permute-start.5 = (f32[4,8,8,128]{3,2,1,0:T(8,128)S(1)}, f32[4,8,8,128]{3,2,1,0:T(8,128)S(1)}, u32[]{:S(2)}, u32[]{:S(2)}) collective-permute-start(f32[4,8,8,128]{3,2,1,0:T(8,128)S(1)} %get-tuple-element.119), channel_id=1, source_target_pairs={{0,24},{8,0},{16,8},{24,16},{1,25},{9,1},{17,9},{25,17},{2,26},{10... | collective-permute-start | bytes 393224 | tf_op jit(solution)/shard_map/cond/branch_3_fun/ppermute | solution.py:457

commit v3 on v2

--- a/solution.py
+++ b/solution.py
@@ -66,6 +66,18 @@
     if at >= size:
         return high[first + width * member + at - size]
     return own[member, at]
+
+
+def unrolled(begin, end, at_once, body, carry=()):
+    while (end - begin) % at_once:
+        at_once -= 1
+
+    def several(i, carry):
+        for more in range(at_once):
+            carry = body(begin + i * at_once + more, carry)
+        return carry
+
+    return lax.fori_loop(0, (end - begin) // at_once, several, carry)
 
 
 def pack_kernel(s, c0, cw, f0, fw, cup, cdown, fup, fdown, sems):
@@ -132,28 +144,26 @@
     for step in range(2):
         src, flat, dst = pads[step], flats[step], pads[step + 1]
 
-        def two_layers(t, carry, step=step, src=src, flat=flat, dst=dst):
-            for odd in range(2):
-                j = 2 * t + odd + step + 1
-                co = coefficients([wind[d, j - 1] for d in range(3)])
-                for f in range(q):
-                    center = src[f, j, own, :]
-                    row = (f * s.ep + j) * PAD + TOP
-                    rate = rate_of(
-                        co,
-                        center,
-                        src[f, j - 1, own, :],
-                        src[f, j + 1, own, :],
-                        flat[pl.ds(row - 1, y), :],
-                        flat[pl.ds(row + 1, y), :],
-                        pltpu.roll(center, 1, 1),
-                        pltpu.roll(center, z - 1, 1),
-                    )
-                    base = center if step == 0 else pad0[f, j, own, :]
-                    dst[f, j, own, :] = base + section_weights[step] * rate
+        def layer(j, carry, step=step, src=src, flat=flat, dst=dst):
+            co = coefficients([wind[d, j - 1] for d in range(3)])
+            for f in range(q):
+                center = src[f, j, own, :]
+                row = (f * s.ep + j) * PAD + TOP
+                rate = rate_of(
+                    co,
+                    center,
+                    src[f, j - 1, own, :],
+                    src[f, j + 1, own, :],
+                    flat[pl.ds(row - 1, y), :],
+                    flat[pl.ds(row + 1, y), :],
+                    pltpu.roll(center, 1, 1),
+                    pltpu.roll(center, z - 1, 1),
+                )
+                base = center if step == 0 else pad0[f, j, own, :]
+                dst[f, j, own, :] = base + section_weights[step] * rate
             return carry
 
-        lax.fori_loop(0, s.ex // 2 - step, two_layers, 0)
+        unrolled(step + 1, s.ex + 1 - step, 5 if step == 0 else 6, layer)
     lane_x = lanes_of((s.ex, z))
     lane_y = lanes_of((y, z))
     ends = None
@@ -289,7 +299,7 @@
 
         begin, end = step, s.ex - step
         start = tuple(jnp.zeros((24, z), F32) for _ in range(q)) if step == 0 else ()
-        packed = lax.fori_loop(begin, end, layer, start)
+        packed = unrolled(begin, end, 4 + 2 * (step == 1), layer, start)
         if step == 2:
             break
         for f in range(q):
@@ -402,7 +412,7 @@
                         out[f, b - 2] = value
             return tuple(pltpu.roll(g, z - 2, 1) for g in ghosts)
 
-        lax.fori_loop(begin, end, pair_of_layers, carried)
+        unrolled(begin, end, 2, pair_of_layers, carried)
     rz = lax.broadcasted_iota(jnp.int32, (z, z), 0)
     cz = lax.broadcasted_iota(jnp.int32, (z, z), 1)
     flat = out.reshape(q * fx * y, z)
@@ -490,7 +500,7 @@
     neighbours = jnp.stack([level > 0, level < lax.axis_size("gz") - 1]).astype(jnp.int32).reshape(1, 2)
     cup, cdown, fup, fdown = pl.pallas_call(
         functools.partial(pack_kernel, s),
-        out_shape=(shape(s.halo, y, z),) * 4,
+        out_shape=(shape(s.halo, y, z),) * 2 + (shape(s.halo + 2, y, z),) * 2,
         in_specs=[HBM] * 4,
         out_specs=(VMEM,) * 4,
         scratch_shapes=[pltpu.SemaphoreType.DMA((4 * (q + 3),))],
@@ -518,7 +528,7 @@
         cost_estimate=SHORT,
         name="slab",
     )(coarse_fields, coarse_wind, lo, hi)
-    yrows, slab = lax.optimization_barrier((yrows, slab))
+    yrows, slab, flo, fhi = lax.optimization_barrier((yrows, slab, flo, fhi))
     padded = pltpu.VMEM((q, s.ep, WPAD, z), F32)
     wind_rows = pltpu.VMEM((3, s.ex, 24, z), F32)
     zown = pl.pallas_call(
@@ -532,7 +542,6 @@
         name="zpack",
     )(coarse_fields, coarse_wind, lo, hi, *yrows)
     zin = z_columns(zown)
-    slab, flo, fhi = lax.optimization_barrier((slab, flo, fhi))
     slab, _ = move_by(slab, (size - offset) % size)
     def coarse(*operands):
         return pl.pallas_call(

time: 60.7 us -> 54 us (0.89)
  Pallas kernels: 31.4 us -> 25.3 us
  waiting for transfers between devices: 13.8 us -> 9.15 us
  starting transfers between devices: 12.4 us -> 16.5 us
    ppermute x8, waiting for transfers between devices: 13.8 us -> 9.14 us  [ring(): lax.ppermute(array, axis, [(i, (i + by) % size) for i in range(size)])]
    pallas_call x1, Pallas kernels: 11.7 us -> 7.09 us  [coarse(): pl.pallas_call(functools.partial(coarse_kernel, s), out_shape=shape(q, x,...]
    ppermute x8, starting transfers between devices: 10.8 us -> 14.5 us  [ring(): lax.ppermute(array, axis, [(i, (i + by) % size) for i in range(size)])]
    pallas_call x1, Pallas kernels: 5.13 us -> 4.31 us  [shards(): pl.pallas_call(functools.partial(slab_kernel, s), out_shape=shape(s.slab,...]
    pallas_call x1, Pallas kernels: 9.49 us -> 8.87 us  [shards(): pl.pallas_call(functools.partial(fine_kernel, s), out_shape=(shape(q, fx,...]
  transfers between devices with their start and end apart: 9 -> 9, of which waited for: 3 -> 3; matrix products, arithmetic and copies ran while one was open for 1% -> 1% of each run, Pallas kernels for 46% -> 39%
where the time goes in v3:
time: 54 us; the launch traced here: 53.9 us
  Pallas kernels  25.3 us (47%)
  starting transfers between devices  16.5 us (31%)
  waiting for transfers between devices  9.15 us (17%)
  between operations  1.42 us (3%)
  local copies, waits for them, and re-layouts  1.36 us (3%)
    ppermute x8, starting transfers between devices, ring(): lax.ppermute(array, axis, [(i, (i + by) % size) for i in range(size)])  14.5 us
    ppermute x8, waiting for transfers between devices, ring(): lax.ppermute(array, axis, [(i, (i + by) % size) for i in range(size)])  9.14 us
    pallas_call x1, Pallas kernels, shards(): pl.pallas_call(functools.partial(fine_kernel, s), out_shape=(shape(q, fx,...  8.87 us
    pallas_call x1, Pallas kernels, coarse(): pl.pallas_call(functools.partial(coarse_kernel, s), out_shape=shape(q, x,...  7.09 us
    pallas_call x1, Pallas kernels, shards(): pl.pallas_call(functools.partial(slab_kernel, s), out_shape=shape(s.slab,...  4.31 us
    pallas_call x1, Pallas kernels, shards(): pl.pallas_call(functools.partial(pack_kernel, s), out_shape=(shape(s.halo...  2.11 us
    ppermute x1, starting transfers between devices, z_columns(): return lax.ppermute(zown, 'gz', [(0, 1), (1, 0)])  2.01 us
    pallas_call x1, Pallas kernels, shards(): pl.pallas_call(functools.partial(zpack_kernel, s), out_shape=shape(q + 3,...  1.14 us
  transfers between devices with their start and end apart: 9, of which 3 were waited for; matrix products, arithmetic and copies ran while one was open for 1% of the time, Pallas kernels for 39%

profile of v3, /device:TPU:0, one launch (start us, length us, event | category | flops | bytes accessed | tf_op | source)
XLA Modules:
  0.0 53.9 jit_solution(5474731263033681667)
XLA Ops:
  0.6 0.0 copy-start.3
  0.6 0.0 copy-start.2
  0.6 2.1 %pack.1 = (f32[18,16,128]{2,1,0:T(8,128)}, f32[18,16,128]{2,1,0:T(8,128)}, f32[20,16,128]{2,1,0:T(8,128)}, f32[20,16,128]{2,1,0:T(8,128)}) custom-call(f32[4,16,16,128]{3,2,1,0:T(8,128)} %c0.7, f32[3,16,16,128]{3,2,1,0:T(8,128)} %cw.7, f32[4,32,16,128]{3,2,1,0:T(8,128)} %f0.3, f32[3,32,16,128]{3,2,1,0:T(8,128)} %fw.3), custom_call_target="tpu_custom_call" | custom-call | flops 1 | bytes 1 | tf_op jit(solution)/shard_map/pack/pallas_call | solution.py:501
  2.8 3.1 %collective-permute-start.6 = (f32[18,16,128]{2,1,0:T(8,128)}, f32[18,16,128]{2,1,0:T(8,128)S(1)}, u32[]{:S(2)}, u32[]{:S(2)}) collective-permute-start(f32[18,16,128]{2,1,0:T(8,128)} %get-tuple-element.146), channel_id=1, source_target_pairs={{0,8},{8,16},{16,24},{24,0},{1,9},{9,17},{17,25},{25,1},{2,10},{10... | collective-permute-start | bytes 442376 | tf_op jit(solution)/shard_map/ppermute | solution.py:467
  5.8 2.1 %collective-permute-start.7 = (f32[18,16,128]{2,1,0:T(8,128)}, f32[18,16,128]{2,1,0:T(8,128)S(1)}, u32[]{:S(2)}, u32[]{:S(2)}) collective-permute-start(f32[18,16,128]{2,1,0:T(8,128)} %get-tuple-element.147), channel_id=1, source_target_pairs={{0,24},{8,0},{16,8},{24,16},{1,25},{9,1},{17,9},{25,17},{2,26},{10... | collective-permute-start | bytes 442376 | tf_op jit(solution)/shard_map/ppermute | solution.py:467
  7.9 0.0 collective-permute-start.10
  7.9 3.8 %collective-permute-start.11 = (f32[20,16,128]{2,1,0:T(8,128)}, f32[20,16,128]{2,1,0:T(8,128)S(1)}, u32[]{:S(2)}, u32[]{:S(2)}) collective-permute-start(f32[20,16,128]{2,1,0:T(8,128)} %get-tuple-element.151), channel_id=1, source_target_pairs={{0,24},{8,0},{16,8},{24,16},{1,25},{9,1},{17,9},{25,17},{2,26},{10... | collective-permute-start | bytes 491528 | tf_op jit(solution)/shard_map/ppermute | solution.py:467
  11.8 1.0 %collective-permute-done.6.lo = f32[18,16,128]{2,1,0:T(8,128)S(1)} collective-permute-done((f32[18,16,128]{2,1,0:T(8,128)}, f32[18,16,128]{2,1,0:T(8,128)S(1)}, u32[]{:S(2)}, u32[]{:S(2)}) %collective-permute-start.6) | collective-permute-done | bytes 147488 | tf_op jit(solution)/shard_map/ppermute | solution.py:467
  12.8 3.3 %collective-permute-done.7.hi = f32[18,16,128]{2,1,0:T(8,128)S(1)} collective-permute-done((f32[18,16,128]{2,1,0:T(8,128)}, f32[18,16,128]{2,1,0:T(8,128)S(1)}, u32[]{:S(2)}, u32[]{:S(2)}) %collective-permute-start.7) | collective-permute-done | bytes 147488 | tf_op jit(solution)/shard_map/ppermute | solution.py:467
  16.1 0.0 copy-done.3
  16.1 0.0 copy-done.2
  16.1 0.8 %ypack.1 = (f32[318,128]{1,0:T(8,128)}, f32[318,128]{1,0:T(8,128)}) custom-call(f32[4,16,16,128]{3,2,1,0:T(8,128)S(1)} %copy-done.2, f32[3,16,16,128]{3,2,1,0:T(8,128)S(1)} %copy-done.3, f32[18,16,128]{2,1,0:T(8,128)S(1)} %collective-permute-done.6.lo, f32[18,16,128]{2,1,0:T(8,128)S(1)} %collective-permute-done.7.hi), custom_call_target="tpu_custom_call" | custom-call | flops 1 | bytes 1 | tf_op jit(solution)/shard_map/ypack/pallas_call | solution.py:512
  17.0 0.0 collective-permute-start.8
  17.0 1.7 %collective-permute-start.9 = (f32[318,128]{1,0:T(8,128)}, f32[318,128]{1,0:T(8,128)S(1)}, u32[]{:S(2)}, u32[]{:S(2)}) collective-permute-start(f32[318,128]{1,0:T(8,128)} %get-tuple-element.149), channel_id=1, source_target_pairs={{0,6},{2,0},{4,2},{6,4},{1,7},{3,1},{5,3},{7,5},{8,14},{10,8},{12,... | collective-permute-start | bytes 488456 | tf_op jit(solution)/shard_map/ppermute | solution.py:467
  19.4 4.3 %slab.1 = f32[304,128]{1,0:T(8,128)} custom-call(f32[4,16,16,128]{3,2,1,0:T(8,128)S(1)} %copy-done.2, f32[3,16,16,128]{3,2,1,0:T(8,128)S(1)} %copy-done.3, f32[18,16,128]{2,1,0:T(8,128)S(1)} %collective-permute-done.6.lo, f32[18,16,128]{2,1,0:T(8,128)S(1)} %collective-permute-done.7.hi), custom_call_target="tpu_custom_call" | custom-call | flops 1 | bytes 1 | tf_op jit(solution)/shard_map/slab/pallas_call | solution.py:521
  23.7 0.0 copy-start
  23.7 0.0 collective-permute-done.10.flo
  23.7 0.0 collective-permute-done.11.fhi
  23.7 0.0 collective-permute-done.8.below
  23.7 0.0 collective-permute-done.9.above
  23.7 0.0 copy-start.4
  23.8 0.7 %copy-done.4 = f32[318,128]{1,0:T(8,128)} copy-done((f32[318,128]{1,0:T(8,128)}, f32[318,128]{1,0:T(8,128)S(1)}, u32[]{:S(2)}) %copy-start.4) | copy-done | bytes 162840
  24.4 1.1 %zpack.1 = f32[7,24,128]{2,1,0:T(8,128)} custom-call(f32[4,16,16,128]{3,2,1,0:T(8,128)S(1)} %copy-done.2, f32[3,16,16,128]{3,2,1,0:T(8,128)S(1)} %copy-done.3, f32[18,16,128]{2,1,0:T(8,128)S(1)} %collective-permute-done.6.lo, f32[18,16,128]{2,1,0:T(8,128)S(1)} %collective-permute-done.7.hi, f32[318,128]{1,0:T(8,128)S(1)} %collective-permute-done.8.below, ...), custom_call_target="tpu_custom_call" | custom-call | flops 1 | bytes 1 | tf_op jit(solution)/shard_map/zpack/pallas_call | solution.py:534
  25.6 0.0 copy-start.1
  25.6 2.0 %collective-permute-start.12 = (f32[7,24,128]{2,1,0:T(8,128)}, f32[7,24,128]{2,1,0:T(8,128)}, u32[]{:S(2)}, u32[]{:S(2)}) collective-permute-start(f32[7,24,128]{2,1,0:T(8,128)} %zpack.1), channel_id=1, source_target_pairs={{0,1},{1,0},{2,3},{3,2},{4,5},{5,4},{6,7},{7,6},{8,9},{9,8},{10,11... | collective-permute-start | bytes 258056 | tf_op jit(solution)/shard_map/ppermute | solution.py:489
  27.6 0.1 add_convert_fusion
  27.7 6.8 %conditional.2 = (f32[304,128]{1,0:T(8,128)}) conditional(s32[]{:T(128)} %clamp.7, f32[304,128]{1,0:T(8,128)} %slab.1, f32[304,128]{1,0:T(8,128)} %slab.1, f32[304,128]{1,0:T(8,128)} %slab.1, f32[304,128]{1,0:T(8,128)} %slab.1), branch_computations={%region_0.1_spmd, %region_1.2_spmd, %region_2.3_spmd, %region_3.4_... | conditional | bytes 933936 | solution.py:478
  27.7 1.4 %collective-permute-start.2 = (f32[304,128]{1,0:T(8,128)}, f32[304,128]{1,0:T(8,128)S(1)}, u32[]{:S(2)}, u32[]{:S(2)}) collective-permute-start(f32[304,128]{1,0:T(8,128)} %param.3), channel_id=1, source_target_pairs={{0,24},{8,0},{16,8},{24,16},{1,25},{9,1},{17,9},{25,17},{2,26},{10... | collective-permute-start | bytes 466952 | tf_op jit(solution)/shard_map/cond/branch_3_fun/ppermute | solution.py:467
  29.0 4.8 %collective-permute-done.2 = f32[304,128]{1,0:T(8,128)S(1)} collective-permute-done((f32[304,128]{1,0:T(8,128)}, f32[304,128]{1,0:T(8,128)S(1)}, u32[]{:S(2)}, u32[]{:S(2)}) %collective-permute-start.2) | collective-permute-done | bytes 155680 | tf_op jit(solution)/shard_map/cond/branch_3_fun/ppermute | solution.py:467
  33.8 0.7 %copy.10 = f32[304,128]{1,0:T(8,128)} copy(f32[304,128]{1,0:T(8,128)S(1)} %collective-permute-done.2) | data formatting | bytes 311296 | tf_op jit(solution)/shard_map/cond
  34.5 0.0 copy-done
  34.5 0.0 copy-done.1
  34.5 0.0 copy-start.5
  34.5 8.9 %fine.1 = (f32[4,32,16,128]{3,2,1,0:T(8,128)}, f32[4,8,8,128]{3,2,1,0:T(8,128)S(1)}) custom-call(f32[4,32,16,128]{3,2,1,0:T(8,128)S(1)} %copy-done, f32[3,32,16,128]{3,2,1,0:T(8,128)S(1)} %copy-done.1, f32[20,16,128]{2,1,0:T(8,128)S(1)} %collective-permute-done.10.flo, f32[20,16,128]{2,1,0:T(8,128)S(1)} %collective-permute-done.11.fhi, ...), custom_call_target="tpu_custom_call" | custom-call | tf_op jit(solution)/shard_map/fine/pallas_call | solution.py:559
  43.3 0.0 collective-permute-done.12
  43.4 0.0 copy-done.5
  43.4 9.6 %conditional.3 = (f32[4,8,8,128]{3,2,1,0:T(8,128)S(1)}, f32[4,16,16,128]{3,2,1,0:T(8,128)S(1)}) conditional(s32[]{:T(128)} %clamp.6, (s32[1,2]{1,0:T(1,128)S(1)}, f32[4,16,16,128]{3,2,1,0:T(8,128)S(1)}, f32[3,16,16,128]{3,2,1,0:T(8,128)S(1)}, f32[18,16,128]{2,1,0:T(8,128)S(1)}, f32[18,16,128]{2,1,0:T(8,128)S(1)}, ...), branch_computations={%region_4.5_spmd, %region_5.6_spmd, %region_6.7_spmd, %region_7.8_... | conditional | flops 40000000 | bytes 4786488 | solution.py:478
  43.4 2.4 %collective-permute-start.3 = (f32[4,8,8,128]{3,2,1,0:T(8,128)S(1)}, f32[4,8,8,128]{3,2,1,0:T(8,128)S(1)}, u32[]{:S(2)}, u32[]{:S(2)}) collective-permute-start(f32[4,8,8,128]{3,2,1,0:T(8,128)S(1)} %get-tuple-element.99), channel_id=1, source_target_pairs={{0,8},{8,16},{16,24},{24,0},{1,9},{9,17},{17,25},{25,1},{2,10},{10... | collective-permute-start | bytes 393224 | tf_op jit(solution)/shard_map/cond/branch_1_fun/ppermute | solution.py:467
  45.8 7.1 %coarse.5 = f32[4,16,16,128]{3,2,1,0:T(8,128)S(1)} custom-call(s32[1,2]{1,0:T(1,128)S(1)} %get-tuple-element.100.sides, f32[4,16,16,128]{3,2,1,0:T(8,128)S(1)} %get-tuple-element.101.c0, f32[3,16,16,128]{3,2,1,0:T(8,128)S(1)} %get-tuple-element.102.cw, f32[18,16,128]{2,1,0:T(8,128)S(1)} %get-tuple-element.103.lo, f32[18,16,128]{2,1,0:T(8,128)S(1)} %get-tuple-element.104.hi, ...), custom_call_target="tpu_custom_call" | custom-call | flops 40000000 | bytes 4000000 | tf_op jit(solution)/shard_map/cond/branch_1_fun/coarse/pallas_call | solution.py:547
  52.9 0.0 collective-permute-done.3
  52.9 0.9 %merge.1 = f32[4,16,16,128]{3,2,1,0:T(8,128)} custom-call(f32[4,16,16,128]{3,2,1,0:T(8,128)S(1)} %get-tuple-element.158.c3, f32[4,8,8,128]{3,2,1,0:T(8,128)S(1)} %get-tuple-element.159.avg), custom_call_target="tpu_custom_call" | custom-call | tf_op jit(solution)/shard_map/merge/pallas_call | solution.py:581
  (1 shorter events, 0.0 us)
Async XLA Ops:
  0.6 15.5 %copy-start.3 = (f32[3,16,16,128]{3,2,1,0:T(8,128)S(1)}, f32[3,16,16,128]{3,2,1,0:T(8,128)}, u32[]{:S(2)}) copy-start(f32[3,16,16,128]{3,2,1,0:T(8,128)} %cw.7) | copy-start | bytes 1179652
  0.6 15.5 %copy-start.2 = (f32[4,16,16,128]{3,2,1,0:T(8,128)S(1)}, f32[4,16,16,128]{3,2,1,0:T(8,128)}, u32[]{:S(2)}) copy-start(f32[4,16,16,128]{3,2,1,0:T(8,128)} %c0.7) | copy-start | bytes 1572868
  2.8 10.0 %collective-permute-start.6 = (f32[18,16,128]{2,1,0:T(8,128)}, f32[18,16,128]{2,1,0:T(8,128)S(1)}, u32[]{:S(2)}, u32[]{:S(2)}) collective-permute-start(f32[18,16,128]{2,1,0:T(8,128)} %get-tuple-element.146), channel_id=1, source_target_pairs={{0,8},{8,16},{16,24},{24,0},{1,9},{9,17},{17,25},{25,1},{2,10},{10... | collective-permute-start | bytes 442376 | tf_op jit(solution)/shard_map/ppermute | solution.py:467
  5.8 10.3 %collective-permute-start.7 = (f32[18,16,128]{2,1,0:T(8,128)}, f32[18,16,128]{2,1,0:T(8,128)S(1)}, u32[]{:S(2)}, u32[]{:S(2)}) collective-permute-start(f32[18,16,128]{2,1,0:T(8,128)} %get-tuple-element.147), channel_id=1, source_target_pairs={{0,24},{8,0},{16,8},{24,16},{1,25},{9,1},{17,9},{25,17},{2,26},{10... | collective-permute-start | bytes 442376 | tf_op jit(solution)/shard_map/ppermute | solution.py:467
  7.9 15.8 %collective-permute-start.10 = (f32[20,16,128]{2,1,0:T(8,128)}, f32[20,16,128]{2,1,0:T(8,128)S(1)}, u32[]{:S(2)}, u32[]{:S(2)}) collective-permute-start(f32[20,16,128]{2,1,0:T(8,128)} %get-tuple-element.150), channel_id=1, source_target_pairs={{0,8},{8,16},{16,24},{24,0},{1,9},{9,17},{17,25},{25,1},{2,10},{10... | collective-permute-start | bytes 491528 | tf_op jit(solution)/shard_map/ppermute | solution.py:467
  7.9 15.8 %collective-permute-start.11 = (f32[20,16,128]{2,1,0:T(8,128)}, f32[20,16,128]{2,1,0:T(8,128)S(1)}, u32[]{:S(2)}, u32[]{:S(2)}) collective-permute-start(f32[20,16,128]{2,1,0:T(8,128)} %get-tuple-element.151), channel_id=1, source_target_pairs={{0,24},{8,0},{16,8},{24,16},{1,25},{9,1},{17,9},{25,17},{2,26},{10... | collective-permute-start | bytes 491528 | tf_op jit(solution)/shard_map/ppermute | solution.py:467
  17.0 6.8 %collective-permute-start.8 = (f32[318,128]{1,0:T(8,128)}, f32[318,128]{1,0:T(8,128)S(1)}, u32[]{:S(2)}, u32[]{:S(2)}) collective-permute-start(f32[318,128]{1,0:T(8,128)} %get-tuple-element.148), channel_id=1, source_target_pairs={{0,2},{2,4},{4,6},{6,0},{1,3},{3,5},{5,7},{7,1},{8,10},{10,12},{12... | collective-permute-start | bytes 488456 | tf_op jit(solution)/shard_map/ppermute | solution.py:467
  17.0 6.8 %collective-permute-start.9 = (f32[318,128]{1,0:T(8,128)}, f32[318,128]{1,0:T(8,128)S(1)}, u32[]{:S(2)}, u32[]{:S(2)}) collective-permute-start(f32[318,128]{1,0:T(8,128)} %get-tuple-element.149), channel_id=1, source_target_pairs={{0,6},{2,0},{4,2},{6,4},{1,7},{3,1},{5,3},{7,5},{8,14},{10,8},{12,... | collective-permute-start | bytes 488456 | tf_op jit(solution)/shard_map/ppermute | solution.py:467
  23.7 10.7 %copy-start = (f32[4,32,16,128]{3,2,1,0:T(8,128)S(1)}, f32[4,32,16,128]{3,2,1,0:T(8,128)}, u32[]{:S(2)}) copy-start(f32[4,32,16,128]{3,2,1,0:T(8,128)} %f0.3) | copy-start | bytes 3145732
  23.7 0.7 %copy-start.4 = (f32[318,128]{1,0:T(8,128)}, f32[318,128]{1,0:T(8,128)S(1)}, u32[]{:S(2)}) copy-start(f32[318,128]{1,0:T(8,128)S(1)} %collective-permute-done.9.above) | copy-start | bytes 488452
  25.6 8.9 %copy-start.1 = (f32[3,32,16,128]{3,2,1,0:T(8,128)S(1)}, f32[3,32,16,128]{3,2,1,0:T(8,128)}, u32[]{:S(2)}) copy-start(f32[3,32,16,128]{3,2,1,0:T(8,128)} %fw.3) | copy-start | bytes 2359300
  25.6 17.8 %collective-permute-start.12 = (f32[7,24,128]{2,1,0:T(8,128)}, f32[7,24,128]{2,1,0:T(8,128)}, u32[]{:S(2)}, u32[]{:S(2)}) collective-permute-start(f32[7,24,128]{2,1,0:T(8,128)} %zpack.1), channel_id=1, source_target_pairs={{0,1},{1,0},{2,3},{3,2},{4,5},{5,4},{6,7},{7,6},{8,9},{9,8},{10,11... | collective-permute-start | bytes 258056 | tf_op jit(solution)/shard_map/ppermute | solution.py:489
  27.7 6.1 %collective-permute-start.2 = (f32[304,128]{1,0:T(8,128)}, f32[304,128]{1,0:T(8,128)S(1)}, u32[]{:S(2)}, u32[]{:S(2)}) collective-permute-start(f32[304,128]{1,0:T(8,128)} %param.3), channel_id=1, source_target_pairs={{0,24},{8,0},{16,8},{24,16},{1,25},{9,1},{17,9},{25,17},{2,26},{10... | collective-permute-start | bytes 466952 | tf_op jit(solution)/shard_map/cond/branch_3_fun/ppermute | solution.py:467
  34.5 8.9 %copy-start.5 = (f32[318,128]{1,0:T(8,128)S(1)}, f32[318,128]{1,0:T(8,128)}, u32[]{:S(2)}) copy-start(f32[318,128]{1,0:T(8,128)} %copy-done.4) | copy-start | bytes 488452
  43.4 9.5 %collective-permute-start.3 = (f32[4,8,8,128]{3,2,1,0:T(8,128)S(1)}, f32[4,8,8,128]{3,2,1,0:T(8,128)S(1)}, u32[]{:S(2)}, u32[]{:S(2)}) collective-permute-start(f32[4,8,8,128]{3,2,1,0:T(8,128)S(1)} %get-tuple-element.99), channel_id=1, source_target_pairs={{0,8},{8,16},{16,24},{24,0},{1,9},{9,17},{17,25},{25,1},{2,10},{10... | collective-permute-start | bytes 393224 | tf_op jit(solution)/shard_map/cond/branch_1_fun/ppermute | solution.py:467

commit v4 on v3

--- a/solution.py
+++ b/solution.py
@@ -84,13 +84,10 @@
     moves = []
     for fields, wind, up, down in ((c0, cw, cup, cdown), (f0, fw, fup, fdown)):
         size = fields.shape[1]
-        for f in range(s.q):
-            moves.append((fields.at[f, size - 3 : size], up.at[3 * f : 3 * f + 3]))
-            moves.append((fields.at[f, 0:3], down.at[3 * f : 3 * f + 3]))
-        for d in range(3):
-            at = 3 * s.q + 2 * d
-            moves.append((wind.at[d, size - 2 : size], up.at[at : at + 2]))
-            moves.append((wind.at[d, 0:2], down.at[at : at + 2]))
+        for own, members, width, first in ((fields, s.q, 3, 0), (wind, 3, 2, 3 * s.q)):
+            for dst, at in ((up, size - width), (down, 0)):
+                place = dst.at[first : first + members * width].reshape(members, width, s.y, s.z)
+                moves.append((own.at[:, at : at + width], place))
     moves = [pltpu.make_async_copy(src, dst, sems.at[i]) for i, (src, dst) in enumerate(moves)]
     for move in moves:
         move.start()
@@ -320,22 +317,11 @@
 
 
 def fine_kernel(s, f0, fw, flo, fhi, slab, out, avg, *scratch):
-    s0, s1, s2, wide_wind, faces, zface, sems = scratch
-    states = (s0, s1, s2)
+    s1, s2, faces, ghost_rows, zface, sems = scratch
+    states = (None, s1, s2, s1)
     q, y, z, fx, fe = s.q, s.y, s.z, s.fx, s.fe
     layers = fx + 6
     rows = slice(TOP, TOP + y)
-    pairs = [(f0, s0.at[:, 3 : 3 + fx, rows]), (fw, wide_wind.at[:, 2 : 2 + fx])]
-    for f in range(q):
-        pairs.append((flo.at[3 * f : 3 * f + 3], s0.at[f, 0:3, rows]))
-        pairs.append((fhi.at[3 * f : 3 * f + 3], s0.at[f, 3 + fx : 6 + fx, rows]))
-    for d in range(3):
-        at = 3 * q + 2 * d
-        pairs.append((flo.at[at : at + 2], wide_wind.at[d, 0:2]))
-        pairs.append((fhi.at[at : at + 2], wide_wind.at[d, 2 + fx : 4 + fx]))
-    moves = [pltpu.make_async_copy(src, dst, sems.at[i]) for i, (src, dst) in enumerate(pairs)]
-    for move in moves:
-        move.start()
     r = lax.broadcasted_iota(jnp.int32, (z, 2 * z), 0)
     c = lax.broadcasted_iota(jnp.int32, (z, 2 * z), 1)
     near = c // 2
@@ -348,7 +334,6 @@
     edge = (lane_x == 0) | (lane_x == z - 1)
     half = fe // 2
     for k in range(3):
-        flat = states[k].reshape(q * layers * PAD, z)
         for f in range(q):
             for side in range(2):
                 e = 4 * (q * k + f) + 2 * side + 1
@@ -359,10 +344,13 @@
                 a = here[0:half, :]
                 b = here[1 : half + 1, :]
                 d = here[2 : half + 2, :]
-                row = TOP - 1 if side == 0 else TOP + y
-                base = (f * layers + 1) * PAD + row
-                flat[pl.ds(base, half, stride=2 * PAD), :] = 0.25 * a + 0.75 * b
-                flat[pl.ds(base + PAD, half, stride=2 * PAD), :] = 0.75 * b + 0.25 * d
+                if k == 0:
+                    flat, base, stride = ghost_rows, (2 * f + side) * fe, 1
+                else:
+                    flat, stride = states[k].reshape(q * layers * PAD, z), PAD
+                    base = (f * layers + 1) * PAD + (TOP - 1 if side == 0 else TOP + y)
+                flat[pl.ds(base, half, stride=2 * stride), :] = 0.25 * a + 0.75 * b
+                flat[pl.ds(base + stride, half, stride=2 * stride), :] = 0.75 * b + 0.25 * d
     evens, odds = [], []
     for f in range(q):
         at = s.rows_e + f * s.rows_z
@@ -376,60 +364,97 @@
         d = pltpu.roll(a, z - 4, 1)
         evens.append(0.25 * a + 0.75 * b)
         odds.append(0.75 * b + 0.25 * d)
-    for move in moves:
-        move.wait()
     lane = lanes_of((y, z))
     is_first, is_last = lane == 0, lane == z - 1
+    row_in = lax.broadcasted_iota(jnp.int32, (y, z), 0)
+    is_low, is_high = row_in == 0, row_in == y - 1
+    flat_f0 = f0.reshape(q * fx * y, z)
+
+    def ghosts_at(k, t):
+        shift = -(2 * s.ex * k + 2 * t) % z
+        return tuple(pltpu.roll(g, shift, 1) if shift else g for g in evens + odds)
+
+    def pair_of_layers(k, t, ghosts, inner):
+        src = states[k]
+        for odd in range(2):
+            b = 2 * t + odd
+            at = b - 2
+
+            def field(f, at):
+                return f0[f, at] if inner else layer_of(s, f0, flo, fhi, f, at, 3, 0)
+
+            if inner:
+                winds = [fw[d, at] for d in range(3)]
+            else:
+                winds = [layer_of(s, fw, flo, fhi, d, at, 2, 3 * q) for d in range(3)]
+            co = coefficients(winds)
+            for f in range(q):
+                if k == 0:
+                    center, x_low, x_high = field(f, at), field(f, at - 1), field(f, at + 1)
+                    if inner:
+                        row = (f * fx + at) * y
+                        y_low, y_high = flat_f0[pl.ds(row - 1, y), :], flat_f0[pl.ds(row + 1, y), :]
+                    else:
+                        y_low, y_high = pltpu.roll(center, 1, 0), pltpu.roll(center, y - 1, 0)
+                    y_low = jnp.where(is_low, ghost_rows[pl.ds(2 * f * fe + b, 1), :], y_low)
+                    y_high = jnp.where(is_high, ghost_rows[pl.ds((2 * f + 1) * fe + b, 1), :], y_high)
+                    base = center
+                else:
+                    flat = src.reshape(q * layers * PAD, z)
+                    row = (f * layers + b + 1) * PAD + TOP
+                    center, x_low, x_high = src[f, b + 1, rows, :], src[f, b, rows, :], src[f, b + 2, rows, :]
+                    y_low, y_high = flat[pl.ds(row - 1, y), :], flat[pl.ds(row + 1, y), :]
+                    base = field(f, at)
+                ghost = ghosts[odd * q + f]
+                rate = rate_of(
+                    co,
+                    center,
+                    x_low,
+                    x_high,
+                    y_low,
+                    y_high,
+                    pltpu.roll(jnp.where(is_last, ghost, center), 1, 1),
+                    pltpu.roll(jnp.where(is_first, ghost, center), z - 1, 1),
+                )
+                states[k + 1][f, b + 1, rows, :] = base + section_weights[k] * rate
+        return tuple(pltpu.roll(g, z - 2, 1) for g in ghosts)
+
+    moves = []
     for k in range(3):
-        src, fraction = states[k], section_weights[k]
-        flat = src.reshape(q * layers * PAD, z)
-        begin, end = (0, half) if k < 2 else (1, half - 1)
-        shift = -(2 * s.ex * k + 2 * begin) % z
-        carried = tuple(pltpu.roll(g, shift, 1) if shift else g for g in evens + odds)
-
-        def pair_of_layers(t, ghosts, k=k, src=src, flat=flat, fraction=fraction):
-            for odd in range(2):
-                b = 2 * t + odd
-                co = coefficients([wide_wind[d, b] for d in range(3)])
-                for f in range(q):
-                    center = src[f, b + 1, rows, :]
-                    ghost = ghosts[odd * q + f]
-                    row = (f * layers + b + 1) * PAD + TOP
-                    rate = rate_of(
-                        co,
-                        center,
-                        src[f, b, rows, :],
-                        src[f, b + 2, rows, :],
-                        flat[pl.ds(row - 1, y), :],
-                        flat[pl.ds(row + 1, y), :],
-                        pltpu.roll(jnp.where(is_last, ghost, center), 1, 1),
-                        pltpu.roll(jnp.where(is_first, ghost, center), z - 1, 1),
-                    )
-                    value = (center if k == 0 else s0[f, b + 1, rows, :]) + fraction * rate
-                    if k < 2:
-                        states[k + 1][f, b + 1, rows, :] = value
-                    else:
-                        out[f, b - 2] = value
-            return tuple(pltpu.roll(g, z - 2, 1) for g in ghosts)
-
-        unrolled(begin, end, 2, pair_of_layers, carried)
+        if k < 2:
+            outer = 2 - k
+            for t in list(range(outer)) + list(range(half - outer, half)):
+                pair_of_layers(k, t, ghosts_at(k, t), False)
+            unrolled(outer, half - outer, 2, lambda t, g, k=k: pair_of_layers(k, t, g, True), ghosts_at(k, outer))
+            continue
+        carried = ghosts_at(k, 1)
+        part = (half - 2) // 4
+        for i in range(4):
+            carried = unrolled(
+                1 + i * part, 1 + (i + 1) * part, 2, lambda t, g, k=k: pair_of_layers(k, t, g, True), carried
+            )
+            begin, end = 2 * part * i, 2 * part * (i + 1)
+            moves.append(pltpu.make_async_copy(s1.at[:, 3 + begin : 3 + end, rows], out.at[:, begin:end], sems.at[i]))
+            moves[-1].start()
     rz = lax.broadcasted_iota(jnp.int32, (z, z), 0)
     cz = lax.broadcasted_iota(jnp.int32, (z, z), 1)
-    flat = out.reshape(q * fx * y, z)
+    flat = s1.reshape(q * layers * PAD, z)
     pairs_z = [jnp.where(cz == rz // 2 + odd * s.sz, 0.125, 0.0).astype(BF16) for odd in range(2)]
     for f in range(q):
         sums = []
         for odd in range(2):
             parts = []
             for p in range(s.x // 2):
-                base = (f * fx + 4 * p + 2 * odd) * y
+                base = (f * layers + 3 + 4 * p + 2 * odd) * PAD + TOP
                 part = None
-                for more in (0, 1, y, y + 1):
+                for more in (0, 1, PAD, PAD + 1):
                     piece = flat[pl.ds(base + more, y // 2, stride=2), :]
                     part = piece if part is None else part + piece
                 parts.append(part)
             sums.append(times(jnp.concatenate(parts, axis=0), pairs_z[odd]))
         avg[f] = (sums[0] + sums[1]).reshape(s.x // 2, y // 2, z)
+    for move in moves:
+        move.wait()
 
 
 def merge_kernel(s, c3, avg, out):
@@ -503,7 +528,7 @@
         out_shape=(shape(s.halo, y, z),) * 2 + (shape(s.halo + 2, y, z),) * 2,
         in_specs=[HBM] * 4,
         out_specs=(VMEM,) * 4,
-        scratch_shapes=[pltpu.SemaphoreType.DMA((4 * (q + 3),))],
+        scratch_shapes=[pltpu.SemaphoreType.DMA((8,))],
         cost_estimate=SHORT,
         name="pack",
     )(coarse_fields, coarse_wind, fine_fields, fine_wind)
@@ -531,18 +556,20 @@
     yrows, slab, flo, fhi = lax.optimization_barrier((yrows, slab, flo, fhi))
     padded = pltpu.VMEM((q, s.ep, WPAD, z), F32)
     wind_rows = pltpu.VMEM((3, s.ex, 24, z), F32)
-    zown = pl.pallas_call(
-        functools.partial(zpack_kernel, s),
-        out_shape=shape(q + 3, 24, z),
-        in_specs=[VMEM] * 6,
-        out_specs=VMEM,
-        scratch_shapes=[padded, wind_rows],
-        compiler_params=params(24),
-        cost_estimate=SHORT,
-        name="zpack",
-    )(coarse_fields, coarse_wind, lo, hi, *yrows)
+    def zpack(*operands):
+        return pl.pallas_call(
+            functools.partial(zpack_kernel, s),
+            out_shape=shape(q + 3, 24, z),
+            in_specs=[VMEM] * 6,
+            out_specs=VMEM,
+            scratch_shapes=[padded, wind_rows],
+            compiler_params=params(24),
+            cost_estimate=pl.CostEstimate(flops=4_000_000, bytes_accessed=2_000_000, transcendentals=0),
+            name="zpack",
+        )(*operands)
+
+    slab, zown = move_by(slab, (size - offset) % size, (zpack, (coarse_fields, coarse_wind, lo, hi, *yrows)))
     zin = z_columns(zown)
-    slab, _ = move_by(slab, (size - offset) % size)
     def coarse(*operands):
         return pl.pallas_call(
             functools.partial(coarse_kernel, s),
@@ -559,16 +586,15 @@
     fine_next, averaged = pl.pallas_call(
         functools.partial(fine_kernel, s),
         out_shape=(shape(q, fx, y, z), shape(q, x // 2, y // 2, z)),
-        in_specs=[ANY, ANY, ANY, ANY, VMEM],
-        out_specs=(VMEM, VMEM),
+        in_specs=[VMEM] * 5,
+        out_specs=(HBM, VMEM),
         scratch_shapes=[
             pltpu.VMEM((q, layers, PAD, z), F32),
             pltpu.VMEM((q, layers, PAD, z), F32),
-            pltpu.VMEM((q, layers, PAD, z), F32),
-            pltpu.VMEM((3, s.fe, y, z), F32),
             pltpu.VMEM((6 * q, s.ep, z), F32),
+            pltpu.VMEM((2 * q * s.fe, z), F32),
             pltpu.VMEM((q * y, z), F32),
-            pltpu.SemaphoreType.DMA((2 + 2 * (q + 3),)),
+            pltpu.SemaphoreType.DMA((4,)),
         ],
         compiler_params=params(32),
         name="fine",

time: 54 us -> 51.3 us (0.950)
  waiting for transfers between devices: 9.15 us -> 7.52 us
  Pallas kernels: 25.3 us -> 24.3 us
  local copies, waits for them, and re-layouts: 1.36 us -> 0.71 us
    ppermute x1, starting transfers between devices: 2.01 us -> 4.35 us  [z_columns(): return lax.ppermute(zown, 'gz', [(0, 1), (1, 0)])]
    ppermute x8, starting transfers between devices: 14.5 us -> 12.5 us  [ring(): lax.ppermute(array, axis, [(i, (i + by) % size) for i in range(size)])]
    ppermute x8, waiting for transfers between devices: 9.14 us -> 7.51 us  [ring(): lax.ppermute(array, axis, [(i, (i + by) % size) for i in range(size)])]
    pallas_call x1, Pallas kernels: 8.87 us -> 7.72 us  [shards(): pl.pallas_call(functools.partial(fine_kernel, s), out_shape=(shape(q, fx,...]
    pallas_call x1, Pallas kernels: 1.14 us -> 2.06 us  [zpack(): pl.pallas_call(functools.partial(zpack_kernel, s), out_shape=shape(q + 3,...]
    pallas_call x1, Pallas kernels: 4.31 us -> 3.64 us  [shards(): pl.pallas_call(functools.partial(slab_kernel, s), out_shape=shape(s.slab,...]
    cond x2, local copies, waits for them, and re-layouts: 0.68 us -> 0.02 us
  transfers between devices with their start and end apart: 9 -> 9, of which waited for: 3 -> 4; matrix products, arithmetic and copies ran while one was open for 1% -> 0% of each run, Pallas kernels for 39% -> 42%
where the time goes in v4:
time: 51.3 us; the launch traced here: 50.9 us
  Pallas kernels  24.3 us (47%)
  starting transfers between devices  16.8 us (33%)
  waiting for transfers between devices  7.52 us (15%)
  between operations  1.44 us (3%)
  local copies, waits for them, and re-layouts  0.71 us (1%)
    ppermute x8, starting transfers between devices, ring(): lax.ppermute(array, axis, [(i, (i + by) % size) for i in range(size)])  12.5 us
    pallas_call x1, Pallas kernels, shards(): pl.pallas_call(functools.partial(fine_kernel, s), out_shape=(shape(q, fx,...  7.72 us
    ppermute x8, waiting for transfers between devices, ring(): lax.ppermute(array, axis, [(i, (i + by) % size) for i in range(size)])  7.51 us
    pallas_call x1, Pallas kernels, coarse(): pl.pallas_call(functools.partial(coarse_kernel, s), out_shape=shape(q, x,...  7.05 us
    ppermute x1, starting transfers between devices, z_columns(): return lax.ppermute(zown, 'gz', [(0, 1), (1, 0)])  4.35 us
    pallas_call x1, Pallas kernels, shards(): pl.pallas_call(functools.partial(slab_kernel, s), out_shape=shape(s.slab,...  3.64 us
    pallas_call x1, Pallas kernels, zpack(): pl.pallas_call(functools.partial(zpack_kernel, s), out_shape=shape(q + 3,...  2.06 us
    pallas_call x1, Pallas kernels, shards(): pl.pallas_call(functools.partial(pack_kernel, s), out_shape=(shape(s.halo...  2.05 us
  transfers between devices with their start and end apart: 9, of which 4 were waited for; matrix products, arithmetic and copies ran while one was open for 0% of the time, Pallas kernels for 42%

profile of v4, /device:TPU:0, one launch (start us, length us, event | category | flops | bytes accessed | tf_op | source)
XLA Modules:
  0.0 50.9 jit_solution(12142597977270986809)
XLA Ops:
  0.6 0.0 copy-start.3
  0.6 0.0 copy-start.2
  0.6 2.1 %pack.1 = (f32[18,16,128]{2,1,0:T(8,128)}, f32[18,16,128]{2,1,0:T(8,128)}, f32[20,16,128]{2,1,0:T(8,128)}, f32[20,16,128]{2,1,0:T(8,128)}) custom-call(f32[4,16,16,128]{3,2,1,0:T(8,128)} %c0.5, f32[3,16,16,128]{3,2,1,0:T(8,128)} %cw.5, f32[4,32,16,128]{3,2,1,0:T(8,128)} %f0.3, f32[3,32,16,128]{3,2,1,0:T(8,128)} %fw.3), custom_call_target="tpu_custom_call" | custom-call | flops 1 | bytes 1 | tf_op jit(solution)/shard_map/pack/pallas_call | solution.py:526
  2.7 3.1 %collective-permute-start.6 = (f32[18,16,128]{2,1,0:T(8,128)}, f32[18,16,128]{2,1,0:T(8,128)S(1)}, u32[]{:S(2)}, u32[]{:S(2)}) collective-permute-start(f32[18,16,128]{2,1,0:T(8,128)} %get-tuple-element.223), channel_id=1, source_target_pairs={{0,8},{8,16},{16,24},{24,0},{1,9},{9,17},{17,25},{25,1},{2,10},{10... | collective-permute-start | bytes 442376 | tf_op jit(solution)/shard_map/ppermute | solution.py:492
  5.8 2.1 %collective-permute-start.7 = (f32[18,16,128]{2,1,0:T(8,128)}, f32[18,16,128]{2,1,0:T(8,128)S(1)}, u32[]{:S(2)}, u32[]{:S(2)}) collective-permute-start(f32[18,16,128]{2,1,0:T(8,128)} %get-tuple-element.224), channel_id=1, source_target_pairs={{0,24},{8,0},{16,8},{24,16},{1,25},{9,1},{17,9},{25,17},{2,26},{10... | collective-permute-start | bytes 442376 | tf_op jit(solution)/shard_map/ppermute | solution.py:492
  7.9 0.0 collective-permute-start.10
  7.9 3.8 %collective-permute-start.11 = (f32[20,16,128]{2,1,0:T(8,128)}, f32[20,16,128]{2,1,0:T(8,128)S(1)}, u32[]{:S(2)}, u32[]{:S(2)}) collective-permute-start(f32[20,16,128]{2,1,0:T(8,128)} %get-tuple-element.228), channel_id=1, source_target_pairs={{0,24},{8,0},{16,8},{24,16},{1,25},{9,1},{17,9},{25,17},{2,26},{10... | collective-permute-start | bytes 491528 | tf_op jit(solution)/shard_map/ppermute | solution.py:492
  11.7 1.0 %collective-permute-done.6.lo = f32[18,16,128]{2,1,0:T(8,128)S(1)} collective-permute-done((f32[18,16,128]{2,1,0:T(8,128)}, f32[18,16,128]{2,1,0:T(8,128)S(1)}, u32[]{:S(2)}, u32[]{:S(2)}) %collective-permute-start.6) | collective-permute-done | bytes 147488 | tf_op jit(solution)/shard_map/ppermute | solution.py:492
  12.7 3.3 %collective-permute-done.7.hi = f32[18,16,128]{2,1,0:T(8,128)S(1)} collective-permute-done((f32[18,16,128]{2,1,0:T(8,128)}, f32[18,16,128]{2,1,0:T(8,128)S(1)}, u32[]{:S(2)}, u32[]{:S(2)}) %collective-permute-start.7) | collective-permute-done | bytes 147488 | tf_op jit(solution)/shard_map/ppermute | solution.py:492
  16.1 0.0 copy-done.3
  16.1 0.0 copy-done.2
  16.1 0.8 %ypack.1 = (f32[318,128]{1,0:T(8,128)}, f32[318,128]{1,0:T(8,128)}) custom-call(f32[4,16,16,128]{3,2,1,0:T(8,128)S(1)} %copy-done.2, f32[3,16,16,128]{3,2,1,0:T(8,128)S(1)} %copy-done.3, f32[18,16,128]{2,1,0:T(8,128)S(1)} %collective-permute-done.6.lo, f32[18,16,128]{2,1,0:T(8,128)S(1)} %collective-permute-done.7.hi), custom_call_target="tpu_custom_call" | custom-call | flops 1 | bytes 1 | tf_op jit(solution)/shard_map/ypack/pallas_call | solution.py:537
  16.9 0.0 collective-permute-start.8
  16.9 1.7 %collective-permute-start.9 = (f32[318,128]{1,0:T(8,128)}, f32[318,128]{1,0:T(8,128)S(1)}, u32[]{:S(2)}, u32[]{:S(2)}) collective-permute-start(f32[318,128]{1,0:T(8,128)} %get-tuple-element.226), channel_id=1, source_target_pairs={{0,6},{2,0},{4,2},{6,4},{1,7},{3,1},{5,3},{7,5},{8,14},{10,8},{12,... | collective-permute-start | bytes 488456 | tf_op jit(solution)/shard_map/ppermute | solution.py:492
  19.3 3.6 %slab.1 = f32[304,128]{1,0:T(8,128)S(1)} custom-call(f32[4,16,16,128]{3,2,1,0:T(8,128)S(1)} %copy-done.2, f32[3,16,16,128]{3,2,1,0:T(8,128)S(1)} %copy-done.3, f32[18,16,128]{2,1,0:T(8,128)S(1)} %collective-permute-done.6.lo, f32[18,16,128]{2,1,0:T(8,128)S(1)} %collective-permute-done.7.hi), custom_call_target="tpu_custom_call" | custom-call | flops 1 | bytes 1 | tf_op jit(solution)/shard_map/slab/pallas_call | solution.py:546
  23.0 0.0 collective-permute-done.10.flo
  23.0 0.0 collective-permute-done.11.fhi
  23.0 0.0 collective-permute-done.8
  23.0 0.2 collective-permute-done.9
  23.2 0.0 copy-start.4
  23.2 0.7 %copy-done.4 = f32[318,128]{1,0:T(8,128)} copy-done((f32[318,128]{1,0:T(8,128)}, f32[318,128]{1,0:T(8,128)S(1)}, u32[]{:S(2)}) %copy-start.4) | copy-done | bytes 162840
  23.9 0.0 copy-start
  23.9 0.0 copy-start.1
  23.9 6.7 %conditional.2 = (f32[304,128]{1,0:T(8,128)S(1)}, f32[7,24,128]{2,1,0:T(8,128)}) conditional(s32[]{:T(128)} %clamp.7, (f32[4,16,16,128]{3,2,1,0:T(8,128)S(1)}, f32[3,16,16,128]{3,2,1,0:T(8,128)S(1)}, f32[18,16,128]{2,1,0:T(8,128)S(1)}, f32[18,16,128]{2,1,0:T(8,128)S(1)}, f32[318,128]{1,0:T(8,128)S(1)}, ...), branch_computations={%region_0.1_spmd, %region_1.2_spmd, %region_2.3_spmd, %region_3.4_... | conditional | flops 4000000 | bytes 2933944 | solution.py:503
  23.9 1.7 %collective-permute-start.2 = (f32[304,128]{1,0:T(8,128)S(1)}, f32[304,128]{1,0:T(8,128)S(1)}, u32[]{:S(2)}, u32[]{:S(2)}) collective-permute-start(f32[304,128]{1,0:T(8,128)S(1)} %get-tuple-element.157), channel_id=1, source_target_pairs={{0,24},{8,0},{16,8},{24,16},{1,25},{9,1},{17,9},{25,17},{2,26},{10... | collective-permute-start | bytes 466952 | tf_op jit(solution)/shard_map/cond/branch_3_fun/ppermute | solution.py:492
  25.6 2.1 %zpack.7 = f32[7,24,128]{2,1,0:T(8,128)} custom-call(f32[4,16,16,128]{3,2,1,0:T(8,128)S(1)} %get-tuple-element.158.c0, f32[3,16,16,128]{3,2,1,0:T(8,128)S(1)} %get-tuple-element.159.cw, f32[18,16,128]{2,1,0:T(8,128)S(1)} %get-tuple-element.160.lo, f32[18,16,128]{2,1,0:T(8,128)S(1)} %get-tuple-element.161.hi, f32[318,128]{1,0:T(8,128)S(1)} %get-tuple-element.162.below, ...), custom_call_target="tpu_custom_call" | custom-call | flops 4000000 | bytes 2000000 | tf_op jit(solution)/shard_map/cond/branch_3_fun/zpack/pallas_call | solution.py:560
  27.6 2.9 %collective-permute-done.2 = f32[304,128]{1,0:T(8,128)S(1)} collective-permute-done((f32[304,128]{1,0:T(8,128)S(1)}, f32[304,128]{1,0:T(8,128)S(1)}, u32[]{:S(2)}, u32[]{:S(2)}) %collective-permute-start.2) | collective-permute-done | bytes 155680 | tf_op jit(solution)/shard_map/cond/branch_3_fun/ppermute | solution.py:492
  30.6 0.0 copy-start.6
  30.6 4.3 %collective-permute-start.12 = (f32[7,24,128]{2,1,0:T(8,128)}, f32[7,24,128]{2,1,0:T(8,128)S(1)}, u32[]{:S(2)}, u32[]{:S(2)}) collective-permute-start(f32[7,24,128]{2,1,0:T(8,128)} %get-tuple-element.232), channel_id=1, source_target_pairs={{0,1},{1,0},{2,3},{3,2},{4,5},{5,4},{6,7},{7,6},{8,9},{9,8},{10,11... | collective-permute-start | bytes 258056 | tf_op jit(solution)/shard_map/ppermute | solution.py:514
  34.9 0.1 add_convert_fusion
  35.0 0.0 copy-done.6
  35.0 0.0 copy-done
  35.0 0.0 copy-done.1
  35.0 0.0 copy-start.5
  35.0 7.7 %fine.1 = (f32[4,32,16,128]{3,2,1,0:T(8,128)}, f32[4,8,8,128]{3,2,1,0:T(8,128)S(1)}) custom-call(f32[4,32,16,128]{3,2,1,0:T(8,128)S(1)} %copy-done, f32[3,32,16,128]{3,2,1,0:T(8,128)S(1)} %copy-done.1, f32[20,16,128]{2,1,0:T(8,128)S(1)} %collective-permute-done.10.flo, f32[20,16,128]{2,1,0:T(8,128)S(1)} %collective-permute-done.11.fhi, f32[304,128]{1,0:T(8,128)} %copy-done.6), custom_call_target="tpu_custom_call" | custom-call | tf_op jit(solution)/shard_map/fine/pallas_call | solution.py:586
  42.8 0.0 collective-permute-done.12
  42.8 0.0 copy-done.5
  42.8 7.2 %conditional.3 = (f32[4,8,8,128]{3,2,1,0:T(8,128)S(1)}, f32[4,16,16,128]{3,2,1,0:T(8,128)S(1)}) conditional(s32[]{:T(128)} %clamp.6, (s32[1,2]{1,0:T(1,128)S(1)}, f32[4,16,16,128]{3,2,1,0:T(8,128)S(1)}, f32[3,16,16,128]{3,2,1,0:T(8,128)S(1)}, f32[18,16,128]{2,1,0:T(8,128)S(1)}, f32[18,16,128]{2,1,0:T(8,128)S(1)}, ...), branch_computations={%region_4.5_spmd, %region_5.6_spmd, %region_6.7_spmd, %region_7.8_... | conditional | flops 40000000 | bytes 4786488 | solution.py:503
  42.8 0.1 collective-permute-start.3
  42.9 7.1 %coarse.5 = f32[4,16,16,128]{3,2,1,0:T(8,128)S(1)} custom-call(s32[1,2]{1,0:T(1,128)S(1)} %get-tuple-element.175.sides, f32[4,16,16,128]{3,2,1,0:T(8,128)S(1)} %get-tuple-element.176.c0, f32[3,16,16,128]{3,2,1,0:T(8,128)S(1)} %get-tuple-element.177.cw, f32[18,16,128]{2,1,0:T(8,128)S(1)} %get-tuple-element.178.lo, f32[18,16,128]{2,1,0:T(8,128)S(1)} %get-tuple-element.179.hi, ...), custom_call_target="tpu_custom_call" | custom-call | flops 40000000 | bytes 4000000 | tf_op jit(solution)/shard_map/cond/branch_1_fun/coarse/pallas_call | solution.py:574
  49.9 0.0 collective-permute-done.3
  50.0 0.9 %merge.1 = f32[4,16,16,128]{3,2,1,0:T(8,128)} custom-call(f32[4,16,16,128]{3,2,1,0:T(8,128)S(1)} %get-tuple-element.237.c3, f32[4,8,8,128]{3,2,1,0:T(8,128)S(1)} %get-tuple-element.238.avg), custom_call_target="tpu_custom_call" | custom-call | tf_op jit(solution)/shard_map/merge/pallas_call | solution.py:607
  (2 shorter events, 0.0 us)
Async XLA Ops:
  0.6 15.4 %copy-start.3 = (f32[3,16,16,128]{3,2,1,0:T(8,128)S(1)}, f32[3,16,16,128]{3,2,1,0:T(8,128)}, u32[]{:S(2)}) copy-start(f32[3,16,16,128]{3,2,1,0:T(8,128)} %cw.5) | copy-start | bytes 1179652
  0.6 15.4 %copy-start.2 = (f32[4,16,16,128]{3,2,1,0:T(8,128)S(1)}, f32[4,16,16,128]{3,2,1,0:T(8,128)}, u32[]{:S(2)}) copy-start(f32[4,16,16,128]{3,2,1,0:T(8,128)} %c0.5) | copy-start | bytes 1572868
  2.7 10.0 %collective-permute-start.6 = (f32[18,16,128]{2,1,0:T(8,128)}, f32[18,16,128]{2,1,0:T(8,128)S(1)}, u32[]{:S(2)}, u32[]{:S(2)}) collective-permute-start(f32[18,16,128]{2,1,0:T(8,128)} %get-tuple-element.223), channel_id=1, source_target_pairs={{0,8},{8,16},{16,24},{24,0},{1,9},{9,17},{17,25},{25,1},{2,10},{10... | collective-permute-start | bytes 442376 | tf_op jit(solution)/shard_map/ppermute | solution.py:492
  5.8 10.3 %collective-permute-start.7 = (f32[18,16,128]{2,1,0:T(8,128)}, f32[18,16,128]{2,1,0:T(8,128)S(1)}, u32[]{:S(2)}, u32[]{:S(2)}) collective-permute-start(f32[18,16,128]{2,1,0:T(8,128)} %get-tuple-element.224), channel_id=1, source_target_pairs={{0,24},{8,0},{16,8},{24,16},{1,25},{9,1},{17,9},{25,17},{2,26},{10... | collective-permute-start | bytes 442376 | tf_op jit(solution)/shard_map/ppermute | solution.py:492
  7.9 15.1 %collective-permute-start.10 = (f32[20,16,128]{2,1,0:T(8,128)}, f32[20,16,128]{2,1,0:T(8,128)S(1)}, u32[]{:S(2)}, u32[]{:S(2)}) collective-permute-start(f32[20,16,128]{2,1,0:T(8,128)} %get-tuple-element.227), channel_id=1, source_target_pairs={{0,8},{8,16},{16,24},{24,0},{1,9},{9,17},{17,25},{25,1},{2,10},{10... | collective-permute-start | bytes 491528 | tf_op jit(solution)/shard_map/ppermute | solution.py:492
  7.9 15.1 %collective-permute-start.11 = (f32[20,16,128]{2,1,0:T(8,128)}, f32[20,16,128]{2,1,0:T(8,128)S(1)}, u32[]{:S(2)}, u32[]{:S(2)}) collective-permute-start(f32[20,16,128]{2,1,0:T(8,128)} %get-tuple-element.228), channel_id=1, source_target_pairs={{0,24},{8,0},{16,8},{24,16},{1,25},{9,1},{17,9},{25,17},{2,26},{10... | collective-permute-start | bytes 491528 | tf_op jit(solution)/shard_map/ppermute | solution.py:492
  16.9 6.1 %collective-permute-start.8 = (f32[318,128]{1,0:T(8,128)}, f32[318,128]{1,0:T(8,128)S(1)}, u32[]{:S(2)}, u32[]{:S(2)}) collective-permute-start(f32[318,128]{1,0:T(8,128)} %get-tuple-element.225), channel_id=1, source_target_pairs={{0,2},{2,4},{4,6},{6,0},{1,3},{3,5},{5,7},{7,1},{8,10},{10,12},{12... | collective-permute-start | bytes 488456 | tf_op jit(solution)/shard_map/ppermute | solution.py:492
  16.9 6.3 %collective-permute-start.9 = (f32[318,128]{1,0:T(8,128)}, f32[318,128]{1,0:T(8,128)S(1)}, u32[]{:S(2)}, u32[]{:S(2)}) collective-permute-start(f32[318,128]{1,0:T(8,128)} %get-tuple-element.226), channel_id=1, source_target_pairs={{0,6},{2,0},{4,2},{6,4},{1,7},{3,1},{5,3},{7,5},{8,14},{10,8},{12,... | collective-permute-start | bytes 488456 | tf_op jit(solution)/shard_map/ppermute | solution.py:492
  23.2 0.7 %copy-start.4 = (f32[318,128]{1,0:T(8,128)}, f32[318,128]{1,0:T(8,128)S(1)}, u32[]{:S(2)}) copy-start(f32[318,128]{1,0:T(8,128)S(1)} %collective-permute-done.9) | copy-start | bytes 488452
  23.9 11.1 %copy-start = (f32[4,32,16,128]{3,2,1,0:T(8,128)S(1)}, f32[4,32,16,128]{3,2,1,0:T(8,128)}, u32[]{:S(2)}) copy-start(f32[4,32,16,128]{3,2,1,0:T(8,128)} %f0.3) | copy-start | bytes 3145732
  23.9 11.1 %copy-start.1 = (f32[3,32,16,128]{3,2,1,0:T(8,128)S(1)}, f32[3,32,16,128]{3,2,1,0:T(8,128)}, u32[]{:S(2)}) copy-start(f32[3,32,16,128]{3,2,1,0:T(8,128)} %fw.3) | copy-start | bytes 2359300
  23.9 6.7 %collective-permute-start.2 = (f32[304,128]{1,0:T(8,128)S(1)}, f32[304,128]{1,0:T(8,128)S(1)}, u32[]{:S(2)}, u32[]{:S(2)}) collective-permute-start(f32[304,128]{1,0:T(8,128)S(1)} %get-tuple-element.157), channel_id=1, source_target_pairs={{0,24},{8,0},{16,8},{24,16},{1,25},{9,1},{17,9},{25,17},{2,26},{10... | collective-permute-start | bytes 466952 | tf_op jit(solution)/shard_map/cond/branch_3_fun/ppermute | solution.py:492
  30.6 4.4 %copy-start.6 = (f32[304,128]{1,0:T(8,128)}, f32[304,128]{1,0:T(8,128)S(1)}, u32[]{:S(2)}) copy-start(f32[304,128]{1,0:T(8,128)S(1)} %get-tuple-element.235.slab) | copy-start | bytes 466948
  30.6 12.2 %collective-permute-start.12 = (f32[7,24,128]{2,1,0:T(8,128)}, f32[7,24,128]{2,1,0:T(8,128)S(1)}, u32[]{:S(2)}, u32[]{:S(2)}) collective-permute-start(f32[7,24,128]{2,1,0:T(8,128)} %get-tuple-element.232), channel_id=1, source_target_pairs={{0,1},{1,0},{2,3},{3,2},{4,5},{5,4},{6,7},{7,6},{8,9},{9,8},{10,11... | collective-permute-start | bytes 258056 | tf_op jit(solution)/shard_map/ppermute | solution.py:514
  35.0 7.8 %copy-start.5 = (f32[318,128]{1,0:T(8,128)S(1)}, f32[318,128]{1,0:T(8,128)}, u32[]{:S(2)}) copy-start(f32[318,128]{1,0:T(8,128)} %copy-done.4) | copy-start | bytes 488452
  42.8 7.1 %collective-permute-start.3 = (f32[4,8,8,128]{3,2,1,0:T(8,128)S(1)}, f32[4,8,8,128]{3,2,1,0:T(8,128)S(1)}, u32[]{:S(2)}, u32[]{:S(2)}) collective-permute-start(f32[4,8,8,128]{3,2,1,0:T(8,128)S(1)} %get-tuple-element.174), channel_id=1, source_target_pairs={{0,8},{8,16},{16,24},{24,0},{1,9},{9,17},{17,25},{25,1},{2,10},{10... | collective-permute-start | bytes 393224 | tf_op jit(solution)/shard_map/cond/branch_1_fun/ppermute | solution.py:492

commit v5 on v4

--- a/solution.py
+++ b/solution.py
@@ -68,7 +68,7 @@
     return own[member, at]
 
 
-def unrolled(begin, end, at_once, body, carry=()):
+def unrolled(begin, end, at_once, body, carry=None):
     while (end - begin) % at_once:
         at_once -= 1
 
@@ -139,20 +139,19 @@
         for at in range(-2, x + 2):
             wind[d, at + 2] = layer_of(s, cw, lo, hi, d, at, 2, 3 * q)
     for step in range(2):
-        src, flat, dst = pads[step], flats[step], pads[step + 1]
-
-        def layer(j, carry, step=step, src=src, flat=flat, dst=dst):
+        src, dst = pads[step], pads[step + 1]
+
+        def layer(j, carry, step=step, src=src, dst=dst):
             co = coefficients([wind[d, j - 1] for d in range(3)])
             for f in range(q):
                 center = src[f, j, own, :]
-                row = (f * s.ep + j) * PAD + TOP
                 rate = rate_of(
                     co,
                     center,
                     src[f, j - 1, own, :],
                     src[f, j + 1, own, :],
-                    flat[pl.ds(row - 1, y), :],
-                    flat[pl.ds(row + 1, y), :],
+                    pltpu.roll(center, 1, 0),
+                    pltpu.roll(center, y - 1, 0),
                     pltpu.roll(center, 1, 1),
                     pltpu.roll(center, z - 1, 1),
                 )
@@ -260,31 +259,37 @@
     for step in range(3):
         src, fraction = pads[step], section_weights[step]
         flat = src.reshape(q * s.ep * WPAD, z)
-        flat0 = pad0.reshape(q * s.ep * WPAD, z)
         flat_wind = wind.reshape(3 * s.ex * 24, z)
         flat_beyond = beyond.reshape(3 * q * 24, z)
         skip, height = (0, 24) if step < 2 else (4, y)
         here = lanes_of((height, z))
         is_first, is_last = here == 0, here == z - 1
 
-        def layer(a, packed, step=step, flat=flat, fraction=fraction, skip=skip, height=height):
+        def layer(a, packed, step=step, src=src, flat=flat, fraction=fraction, skip=skip, height=height):
             made = []
-            co = coefficients([flat_wind[pl.ds((d * s.ex + a) * 24 + skip, height), :] for d in range(3)])
+            if step < 2:
+                co = coefficients([wind[d, a] for d in range(3)])
+            else:
+                co = coefficients([flat_wind[pl.ds((d * s.ex + a) * 24 + skip, height), :] for d in range(3)])
             for f in range(q):
                 row = (f * s.ep + a + 1) * WPAD + 8 + skip
-                center = flat[pl.ds(row, height), :]
+
+                def at_layer(of, layer, row, f=f):
+                    return of[f, layer, BLOCK, :] if step < 2 else of.reshape(flat.shape)[pl.ds(row, height), :]
+
+                center = at_layer(src, a + 1, row)
                 ghost = pltpu.roll(flat_beyond[pl.ds((step * q + f) * 24 + skip, height), :], 2 * z - 6 * a - 3, 1)
                 rate = rate_of(
                     co,
                     center,
-                    flat[pl.ds(row - WPAD, height), :],
-                    flat[pl.ds(row + WPAD, height), :],
+                    at_layer(src, a, row - WPAD),
+                    at_layer(src, a + 2, row + WPAD),
                     flat[pl.ds(row - 1, height), :],
                     flat[pl.ds(row + 1, height), :],
                     pltpu.roll(jnp.where(is_last, ghost, center), 1, 1),
                     pltpu.roll(jnp.where(is_first, ghost, center), z - 1, 1),
                 )
-                base = center if step == 0 else flat0[pl.ds(row, height), :]
+                base = center if step == 0 else at_layer(pad0, a + 1, row)
                 value = base + fraction * rate
                 if step == 2:
                     out[f, a - 2] = value
@@ -351,7 +356,6 @@
                     base = (f * layers + 1) * PAD + (TOP - 1 if side == 0 else TOP + y)
                 flat[pl.ds(base, half, stride=2 * stride), :] = 0.25 * a + 0.75 * b
                 flat[pl.ds(base + stride, half, stride=2 * stride), :] = 0.75 * b + 0.25 * d
-    evens, odds = [], []
     for f in range(q):
         at = s.rows_e + f * s.rows_z
         a = slab[at : at + s.sy, :]
@@ -362,19 +366,15 @@
         a = zface[f * y : f * y + y, :]
         b = pltpu.roll(a, z - 2, 1)
         d = pltpu.roll(a, z - 4, 1)
-        evens.append(0.25 * a + 0.75 * b)
-        odds.append(0.75 * b + 0.25 * d)
+        zface[f * y : f * y + y, :] = 0.25 * a + 0.75 * b
+        zface[(q + f) * y : (q + f + 1) * y, :] = 0.75 * b + 0.25 * d
     lane = lanes_of((y, z))
     is_first, is_last = lane == 0, lane == z - 1
     row_in = lax.broadcasted_iota(jnp.int32, (y, z), 0)
     is_low, is_high = row_in == 0, row_in == y - 1
     flat_f0 = f0.reshape(q * fx * y, z)
 
-    def ghosts_at(k, t):
-        shift = -(2 * s.ex * k + 2 * t) % z
-        return tuple(pltpu.roll(g, shift, 1) if shift else g for g in evens + odds)
-
-    def pair_of_layers(k, t, ghosts, inner):
+    def pair_of_layers(k, t, inner):
         src = states[k]
         for odd in range(2):
             b = 2 * t + odd
@@ -405,7 +405,8 @@
                     center, x_low, x_high = src[f, b + 1, rows, :], src[f, b, rows, :], src[f, b + 2, rows, :]
                     y_low, y_high = flat[pl.ds(row - 1, y), :], flat[pl.ds(row + 1, y), :]
                     base = field(f, at)
-                ghost = ghosts[odd * q + f]
+                ghost = zface[(odd * q + f) * y : (odd * q + f + 1) * y, :]
+                ghost = pltpu.roll(ghost, (2 * z - 2 * s.ex * k - 2 * t) if inner else -(2 * s.ex * k + 2 * t) % z, 1)
                 rate = rate_of(
                     co,
                     center,
@@ -417,22 +418,18 @@
                     pltpu.roll(jnp.where(is_first, ghost, center), z - 1, 1),
                 )
                 states[k + 1][f, b + 1, rows, :] = base + section_weights[k] * rate
-        return tuple(pltpu.roll(g, z - 2, 1) for g in ghosts)
 
     moves = []
     for k in range(3):
         if k < 2:
             outer = 2 - k
             for t in list(range(outer)) + list(range(half - outer, half)):
-                pair_of_layers(k, t, ghosts_at(k, t), False)
-            unrolled(outer, half - outer, 2, lambda t, g, k=k: pair_of_layers(k, t, g, True), ghosts_at(k, outer))
+                pair_of_layers(k, t, False)
+            unrolled(outer, half - outer, 2, lambda t, g, k=k: pair_of_layers(k, t, True))
             continue
-        carried = ghosts_at(k, 1)
         part = (half - 2) // 4
         for i in range(4):
-            carried = unrolled(
-                1 + i * part, 1 + (i + 1) * part, 2, lambda t, g, k=k: pair_of_layers(k, t, g, True), carried
-            )
+            unrolled(1 + i * part, 1 + (i + 1) * part, 2, lambda t, g, k=k: pair_of_layers(k, t, True))
             begin, end = 2 * part * i, 2 * part * (i + 1)
             moves.append(pltpu.make_async_copy(s1.at[:, 3 + begin : 3 + end, rows], out.at[:, begin:end], sems.at[i]))
             moves[-1].start()
@@ -529,6 +526,7 @@
         in_specs=[HBM] * 4,
         out_specs=(VMEM,) * 4,
         scratch_shapes=[pltpu.SemaphoreType.DMA((8,))],
+        compiler_params=params(4),
         cost_estimate=SHORT,
         name="pack",
     )(coarse_fields, coarse_wind, fine_fields, fine_wind)
@@ -539,6 +537,7 @@
         out_shape=(shape(s.rows_f + s.rows_w, z),) * 2,
         in_specs=[VMEM] * 4,
         out_specs=(VMEM,) * 2,
+        compiler_params=params(4),
         cost_estimate=SHORT,
         name="ypack",
     )(coarse_fields, coarse_wind, lo, hi)
@@ -549,7 +548,7 @@
         in_specs=[VMEM] * 4,
         out_specs=VMEM,
         scratch_shapes=[pltpu.VMEM((q, s.ep, PAD, z), F32)] * 3 + [pltpu.VMEM((3, s.ex, y, z), F32)],
-        compiler_params=params(24),
+        compiler_params=params(10),
         cost_estimate=SHORT,
         name="slab",
     )(coarse_fields, coarse_wind, lo, hi)
@@ -563,7 +562,7 @@
             in_specs=[VMEM] * 6,
             out_specs=VMEM,
             scratch_shapes=[padded, wind_rows],
-            compiler_params=params(24),
+            compiler_params=params(6),
             cost_estimate=pl.CostEstimate(flops=4_000_000, bytes_accessed=2_000_000, transcendentals=0),
             name="zpack",
         )(*operands)
@@ -577,7 +576,7 @@
             in_specs=[SMEM] + [VMEM] * 8,
             out_specs=VMEM,
             scratch_shapes=[padded] * 3 + [wind_rows, pltpu.VMEM((3, q, 24, z), F32), pltpu.VMEM((2, q, 24, z), F32)],
-            compiler_params=params(24),
+            compiler_params=params(12),
             cost_estimate=pl.CostEstimate(flops=40_000_000, bytes_accessed=4_000_000, transcendentals=0),
             name="coarse",
         )(*operands)
@@ -593,10 +592,10 @@
             pltpu.VMEM((q, layers, PAD, z), F32),
             pltpu.VMEM((6 * q, s.ep, z), F32),
             pltpu.VMEM((2 * q * s.fe, z), F32),
-            pltpu.VMEM((q * y, z), F32),
+            pltpu.VMEM((2 * q * y, z), F32),
             pltpu.SemaphoreType.DMA((4,)),
         ],
-        compiler_params=params(32),
+        compiler_params=params(10),
         name="fine",
     )(fine_fields, fine_wind, flo, fhi, slab)
     averaged, state = move_by(
@@ -609,7 +608,7 @@
         out_shape=shape(q, x, y, z),
         in_specs=[VMEM, VMEM],
         out_specs=VMEM,
-        compiler_params=params(16),
+        compiler_params=params(4),
         name="merge",
     )(state, averaged)
     return coarse_next, fine_next

time: 51.3 us -> 49.2 us (0.959); the launches traced: 50.9 us -> 50.2 us
  local copies, waits for them, and re-layouts: 0.71 us -> 3.05 us
  Pallas kernels: 24.3 us -> 22.2 us
  starting transfers between devices: 16.8 us -> 14.8 us
  waiting for transfers between devices: 7.52 us -> 8.58 us
    ppermute x1, starting transfers between devices: 4.35 us -> 0.8 us  [z_columns(): return lax.ppermute(zown, 'gz', [(0, 1), (1, 0)])]
    unnamed x14 -> x16, local copies, waits for them, and re-layouts: 0.69 us -> 3.03 us
    ppermute x8, starting transfers between devices: 12.5 us -> 14 us  [ring(): lax.ppermute(array, axis, [(i, (i + by) % size) for i in range(size)])]
    ppermute x8, waiting for transfers between devices: 7.51 us -> 8.58 us  [ring(): lax.ppermute(array, axis, [(i, (i + by) % size) for i in range(size)])]
    pallas_call x1, Pallas kernels: 2.05 us -> 1.1 us  [shards(): pl.pallas_call(functools.partial(pack_kernel, s), out_shape=(shape(s.halo...]
    pallas_call x1, Pallas kernels: 0.83 us -> 0.11 us  [shards(): pl.pallas_call(functools.partial(ypack_kernel, s), out_shape=(shape(s.row...]
    pallas_call x1, Pallas kernels: 7.72 us -> 7.15 us  [shards(): pl.pallas_call(functools.partial(fine_kernel, s), out_shape=(shape(q, fx,...]
  transfers between devices with their start and end apart: 9 -> 9, of which waited for: 4 -> 3; matrix products, arithmetic and copies ran while one was open for 0% -> 0% of each run, Pallas kernels for 42% -> 40%
where the time goes in v5:
time: 49.2 us; the launch traced here: 50.2 us
  Pallas kernels  22.2 us (45%)
  starting transfers between devices  14.8 us (30%)
  waiting for transfers between devices  8.58 us (17%)
  local copies, waits for them, and re-layouts  3.05 us (6%)
  between operations  1.45 us (3%)
    ppermute x8, starting transfers between devices, ring(): lax.ppermute(array, axis, [(i, (i + by) % size) for i in range(size)])  14 us
    ppermute x8, waiting for transfers between devices, ring(): lax.ppermute(array, axis, [(i, (i + by) % size) for i in range(size)])  8.58 us
    pallas_call x1, Pallas kernels, shards(): pl.pallas_call(functools.partial(fine_kernel, s), out_shape=(shape(q, fx,...  7.15 us
    pallas_call x1, Pallas kernels, coarse(): pl.pallas_call(functools.partial(coarse_kernel, s), out_shape=shape(q, x,...  7.05 us
    pallas_call x1, Pallas kernels, shards(): pl.pallas_call(functools.partial(slab_kernel, s), out_shape=shape(s.slab,...  3.7 us
    unnamed x16, local copies, waits for them, and re-layouts  3.03 us
    pallas_call x1, Pallas kernels, zpack(): pl.pallas_call(functools.partial(zpack_kernel, s), out_shape=shape(q + 3,...  2.12 us
    pallas_call x1, Pallas kernels, shards(): pl.pallas_call(functools.partial(pack_kernel, s), out_shape=(shape(s.halo...  1.1 us
  transfers between devices with their start and end apart: 9, of which 3 were waited for; matrix products, arithmetic and copies ran while one was open for 0% of the time, Pallas kernels for 40%

profile of v5, /device:TPU:0, one launch (start us, length us, event | category | flops | bytes accessed | tf_op | source)
XLA Modules:
  0.0 50.2 jit_solution(16696435100795405252)
XLA Ops:
  0.6 0.0 copy-start
  0.6 1.2 %copy-done = f32[4,32,16,128]{3,2,1,0:T(8,128)S(1)} copy-done((f32[4,32,16,128]{3,2,1,0:T(8,128)S(1)}, f32[4,32,16,128]{3,2,1,0:T(8,128)}, u32[]{:S(2)}) %copy-start) | copy-done | bytes 1048600
  1.9 0.0 copy-start.2
  1.9 1.1 %copy-done.2 = f32[3,32,16,128]{3,2,1,0:T(8,128)S(1)} copy-done((f32[3,32,16,128]{3,2,1,0:T(8,128)S(1)}, f32[3,32,16,128]{3,2,1,0:T(8,128)}, u32[]{:S(2)}) %copy-start.2) | copy-done | bytes 786456
  3.0 0.0 copy-start.4
  3.0 0.0 copy-start.5
  3.0 1.1 %pack.1 = (f32[18,16,128]{2,1,0:T(8,128)S(1)}, f32[18,16,128]{2,1,0:T(8,128)S(1)}, f32[20,16,128]{2,1,0:T(8,128)S(1)}, f32[20,16,128]{2,1,0:T(8,128)S(1)}) custom-call(f32[4,16,16,128]{3,2,1,0:T(8,128)} %c0.5, f32[3,16,16,128]{3,2,1,0:T(8,128)} %cw.5, f32[4,32,16,128]{3,2,1,0:T(8,128)S(1)} %copy-done, f32[3,32,16,128]{3,2,1,0:T(8,128)S(1)} %copy-done.2), custom_call_target="tpu_custom_call" | custom-call | flops 1 | bytes 1 | tf_op jit(solution)/shard_map/pack/pallas_call | solution.py:523
  4.1 3.1 %collective-permute-start.6 = (f32[18,16,128]{2,1,0:T(8,128)S(1)}, f32[18,16,128]{2,1,0:T(8,128)S(1)}, u32[]{:S(2)}, u32[]{:S(2)}) collective-permute-start(f32[18,16,128]{2,1,0:T(8,128)S(1)} %get-tuple-element.223), channel_id=1, source_target_pairs={{0,8},{8,16},{16,24},{24,0},{1,9},{9,17},{17,25},{25,1},{2,10},{10... | collective-permute-start | bytes 442376 | tf_op jit(solution)/shard_map/ppermute | solution.py:489
  7.2 2.1 %collective-permute-start.7 = (f32[18,16,128]{2,1,0:T(8,128)S(1)}, f32[18,16,128]{2,1,0:T(8,128)S(1)}, u32[]{:S(2)}, u32[]{:S(2)}) collective-permute-start(f32[18,16,128]{2,1,0:T(8,128)S(1)} %get-tuple-element.224), channel_id=1, source_target_pairs={{0,24},{8,0},{16,8},{24,16},{1,25},{9,1},{17,9},{25,17},{2,26},{10... | collective-permute-start | bytes 442376 | tf_op jit(solution)/shard_map/ppermute | solution.py:489
  9.3 0.0 collective-permute-start.10
  9.3 3.8 %collective-permute-start.11 = (f32[20,16,128]{2,1,0:T(8,128)S(1)}, f32[20,16,128]{2,1,0:T(8,128)S(1)}, u32[]{:S(2)}, u32[]{:S(2)}) collective-permute-start(f32[20,16,128]{2,1,0:T(8,128)S(1)} %get-tuple-element.228), channel_id=1, source_target_pairs={{0,24},{8,0},{16,8},{24,16},{1,25},{9,1},{17,9},{25,17},{2,26},{10... | collective-permute-start | bytes 491528 | tf_op jit(solution)/shard_map/ppermute | solution.py:489
  13.1 0.8 %collective-permute-done.6.lo = f32[18,16,128]{2,1,0:T(8,128)S(1)} collective-permute-done((f32[18,16,128]{2,1,0:T(8,128)S(1)}, f32[18,16,128]{2,1,0:T(8,128)S(1)}, u32[]{:S(2)}, u32[]{:S(2)}) %collective-permute-start.6) | collective-permute-done | bytes 147488 | tf_op jit(solution)/shard_map/ppermute | solution.py:489
  13.9 3.3 %collective-permute-done.7.hi = f32[18,16,128]{2,1,0:T(8,128)S(1)} collective-permute-done((f32[18,16,128]{2,1,0:T(8,128)S(1)}, f32[18,16,128]{2,1,0:T(8,128)S(1)}, u32[]{:S(2)}, u32[]{:S(2)}) %collective-permute-start.7) | collective-permute-done | bytes 147488 | tf_op jit(solution)/shard_map/ppermute | solution.py:489
  17.2 0.0 copy-done.4
  17.2 0.0 copy-done.5
  17.3 0.1 ypack.1
  17.4 0.1 collective-permute-start.8
  17.4 1.7 %collective-permute-start.9 = (f32[318,128]{1,0:T(8,128)S(1)}, f32[318,128]{1,0:T(8,128)S(1)}, u32[]{:S(2)}, u32[]{:S(2)}) collective-permute-start(f32[318,128]{1,0:T(8,128)S(1)} %get-tuple-element.226), channel_id=1, source_target_pairs={{0,6},{2,0},{4,2},{6,4},{1,7},{3,1},{5,3},{7,5},{8,14},{10,8},{12,... | collective-permute-start | bytes 488456 | tf_op jit(solution)/shard_map/ppermute | solution.py:489
  19.9 3.7 %slab.1 = f32[304,128]{1,0:T(8,128)S(1)} custom-call(f32[4,16,16,128]{3,2,1,0:T(8,128)S(1)} %copy-done.4, f32[3,16,16,128]{3,2,1,0:T(8,128)S(1)} %copy-done.5, f32[18,16,128]{2,1,0:T(8,128)S(1)} %collective-permute-done.6.lo, f32[18,16,128]{2,1,0:T(8,128)S(1)} %collective-permute-done.7.hi), custom_call_target="tpu_custom_call" | custom-call | flops 1 | bytes 1 | tf_op jit(solution)/shard_map/slab/pallas_call | solution.py:545
  23.6 0.0 collective-permute-done.10.flo
  23.6 0.0 collective-permute-done.11.fhi
  23.6 0.0 collective-permute-done.8
  23.6 0.0 collective-permute-done.9
  23.6 0.0 copy-start.6
  23.6 0.7 %copy-done.6 = f32[318,128]{1,0:T(8,128)} copy-done((f32[318,128]{1,0:T(8,128)}, f32[318,128]{1,0:T(8,128)S(1)}, u32[]{:S(2)}) %copy-start.6) | copy-done | bytes 162840
  24.3 0.0 copy-start.1
  24.3 0.0 copy-start.3
  24.3 7.0 %conditional.2 = (f32[304,128]{1,0:T(8,128)S(1)}, f32[7,24,128]{2,1,0:T(8,128)}) conditional(s32[]{:T(128)} %clamp.7, (f32[4,16,16,128]{3,2,1,0:T(8,128)S(1)}, f32[3,16,16,128]{3,2,1,0:T(8,128)S(1)}, f32[18,16,128]{2,1,0:T(8,128)S(1)}, f32[18,16,128]{2,1,0:T(8,128)S(1)}, f32[318,128]{1,0:T(8,128)S(1)}, ...), branch_computations={%region_0.1_spmd, %region_1.2_spmd, %region_2.3_spmd, %region_3.4_... | conditional | flops 4000000 | bytes 2933944 | solution.py:500
  24.3 0.5 collective-permute-start
  24.8 2.1 %zpack.5 = f32[7,24,128]{2,1,0:T(8,128)} custom-call(f32[4,16,16,128]{3,2,1,0:T(8,128)S(1)} %get-tuple-element.144.c0, f32[3,16,16,128]{3,2,1,0:T(8,128)S(1)} %get-tuple-element.145.cw, f32[18,16,128]{2,1,0:T(8,128)S(1)} %get-tuple-element.146.lo, f32[18,16,128]{2,1,0:T(8,128)S(1)} %get-tuple-element.147.hi, f32[318,128]{1,0:T(8,128)S(1)} %get-tuple-element.148.below, ...), custom_call_target="tpu_custom_call" | custom-call | flops 4000000 | bytes 2000000 | tf_op jit(solution)/shard_map/cond/branch_1_fun/zpack/pallas_call | solution.py:559
  26.9 4.4 %collective-permute-done = f32[304,128]{1,0:T(8,128)S(1)} collective-permute-done((f32[304,128]{1,0:T(8,128)S(1)}, f32[304,128]{1,0:T(8,128)S(1)}, u32[]{:S(2)}, u32[]{:S(2)}) %collective-permute-start) | collective-permute-done | bytes 155680 | tf_op jit(solution)/shard_map/cond/branch_1_fun/ppermute | solution.py:489
  31.3 0.8 %collective-permute-start.12 = (f32[7,24,128]{2,1,0:T(8,128)}, f32[7,24,128]{2,1,0:T(8,128)S(1)}, u32[]{:S(2)}, u32[]{:S(2)}) collective-permute-start(f32[7,24,128]{2,1,0:T(8,128)} %get-tuple-element.232), channel_id=1, source_target_pairs={{0,1},{1,0},{2,3},{3,2},{4,5},{5,4},{6,7},{7,6},{8,9},{9,8},{10,11... | collective-permute-start | bytes 258056 | tf_op jit(solution)/shard_map/ppermute | solution.py:511
  32.1 0.1 add_convert_fusion
  32.2 0.0 copy-done.1
  32.2 0.0 copy-done.3
  32.2 0.0 copy-start.7
  32.2 7.1 %fine.1 = (f32[4,32,16,128]{3,2,1,0:T(8,128)}, f32[4,8,8,128]{3,2,1,0:T(8,128)S(1)}) custom-call(f32[4,32,16,128]{3,2,1,0:T(8,128)S(1)} %copy-done.1, f32[3,32,16,128]{3,2,1,0:T(8,128)S(1)} %copy-done.3, f32[20,16,128]{2,1,0:T(8,128)S(1)} %collective-permute-done.10.flo, f32[20,16,128]{2,1,0:T(8,128)S(1)} %collective-permute-done.11.fhi, ...), custom_call_target="tpu_custom_call" | custom-call | tf_op jit(solution)/shard_map/fine/pallas_call | solution.py:585
  39.4 0.0 collective-permute-done.12
  39.4 0.0 copy-done.7
  39.4 9.8 %conditional.3 = (f32[4,8,8,128]{3,2,1,0:T(8,128)S(1)}, f32[4,16,16,128]{3,2,1,0:T(8,128)S(1)}) conditional(s32[]{:T(128)} %clamp.6, (s32[1,2]{1,0:T(1,128)S(1)}, f32[4,16,16,128]{3,2,1,0:T(8,128)S(1)}, f32[3,16,16,128]{3,2,1,0:T(8,128)S(1)}, f32[18,16,128]{2,1,0:T(8,128)S(1)}, f32[18,16,128]{2,1,0:T(8,128)S(1)}, ...), branch_computations={%region_4.5_spmd, %region_5.6_spmd, %region_6.7_spmd, %region_7.8_... | conditional | flops 40000000 | bytes 4786488 | solution.py:500
  39.4 2.7 %collective-permute-start.5 = (f32[4,8,8,128]{3,2,1,0:T(8,128)S(1)}, f32[4,8,8,128]{3,2,1,0:T(8,128)S(1)}, u32[]{:S(2)}, u32[]{:S(2)}) collective-permute-start(f32[4,8,8,128]{3,2,1,0:T(8,128)S(1)} %get-tuple-element.194), channel_id=1, source_target_pairs={{0,24},{8,0},{16,8},{24,16},{1,25},{9,1},{17,9},{25,17},{2,26},{10... | collective-permute-start | bytes 393224 | tf_op jit(solution)/shard_map/cond/branch_3_fun/ppermute | solution.py:489
  42.1 7.0 %coarse.7 = f32[4,16,16,128]{3,2,1,0:T(8,128)S(1)} custom-call(s32[1,2]{1,0:T(1,128)S(1)} %get-tuple-element.195.sides, f32[4,16,16,128]{3,2,1,0:T(8,128)S(1)} %get-tuple-element.196.c0, f32[3,16,16,128]{3,2,1,0:T(8,128)S(1)} %get-tuple-element.197.cw, f32[18,16,128]{2,1,0:T(8,128)S(1)} %get-tuple-element.198.lo, f32[18,16,128]{2,1,0:T(8,128)S(1)} %get-tuple-element.199.hi, ...), custom_call_target="tpu_custom_call" | custom-call | flops 40000000 | bytes 4000000 | tf_op jit(solution)/shard_map/cond/branch_3_fun/coarse/pallas_call | solution.py:573
  49.2 0.0 collective-permute-done.5
  49.2 0.9 %merge.1 = f32[4,16,16,128]{3,2,1,0:T(8,128)} custom-call(f32[4,16,16,128]{3,2,1,0:T(8,128)S(1)} %get-tuple-element.237.c3, f32[4,8,8,128]{3,2,1,0:T(8,128)S(1)} %get-tuple-element.238.avg), custom_call_target="tpu_custom_call" | custom-call | tf_op jit(solution)/shard_map/merge/pallas_call | solution.py:606
  (2 shorter events, 0.0 us)
Async XLA Ops:
  0.6 1.2 %copy-start = (f32[4,32,16,128]{3,2,1,0:T(8,128)S(1)}, f32[4,32,16,128]{3,2,1,0:T(8,128)}, u32[]{:S(2)}) copy-start(f32[4,32,16,128]{3,2,1,0:T(8,128)} %f0.3) | copy-start | bytes 3145732
  1.9 1.1 %copy-start.2 = (f32[3,32,16,128]{3,2,1,0:T(8,128)S(1)}, f32[3,32,16,128]{3,2,1,0:T(8,128)}, u32[]{:S(2)}) copy-start(f32[3,32,16,128]{3,2,1,0:T(8,128)} %fw.3) | copy-start | bytes 2359300
  3.0 14.3 %copy-start.4 = (f32[4,16,16,128]{3,2,1,0:T(8,128)S(1)}, f32[4,16,16,128]{3,2,1,0:T(8,128)}, u32[]{:S(2)}) copy-start(f32[4,16,16,128]{3,2,1,0:T(8,128)} %c0.5) | copy-start | bytes 1572868
  3.0 14.3 %copy-start.5 = (f32[3,16,16,128]{3,2,1,0:T(8,128)S(1)}, f32[3,16,16,128]{3,2,1,0:T(8,128)}, u32[]{:S(2)}) copy-start(f32[3,16,16,128]{3,2,1,0:T(8,128)} %cw.5) | copy-start | bytes 1179652
  4.1 9.8 %collective-permute-start.6 = (f32[18,16,128]{2,1,0:T(8,128)S(1)}, f32[18,16,128]{2,1,0:T(8,128)S(1)}, u32[]{:S(2)}, u32[]{:S(2)}) collective-permute-start(f32[18,16,128]{2,1,0:T(8,128)S(1)} %get-tuple-element.223), channel_id=1, source_target_pairs={{0,8},{8,16},{16,24},{24,0},{1,9},{9,17},{17,25},{25,1},{2,10},{10... | collective-permute-start | bytes 442376 | tf_op jit(solution)/shard_map/ppermute | solution.py:489
  7.2 10.1 %collective-permute-start.7 = (f32[18,16,128]{2,1,0:T(8,128)S(1)}, f32[18,16,128]{2,1,0:T(8,128)S(1)}, u32[]{:S(2)}, u32[]{:S(2)}) collective-permute-start(f32[18,16,128]{2,1,0:T(8,128)S(1)} %get-tuple-element.224), channel_id=1, source_target_pairs={{0,24},{8,0},{16,8},{24,16},{1,25},{9,1},{17,9},{25,17},{2,26},{10... | collective-permute-start | bytes 442376 | tf_op jit(solution)/shard_map/ppermute | solution.py:489
  9.3 14.3 %collective-permute-start.10 = (f32[20,16,128]{2,1,0:T(8,128)S(1)}, f32[20,16,128]{2,1,0:T(8,128)S(1)}, u32[]{:S(2)}, u32[]{:S(2)}) collective-permute-start(f32[20,16,128]{2,1,0:T(8,128)S(1)} %get-tuple-element.227), channel_id=1, source_target_pairs={{0,8},{8,16},{16,24},{24,0},{1,9},{9,17},{17,25},{25,1},{2,10},{10... | collective-permute-start | bytes 491528 | tf_op jit(solution)/shard_map/ppermute | solution.py:489
  9.3 14.3 %collective-permute-start.11 = (f32[20,16,128]{2,1,0:T(8,128)S(1)}, f32[20,16,128]{2,1,0:T(8,128)S(1)}, u32[]{:S(2)}, u32[]{:S(2)}) collective-permute-start(f32[20,16,128]{2,1,0:T(8,128)S(1)} %get-tuple-element.228), channel_id=1, source_target_pairs={{0,24},{8,0},{16,8},{24,16},{1,25},{9,1},{17,9},{25,17},{2,26},{10... | collective-permute-start | bytes 491528 | tf_op jit(solution)/shard_map/ppermute | solution.py:489
  17.4 6.2 %collective-permute-start.8 = (f32[318,128]{1,0:T(8,128)S(1)}, f32[318,128]{1,0:T(8,128)S(1)}, u32[]{:S(2)}, u32[]{:S(2)}) collective-permute-start(f32[318,128]{1,0:T(8,128)S(1)} %get-tuple-element.225), channel_id=1, source_target_pairs={{0,2},{2,4},{4,6},{6,0},{1,3},{3,5},{5,7},{7,1},{8,10},{10,12},{12... | collective-permute-start | bytes 488456 | tf_op jit(solution)/shard_map/ppermute | solution.py:489
  17.4 6.2 %collective-permute-start.9 = (f32[318,128]{1,0:T(8,128)S(1)}, f32[318,128]{1,0:T(8,128)S(1)}, u32[]{:S(2)}, u32[]{:S(2)}) collective-permute-start(f32[318,128]{1,0:T(8,128)S(1)} %get-tuple-element.226), channel_id=1, source_target_pairs={{0,6},{2,0},{4,2},{6,4},{1,7},{3,1},{5,3},{7,5},{8,14},{10,8},{12,... | collective-permute-start | bytes 488456 | tf_op jit(solution)/shard_map/ppermute | solution.py:489
  23.6 0.7 %copy-start.6 = (f32[318,128]{1,0:T(8,128)}, f32[318,128]{1,0:T(8,128)S(1)}, u32[]{:S(2)}) copy-start(f32[318,128]{1,0:T(8,128)S(1)} %collective-permute-done.9) | copy-start | bytes 488452
  24.3 7.9 %copy-start.1 = (f32[4,32,16,128]{3,2,1,0:T(8,128)S(1)}, f32[4,32,16,128]{3,2,1,0:T(8,128)}, u32[]{:S(2)}) copy-start(f32[4,32,16,128]{3,2,1,0:T(8,128)} %f0.3) | copy-start | bytes 3145732
  24.3 7.9 %copy-start.3 = (f32[3,32,16,128]{3,2,1,0:T(8,128)S(1)}, f32[3,32,16,128]{3,2,1,0:T(8,128)}, u32[]{:S(2)}) copy-start(f32[3,32,16,128]{3,2,1,0:T(8,128)} %fw.3) | copy-start | bytes 2359300
  24.3 7.0 %collective-permute-start = (f32[304,128]{1,0:T(8,128)S(1)}, f32[304,128]{1,0:T(8,128)S(1)}, u32[]{:S(2)}, u32[]{:S(2)}) collective-permute-start(f32[304,128]{1,0:T(8,128)S(1)} %get-tuple-element.143), channel_id=1, source_target_pairs={{0,8},{8,16},{16,24},{24,0},{1,9},{9,17},{17,25},{25,1},{2,10},{10... | collective-permute-start | bytes 466952 | tf_op jit(solution)/shard_map/cond/branch_1_fun/ppermute | solution.py:489
  31.3 8.0 %collective-permute-start.12 = (f32[7,24,128]{2,1,0:T(8,128)}, f32[7,24,128]{2,1,0:T(8,128)S(1)}, u32[]{:S(2)}, u32[]{:S(2)}) collective-permute-start(f32[7,24,128]{2,1,0:T(8,128)} %get-tuple-element.232), channel_id=1, source_target_pairs={{0,1},{1,0},{2,3},{3,2},{4,5},{5,4},{6,7},{7,6},{8,9},{9,8},{10,11... | collective-permute-start | bytes 258056 | tf_op jit(solution)/shard_map/ppermute | solution.py:511
  32.2 7.2 %copy-start.7 = (f32[318,128]{1,0:T(8,128)S(1)}, f32[318,128]{1,0:T(8,128)}, u32[]{:S(2)}) copy-start(f32[318,128]{1,0:T(8,128)} %copy-done.6) | copy-start | bytes 488452
  39.4 9.8 %collective-permute-start.5 = (f32[4,8,8,128]{3,2,1,0:T(8,128)S(1)}, f32[4,8,8,128]{3,2,1,0:T(8,128)S(1)}, u32[]{:S(2)}, u32[]{:S(2)}) collective-permute-start(f32[4,8,8,128]{3,2,1,0:T(8,128)S(1)} %get-tuple-element.194), channel_id=1, source_target_pairs={{0,24},{8,0},{16,8},{24,16},{1,25},{9,1},{17,9},{25,17},{2,26},{10... | collective-permute-start | bytes 393224 | tf_op jit(solution)/shard_map/cond/branch_3_fun/ppermute | solution.py:489
